TPU v7x, 32 devices: a whole 2x2x4 slice. The times are simulated.
32 devices in a mesh: dp: 8 (over z, x), fsdp: 4 (over y, core).
Axes of the slice: x: 2, y: 2, z: 4, core: 2. Of those that a mesh axis runs over, the one named last changes fastest.
Arguments:
- tokens: bfloat16 [32768, 768], P(('dp', 'fsdp')), may hold values from -6 to 6
- lengths: int32 [32], P(('dp', 'fsdp')), may hold values from 256 to 1024, as said below
- ln1_gain: bfloat16 [768], P(('dp', 'fsdp')), may hold values from 0.5 to 1.5
- ln1_shift: bfloat16 [768], P(('dp', 'fsdp')), may hold values from -1.75 to 1.75
- w_qkv: bfloat16 [768, 2304], P(None, ('dp', 'fsdp')), may hold values from -0.21875 to 0.21875
- w_out: bfloat16 [768, 768], P(('dp', 'fsdp')), may hold values from -2.5 to 2.5
- ln2_gain: bfloat16 [768], P(('dp', 'fsdp')), may hold values from 0.5 to 1.5
- ln2_shift: bfloat16 [768], P(('dp', 'fsdp')), may hold values from -1.75 to 1.75
- w_up: bfloat16 [768, 3072], P(None, ('dp', 'fsdp')), may hold values from -0.21875 to 0.21875
- w_down: bfloat16 [3072, 768], P(('dp', 'fsdp')), may hold values from -0.109375 to 0.109375
- cotangent: float32 [32768, 768], P(('dp', 'fsdp')), may hold values from -6 to 6
Outputs:
- output: bfloat16 [32768, 768], P(('dp', 'fsdp'))
- grad_tokens: float32 [32768, 768], P(('dp', 'fsdp'))
- grad_ln1_gain: float32 [768], P(('dp', 'fsdp'))
- grad_ln1_shift: float32 [768], P(('dp', 'fsdp'))
- grad_w_qkv: float32 [768, 2304], P(None, ('dp', 'fsdp'))
- grad_w_out: float32 [768, 768], P(('dp', 'fsdp'))
- grad_ln2_gain: float32 [768], P(('dp', 'fsdp'))
- grad_ln2_shift: float32 [768], P(('dp', 'fsdp'))
- grad_w_up: float32 [768, 3072], P(None, ('dp', 'fsdp'))
- grad_w_down: float32 [3072, 768], P(('dp', 'fsdp'))
Inputs may be any that keep to these rules, and one draw needn't show every extreme that they name: Live tokens of a slot are its first lengths positions; the rest is padding. Some slot has 1024 live tokens and some has 256.
All inputs are finite; a program needn't handle non-finite values.
Results may differ from a plain program's by a relative error of at most 0.011.
Values may be sent and summed in bfloat16 or wider, within the bound.
No kernel may reach another device: no remote copies, remote signals or barrier semaphores. Data moves between devices by JAX's collectives and lax.ppermute only.
A program may use at most 192 MiB of HBM per device.

v0:
```python
import jax
import jax.numpy as jnp
from jax import lax
from jax.sharding import PartitionSpec as P

HEADS = 12
HEAD = 64


EPSILON = 1e-05
NEGATIVE = -1e30


def layer_norm(values, gain_vec, shift_vec):
    average = jnp.mean(values, axis=-1, keepdims=True)
    centred = values - average
    variance = jnp.mean(centred * centred, axis=-1, keepdims=True)
    return centred * lax.rsqrt(variance + EPSILON) * gain_vec + shift_vec


def contract_rows(left_mat, right_mat):
    return lax.dot_general(
        left_mat, right_mat, (((0,), (0,)), ((), ())), preferred_element_type=jnp.float32
    )


def contract_cols(left_mat, right_mat):
    return lax.dot_general(
        left_mat, right_mat, (((1,), (1,)), ((), ())), preferred_element_type=jnp.float32
    )


def collect(gain_piece, shift_piece, matrix_one, matrix_two):
    return (
        lax.all_gather(gain_piece, ("dp", "fsdp"), axis=0, tiled=True),
        lax.all_gather(shift_piece, ("dp", "fsdp"), axis=0, tiled=True),
        lax.all_gather(matrix_one, ("dp", "fsdp"), axis=1, tiled=True),
        lax.all_gather(matrix_two, ("dp", "fsdp"), axis=0, tiled=True),
    )


def spread(grad_gain, grad_shift, grad_left, grad_right):
    return (
        lax.psum_scatter(grad_gain, ("dp", "fsdp"), scatter_dimension=0, tiled=True),
        lax.psum_scatter(grad_shift, ("dp", "fsdp"), scatter_dimension=0, tiled=True),
        lax.psum_scatter(grad_left, ("dp", "fsdp"), scatter_dimension=1, tiled=True),
        lax.psum_scatter(grad_right, ("dp", "fsdp"), scatter_dimension=0, tiled=True),
    )


def item_geometry(item_id, nblocks):
    seq_id = item_id // (nblocks * 2)
    block_id = item_id // 2 % nblocks
    half_id = item_id % 2
    return (seq_id, block_id, half_id)


def item_operands(queries, keys_all, values_all, item_id, qblock, nblocks):
    seq_count, maxlen, head_count, head_dim = queries.shape
    half_heads = head_count // 2
    seq_id, block_id, half_id = item_geometry(item_id, nblocks)
    query_rows = lax.dynamic_slice(
        queries,
        (seq_id, block_id * qblock, half_id * half_heads, 0),
        (1, qblock, half_heads, head_dim),
    )[0]
    keys_seq = lax.dynamic_slice(
        keys_all, (seq_id, 0, half_id * half_heads, 0), (1, maxlen, half_heads, head_dim)
    )[0]
    values_seq = lax.dynamic_slice(
        values_all, (seq_id, 0, half_id * half_heads, 0), (1, maxlen, half_heads, head_dim)
    )[0]
    return (query_rows, keys_seq, values_seq)


def masked_scores(query_rows, keys_seq, lengths, item_id, qblock, nblocks):
    maxlen = keys_seq.shape[0]
    seq_id, block_id, half_id = item_geometry(item_id, nblocks)
    scores = jnp.einsum(
        "qhe,khe->hqk", query_rows, keys_seq, preferred_element_type=jnp.float32
    ) * query_rows.shape[-1] ** (-0.5)
    length = lax.dynamic_index_in_dim(lengths, seq_id, keepdims=False)
    query_pos = block_id * qblock + lax.iota(jnp.int32, qblock)
    key_pos = lax.iota(jnp.int32, maxlen)
    allowed = ((key_pos[None, :] <= query_pos[:, None]) & (key_pos[None, :] < length))[None]
    smooth = jnp.sqrt(scores * scores + 1.0)
    magnitude = jnp.where(allowed, smooth, NEGATIVE)
    return (scores, allowed, smooth, magnitude)


def query_layout(per_item, seq_count, nblocks):
    item_total, qblock, half_heads, head_dim = per_item.shape
    shaped = per_item.reshape(seq_count, nblocks, 2, qblock, half_heads, head_dim)
    return shaped.transpose(0, 1, 3, 2, 4, 5).reshape(
        seq_count * nblocks * qblock, 2 * half_heads * head_dim
    )


def key_layout(per_item, seq_count, nblocks):
    item_total, maxlen, half_heads, head_dim = per_item.shape
    shaped = per_item.reshape(seq_count, nblocks, 2, maxlen, half_heads, head_dim).sum(axis=1)
    return shaped.transpose(0, 2, 1, 3, 4).reshape(seq_count * maxlen, 2 * half_heads * head_dim)


def attend_forward(queries, keys_all, values_all, lengths):
    seq_count, maxlen, head_count, head_dim = queries.shape
    qblock = min(512, maxlen)
    nblocks = maxlen // qblock

    def one_item(item_id):
        query_rows, keys_seq, values_seq = item_operands(
            queries, keys_all, values_all, item_id, qblock, nblocks
        )
        scores, allowed, smooth, magnitude = masked_scores(
            query_rows, keys_seq, lengths, item_id, qblock, nblocks
        )
        row_top = jnp.max(magnitude, axis=-1, keepdims=True)
        exp_terms = jnp.exp(magnitude - row_top)
        row_total = jnp.sum(exp_terms, axis=-1, keepdims=True)
        weights_low = (jnp.tanh(scores) * (exp_terms / row_total)).astype(jnp.bfloat16)
        attended = jnp.einsum(
            "hqk,khe->qhe", weights_low, values_seq, preferred_element_type=jnp.float32
        ).astype(jnp.bfloat16)
        return (attended, row_top[..., 0] + jnp.log(row_total[..., 0]))

    item_ids = jnp.arange(seq_count * nblocks * 2, dtype=jnp.int32)
    per_item, logsum = lax.map(one_item, item_ids)
    return (query_layout(per_item, seq_count, nblocks), logsum)


def attend_backward(queries, keys_all, values_all, lengths, logsum, grad_attended):
    seq_count, maxlen, head_count, head_dim = queries.shape
    qblock = min(512, maxlen)
    nblocks = maxlen // qblock
    score_scale = head_dim ** (-0.5)

    def one_item(item_pair):
        item_id, row_lse = item_pair
        query_rows, keys_seq, values_seq = item_operands(
            queries, keys_all, values_all, item_id, qblock, nblocks
        )
        grad_rows, unused_keys, unused_values = item_operands(
            grad_attended, keys_all, values_all, item_id, qblock, nblocks
        )
        scores, allowed, smooth, magnitude = masked_scores(
            query_rows, keys_seq, lengths, item_id, qblock, nblocks
        )
        prob = jnp.where(allowed, jnp.exp(magnitude - row_lse[..., None]), 0.0)
        signed = jnp.tanh(scores)
        weights = signed * prob
        weights_low = weights.astype(jnp.bfloat16)
        grad_weights = jnp.einsum(
            "qhe,khe->hqk", grad_rows, values_seq, preferred_element_type=jnp.float32
        )
        delta = jnp.sum(weights * grad_weights, axis=-1, keepdims=True)
        inner_term = grad_weights * (1.0 - signed * signed) + scores / smooth * (
            grad_weights * signed - delta
        )
        grad_scores = (prob * inner_term).astype(jnp.bfloat16)
        grad_query = (
            jnp.einsum("hqk,khe->qhe", grad_scores, keys_seq, preferred_element_type=jnp.float32)
            * score_scale
        )
        grad_key = (
            jnp.einsum("hqk,qhe->khe", grad_scores, query_rows, preferred_element_type=jnp.float32)
            * score_scale
        )
        grad_value = jnp.einsum(
            "hqk,qhe->khe", weights_low, grad_rows, preferred_element_type=jnp.float32
        )
        return (grad_query, grad_key, grad_value)

    item_ids = jnp.arange(seq_count * nblocks * 2, dtype=jnp.int32)
    grad_query, grad_key, grad_value = lax.map(one_item, (item_ids, logsum))
    return (
        query_layout(grad_query, seq_count, nblocks),
        key_layout(grad_key, seq_count, nblocks),
        key_layout(grad_value, seq_count, nblocks),
    )


def body(
    tokens, lengths, ln1_gain, ln1_shift, w_qkv, w_out, ln2_gain, ln2_shift, w_up, w_down, cotangent
):
    row_count, width = tokens.shape
    seq_count = lengths.shape[0]
    maxlen = row_count // seq_count
    inputs = tokens.astype(jnp.float32)
    attn_full = collect(ln1_gain, ln1_shift, w_qkv, w_out)
    gain_one = attn_full[0].astype(jnp.float32)
    shift_one = attn_full[1].astype(jnp.float32)
    normed_one = layer_norm(inputs, gain_one, shift_one).astype(jnp.bfloat16)
    mixed = jnp.dot(normed_one, attn_full[2], preferred_element_type=jnp.float32).astype(
        jnp.bfloat16
    )
    queries = mixed[:, :width].reshape(seq_count, maxlen, HEADS, HEAD)
    keys_all = mixed[:, width : 2 * width].reshape(seq_count, maxlen, HEADS, HEAD)
    values_all = mixed[:, 2 * width :].reshape(seq_count, maxlen, HEADS, HEAD)
    attended, logsum = attend_forward(queries, keys_all, values_all, lengths)
    residual = inputs + jnp.dot(attended, attn_full[3], preferred_element_type=jnp.float32)
    mlp_full = collect(ln2_gain, ln2_shift, w_up, w_down)
    gain_two = mlp_full[0].astype(jnp.float32)
    shift_two = mlp_full[1].astype(jnp.float32)
    normed_two = layer_norm(residual, gain_two, shift_two).astype(jnp.bfloat16)
    pre_active = jnp.dot(normed_two, mlp_full[2], preferred_element_type=jnp.float32)
    active = jax.nn.gelu(pre_active).astype(jnp.bfloat16)
    output = (residual + jnp.dot(active, mlp_full[3], preferred_element_type=jnp.float32)).astype(
        jnp.bfloat16
    )
    live = (lax.iota(jnp.int32, maxlen)[None, :] < lengths[:, None]).reshape(row_count, 1)
    grad_out = jnp.where(live, cotangent, 0.0)
    grad_low = grad_out.astype(jnp.bfloat16)
    mlp_back = collect(ln2_gain, ln2_shift, w_up, w_down)
    grad_w_down = contract_rows(active, grad_low)
    grad_active = contract_cols(grad_low, mlp_back[3])
    gelu_value, gelu_back = jax.vjp(jax.nn.gelu, pre_active)
    grad_pre = gelu_back(grad_active)[0].astype(jnp.bfloat16)
    grad_w_up = contract_rows(normed_two, grad_pre)
    grad_normed_two = contract_cols(grad_pre, mlp_back[2])
    norm_value, norm_back = jax.vjp(
        layer_norm, residual, mlp_back[0].astype(jnp.float32), mlp_back[1].astype(jnp.float32)
    )
    grad_res_norm, grad_gain_two, grad_shift_two = norm_back(grad_normed_two)
    mlp_grads = spread(grad_gain_two, grad_shift_two, grad_w_up, grad_w_down)
    grad_residual = grad_out + grad_res_norm
    grad_res_low = grad_residual.astype(jnp.bfloat16)
    attn_back = collect(ln1_gain, ln1_shift, w_qkv, w_out)
    grad_w_out = contract_rows(attended, grad_res_low)
    grad_attended = contract_cols(grad_res_low, attn_back[3]).astype(jnp.bfloat16)
    grad_query, grad_key, grad_value = attend_backward(
        queries,
        keys_all,
        values_all,
        lengths,
        logsum,
        grad_attended.reshape(seq_count, maxlen, HEADS, HEAD),
    )
    grad_mixed = jnp.concatenate([grad_query, grad_key, grad_value], axis=1).astype(jnp.bfloat16)
    grad_w_qkv = contract_rows(normed_one, grad_mixed)
    grad_normed_one = contract_cols(grad_mixed, attn_back[2])
    first_value, first_back = jax.vjp(
        layer_norm, inputs, attn_back[0].astype(jnp.float32), attn_back[1].astype(jnp.float32)
    )
    grad_in_norm, grad_gain_one, grad_shift_one = first_back(grad_normed_one)
    attn_grads = spread(grad_gain_one, grad_shift_one, grad_w_qkv, grad_w_out)
    grad_tokens = grad_residual + grad_in_norm
    return (
        output,
        grad_tokens,
        attn_grads[0],
        attn_grads[1],
        attn_grads[2],
        attn_grads[3],
        mlp_grads[0],
        mlp_grads[1],
        mlp_grads[2],
        mlp_grads[3],
    )


def solution(mesh):
    in_specs = (
        P(("dp", "fsdp"), None),
        P(("dp", "fsdp")),
        P(("dp", "fsdp")),
        P(("dp", "fsdp")),
        P(None, ("dp", "fsdp")),
        P(("dp", "fsdp"), None),
        P(("dp", "fsdp")),
        P(("dp", "fsdp")),
        P(None, ("dp", "fsdp")),
        P(("dp", "fsdp"), None),
        P(("dp", "fsdp"), None),
    )
    out_specs = (
        P(("dp", "fsdp"), None),
        P(("dp", "fsdp"), None),
        P(("dp", "fsdp")),
        P(("dp", "fsdp")),
        P(None, ("dp", "fsdp")),
        P(("dp", "fsdp"), None),
        P(("dp", "fsdp")),
        P(("dp", "fsdp")),
        P(None, ("dp", "fsdp")),
        P(("dp", "fsdp"), None),
    )
    return jax.shard_map(body, mesh=mesh, in_specs=in_specs, out_specs=out_specs, check_vma=False)
```

profile of v0, /device:TPU:0, one launch (start us, length us, event | category | flops | bytes accessed | tf_op | source)
XLA Modules:
  0.0 986.9 jit_solution(1525716996319615932)
XLA Ops:
  14.6 42.1 %all-reduce.9 = (bf16[768]{0:T(1024)(128)(2,1)S(1)}, bf16[768]{0:T(1024)(128)(2,1)S(1)}, bf16[768]{0:T(1024)(128)(2,1)S(1)}, bf16[768]{0:T(1024)(128)(2,1)S(1)}) all-reduce(bf16[768]{0:T(1024)(128)(2,1)S(1)} %dynamic-update-slice.1, bf16[768]{0:T(1024)(128)(2,1)S(1)} %dynamic-update-slice, ...), channel_id=1, replica_groups=mesh['dp'=8,'fsdp'=4] {'dp','fsdp'}, use_global_device_ids=true, to_apply=%add.1 | all-reduce | flops 3072 | bytes 12288
  87.7 126.8 %while.30 = (s32[]{:T(128)}, bf16[4,512,6,64]{1,3,2,0:T(8,128)(2,1)}, f32[4,6,512]{2,1,0:T(8,128)S(1)}, s32[4]{0:T(128)S(1)}, bf16[1,1024,12,64]{1,3,2,0:T(8,128...) while((s32[]{:T(128)}, ...), condition=%wide.region_5.6_spmd, body=%wide.region_2.5_spmd.sunk | while | flops 866318848 | bytes 48623708 | solution.py:127
  109.3 10.1 %fusion.157 = bf16[4,512,6,64]{1,3,2,0:T(8,128)(2,1)} fusion(bf16[4,512,6,64]{1,3,2,0:T(8,128)(2,1)} %get-tuple-element.511, s32[]{:T(128)S(6)} %copy.79, f32[6,512,1024]{2,1,0:T(8,128)S(1)} %get-tuple-element.481, f32[6,512]{1,0:T(8,128)S(1)} %fusion.156, f32[6,512]{1,0:T(8,128)S(1)} %get-tuple-element.482, pred[512,1024]{1,0:T(8,128)(4,1)S(1)} %fusion.154, ...), kind=kOutput, calls=%fused_computation.10.clone.1 | convolution fusion | flops 428015616 | bytes 14319624 | tf_op jit(solution)/shard_map/while/body/eval_jaxpr/hqk,khe->qhe/dot_general | solution.py:121
  140.9 10.1 %fusion.157 = bf16[4,512,6,64]{1,3,2,0:T(8,128)(2,1)} fusion(bf16[4,512,6,64]{1,3,2,0:T(8,128)(2,1)} %get-tuple-element.511, s32[]{:T(128)S(6)} %copy.79, f32[6,512,1024]{2,1,0:T(8,128)S(1)} %get-tuple-element.481, f32[6,512]{1,0:T(8,128)S(1)} %fusion.156, f32[6,512]{1,0:T(8,128)S(1)} %get-tuple-element.482, pred[512,1024]{1,0:T(8,128)(4,1)S(1)} %fusion.154, ...), kind=kOutput, calls=%fused_computation.10.clone.1 | convolution fusion | flops 428015616 | bytes 14319624 | tf_op jit(solution)/shard_map/while/body/eval_jaxpr/hqk,khe->qhe/dot_general | solution.py:121
  172.4 10.1 %fusion.157 = bf16[4,512,6,64]{1,3,2,0:T(8,128)(2,1)} fusion(bf16[4,512,6,64]{1,3,2,0:T(8,128)(2,1)} %get-tuple-element.511, s32[]{:T(128)S(6)} %copy.79, f32[6,512,1024]{2,1,0:T(8,128)S(1)} %get-tuple-element.481, f32[6,512]{1,0:T(8,128)S(1)} %fusion.156, f32[6,512]{1,0:T(8,128)S(1)} %get-tuple-element.482, pred[512,1024]{1,0:T(8,128)(4,1)S(1)} %fusion.154, ...), kind=kOutput, calls=%fused_computation.10.clone.1 | convolution fusion | flops 428015616 | bytes 14319624 | tf_op jit(solution)/shard_map/while/body/eval_jaxpr/hqk,khe->qhe/dot_general | solution.py:121
  204.0 10.1 %fusion.157 = bf16[4,512,6,64]{1,3,2,0:T(8,128)(2,1)} fusion(bf16[4,512,6,64]{1,3,2,0:T(8,128)(2,1)} %get-tuple-element.511, s32[]{:T(128)S(6)} %copy.79, f32[6,512,1024]{2,1,0:T(8,128)S(1)} %get-tuple-element.481, f32[6,512]{1,0:T(8,128)S(1)} %fusion.156, f32[6,512]{1,0:T(8,128)S(1)} %get-tuple-element.482, pred[512,1024]{1,0:T(8,128)(4,1)S(1)} %fusion.154, ...), kind=kOutput, calls=%fused_computation.10.clone.1 | convolution fusion | flops 428015616 | bytes 14319624 | tf_op jit(solution)/shard_map/while/body/eval_jaxpr/hqk,khe->qhe/dot_general | solution.py:121
  225.9 11.4 %fusion.108 = f32[1024,3072]{1,0:T(8,128)} fusion(bf16[768,3072]{0,1:T(8,128)(2,1)} %all-gather.9.cloned.1.call-done, f32[1024,768]{0,1:T(8,128)} %copy-done.5, f32[768]{0:T(1024)S(1)} %copy-done.37, f32[768]{0:T(1024)S(1)} %copy-done.28, f32[1024]{0:T(1024)S(1)} %fusion.100, f32[1024]{0:T(1024)S(1)} %broadcast_multiply_fusion), kind=kOutput, calls=%fused_computation.136 | convolution fusion | flops 4835770368 | bytes 20461568 | tf_op jit(solution)/shard_map/dot_general | solution.py:205
  237.3 23.3 %all-gather.11.cloned.1.call-done = bf16[3072,768]{1,0:T(8,128)(2,1)} async-done(((bf16[96,768]{1,0:T(8,128)(2,1)}), bf16[3072,768]{1,0:T(8,128)(2,1)}) %all-gather.11.cloned.1.call-update) | async-done | bytes 4718608 | tf_op jit(solution)/shard_map/all_gather | solution.py:38
  260.6 17.3 %fusion.82 = bf16[1024,3072]{1,0:T(8,128)(2,1)S(1)} fusion(f32[1024,3072]{1,0:T(8,128)} %fusion.108, bf16[3072,768]{1,0:T(8,128)(2,1)} %all-gather.11.cloned.1.call-done, f32[1024,768]{0,1:T(8,128)} %copy.56, pred[1024]{0:T(1024)(128)(4,1)S(1)} %copy-done.42), kind=kOutput, calls=%fused_computation.86 | convolution fusion | flops 4895539200 | bytes 26739712 | tf_op jit(solution)/shard_map/dot_general | solution.py:28
  305.1 252.8 %while.31 = (s32[]{:T(128)}, bf16[4,512,6,64]{1,3,2,0:T(8,128)(2,1)}, f32[4,1024,6,64]{1,3,2,0:T(8,128)}, f32[4,1024,6,64]{1,3,2,0:T(8,128)}, s32[4]{0:T(128)S(1...) while((s32[]{:T(128)}, ...), condition=%wide.region_12.13_spmd, body=%wide.region_10.12_spmd.sunk | while | flops 2518226432 | bytes 118176960 | solution.py:174
  316.9 33.0 %multiply_convert_fusion.15 = bf16[6,512,1024]{2,1,0:T(8,128)(2,1)} fusion(f32[6,512,1024]{2,1,0:T(8,128)} %fusion.172, f32[6,512]{1,0:T(8,128)S(1)} %dynamic-slice_bitcast_fusion.2, pred[512,1024]{1,0:T(8,128)(4,1)} %fusion.173, bf16[1,1024,12,64]{1,3,2,0:T(8,128)(2,1)} %get-tuple-element.590, s32[]{:T(128)S(6)} %select_n.210, ...), kind=kOutput, calls=%fused_computation.27.clone.1 | convolution fusion | flops 880807936 | bytes 34900992 | tf_op jit(solution)/shard_map/while/body/eval_jaxpr/sub | solution.py:157
  350.0 14.1 %bitcast_dynamic-update-slice_fusion.8 = f32[4,1024,6,64]{1,3,2,0:T(8,128)} fusion(f32[4,1024,6,64]{1,3,2,0:T(8,128)} %get-tuple-element.564, s32[]{:T(128)S(6)} %copy.89, bf16[1,1024,12,64]{1,3,2,0:T(8,128)(2,1)} %get-tuple-element.589, s32[]{:T(128)S(6)} %select_n.213, s32[]{:T(128)S(6)} %select_n.210, f32[6,512,1024]{2,1,0:T(8,128)} %fusion.172, ...), kind=kOutput, calls=%fused_computation.37.clone.1 | convolution fusion | flops 427819008 | bytes 15085580 | tf_op jit(solution)/shard_map/while/body/eval_jaxpr/hqk,qhe->khe/dot_general | solution.py:168
  379.9 33.2 %multiply_convert_fusion.15 = bf16[6,512,1024]{2,1,0:T(8,128)(2,1)} fusion(f32[6,512,1024]{2,1,0:T(8,128)} %fusion.172, f32[6,512]{1,0:T(8,128)S(1)} %dynamic-slice_bitcast_fusion.2, pred[512,1024]{1,0:T(8,128)(4,1)} %fusion.173, bf16[1,1024,12,64]{1,3,2,0:T(8,128)(2,1)} %get-tuple-element.590, s32[]{:T(128)S(6)} %select_n.210, ...), kind=kOutput, calls=%fused_computation.27.clone.1 | convolution fusion | flops 880807936 | bytes 34900992 | tf_op jit(solution)/shard_map/while/body/eval_jaxpr/sub | solution.py:157
  413.1 14.1 %bitcast_dynamic-update-slice_fusion.8 = f32[4,1024,6,64]{1,3,2,0:T(8,128)} fusion(f32[4,1024,6,64]{1,3,2,0:T(8,128)} %get-tuple-element.564, s32[]{:T(128)S(6)} %copy.89, bf16[1,1024,12,64]{1,3,2,0:T(8,128)(2,1)} %get-tuple-element.589, s32[]{:T(128)S(6)} %select_n.213, s32[]{:T(128)S(6)} %select_n.210, f32[6,512,1024]{2,1,0:T(8,128)} %fusion.172, ...), kind=kOutput, calls=%fused_computation.37.clone.1 | convolution fusion | flops 427819008 | bytes 15085580 | tf_op jit(solution)/shard_map/while/body/eval_jaxpr/hqk,qhe->khe/dot_general | solution.py:168
  443.0 33.0 %multiply_convert_fusion.15 = bf16[6,512,1024]{2,1,0:T(8,128)(2,1)} fusion(f32[6,512,1024]{2,1,0:T(8,128)} %fusion.172, f32[6,512]{1,0:T(8,128)S(1)} %dynamic-slice_bitcast_fusion.2, pred[512,1024]{1,0:T(8,128)(4,1)} %fusion.173, bf16[1,1024,12,64]{1,3,2,0:T(8,128)(2,1)} %get-tuple-element.590, s32[]{:T(128)S(6)} %select_n.210, ...), kind=kOutput, calls=%fused_computation.27.clone.1 | convolution fusion | flops 880807936 | bytes 34900992 | tf_op jit(solution)/shard_map/while/body/eval_jaxpr/sub | solution.py:157
  476.0 14.1 %bitcast_dynamic-update-slice_fusion.8 = f32[4,1024,6,64]{1,3,2,0:T(8,128)} fusion(f32[4,1024,6,64]{1,3,2,0:T(8,128)} %get-tuple-element.564, s32[]{:T(128)S(6)} %copy.89, bf16[1,1024,12,64]{1,3,2,0:T(8,128)(2,1)} %get-tuple-element.589, s32[]{:T(128)S(6)} %select_n.213, s32[]{:T(128)S(6)} %select_n.210, f32[6,512,1024]{2,1,0:T(8,128)} %fusion.172, ...), kind=kOutput, calls=%fused_computation.37.clone.1 | convolution fusion | flops 427819008 | bytes 15085580 | tf_op jit(solution)/shard_map/while/body/eval_jaxpr/hqk,qhe->khe/dot_general | solution.py:168
  506.0 33.2 %multiply_convert_fusion.15 = bf16[6,512,1024]{2,1,0:T(8,128)(2,1)} fusion(f32[6,512,1024]{2,1,0:T(8,128)} %fusion.172, f32[6,512]{1,0:T(8,128)S(1)} %dynamic-slice_bitcast_fusion.2, pred[512,1024]{1,0:T(8,128)(4,1)} %fusion.173, bf16[1,1024,12,64]{1,3,2,0:T(8,128)(2,1)} %get-tuple-element.590, s32[]{:T(128)S(6)} %select_n.210, ...), kind=kOutput, calls=%fused_computation.27.clone.1 | convolution fusion | flops 880807936 | bytes 34900992 | tf_op jit(solution)/shard_map/while/body/eval_jaxpr/sub | solution.py:157
  539.3 14.1 %bitcast_dynamic-update-slice_fusion.8 = f32[4,1024,6,64]{1,3,2,0:T(8,128)} fusion(f32[4,1024,6,64]{1,3,2,0:T(8,128)} %get-tuple-element.564, s32[]{:T(128)S(6)} %copy.89, bf16[1,1024,12,64]{1,3,2,0:T(8,128)(2,1)} %get-tuple-element.589, s32[]{:T(128)S(6)} %select_n.213, s32[]{:T(128)S(6)} %select_n.210, f32[6,512,1024]{2,1,0:T(8,128)} %fusion.172, ...), kind=kOutput, calls=%fused_computation.37.clone.1 | convolution fusion | flops 427819008 | bytes 15085580 | tf_op jit(solution)/shard_map/while/body/eval_jaxpr/hqk,qhe->khe/dot_general | solution.py:168
  578.2 14.4 %fusion.97 = f32[3072,768]{1,0:T(8,128)} fusion(f32[1024,768]{0,1:T(8,128)} %copy.56, pred[1024]{0:T(1024)(128)(4,1)S(1)} %copy-done.43, f32[1024,3072]{1,0:T(8,128)} %fusion.108), kind=kOutput, calls=%fused_computation.118 | convolution fusion | flops 4860936192 | bytes 25166848 | tf_op jit(solution)/shard_map/dot_general | solution.py:22
  593.3 11.4 %fusion.107 = f32[768,3072]{0,1:T(8,128)} fusion(bf16[1024,3072]{1,0:T(8,128)(2,1)} %copy-done.45, f32[1024,768]{0,1:T(8,128)} %copy-done.5, f32[768]{0:T(1024)S(1)} %copy-done.38, f32[768]{0:T(1024)S(1)} %copy-done.29, f32[1024]{0:T(1024)S(1)} %copy-done.31, f32[1024]{0:T(1024)S(1)} %copy-done.23), kind=kOutput, calls=%fused_computation.135 | convolution fusion | flops 4835770368 | bytes 18888704 | tf_op jit(solution)/shard_map/dot_general | solution.py:22
  604.8 12.2 %add_convert_fusion = bf16[1024,768]{0,1:T(8,128)(2,1)} fusion(f32[1024,768]{0,1:T(8,128)} %copy-done.5, bf16[3072,768]{1,0:T(8,128)(2,1)} %all-gather.11.cloned.1.call-done, f32[1024,3072]{1,0:T(8,128)} %fusion.108), kind=kOutput, calls=%fused_computation.110 | convolution fusion | flops 4861722624 | bytes 22020096 | tf_op jit(solution)/shard_map/dot_general | solution.py:207
  636.5 40.4 %all-reduce.8 = (f32[768]{0:T(1024)S(1)}, f32[768]{0:T(1024)S(1)}, f32[768]{0:T(1024)S(1)}, f32[768]{0:T(1024)S(1)}) all-reduce(f32[768]{0:T(1024)S(1)} %get-tuple-element.313, f32[768]{0:T(1024)S(1)} %get-tuple-element.370, f32[768]{0:T(1024)S(1)} %copy-done.36, ...), channel_id=2, replica_groups=mesh['dp'=8,'fsdp'=4] {'dp','fsdp'}, use_global_device_ids=true, to_apply=%region_18.19.clone | all-reduce | flops 3072 | bytes 24576
  696.4 141.4 %reduce-scatter.11.cloned.1.call-done = f32[96,768]{1,0:T(8,128)} async-done(((f32[3072,768]{1,0:T(8,128)}), f32[96,768]{1,0:T(8,128)}) %reduce-scatter.11.cloned.1.call-update) | async-done | bytes 294928 | tf_op jit(solution)/shard_map/reduce_scatter | solution.py:47
  837.8 142.0 %reduce-scatter.9.cloned.1.call-done = f32[768,96]{0,1:T(8,128)} async-done(((f32[768,3072]{0,1:T(8,128)}), f32[768,96]{0,1:T(8,128)}) %reduce-scatter.9.cloned.1.call-update) | async-done | bytes 294928 | tf_op jit(solution)/shard_map/reduce_scatter | solution.py:46
  (261 shorter events, 263.4 us)
Async XLA Ops:
  7.2 66.8 %all-gather.5.cloned.1.call-start = ((), (), s32[]{:S(2)}) async-start(), calls=%async_computation.4 | async-start | bytes 3649536 | tf_op jit(solution)/shard_map/all_gather | solution.py:37
  7.9 212.6 %all-gather.7.cloned.1.call-start = ((), (), s32[]{:S(2)}) async-start(), calls=%async_computation.5 | async-start | bytes 1216512 | tf_op jit(solution)/shard_map/all_gather | solution.py:38
  8.7 217.2 %all-gather.9.cloned.1.call-start = ((), (), s32[]{:S(2)}) async-start(), calls=%async_computation.6 | async-start | bytes 4866048 | tf_op jit(solution)/shard_map/all_gather | solution.py:37
  9.4 251.2 %all-gather.11.cloned.1.call-start = ((), (), s32[]{:S(2)}) async-start(), calls=%async_computation.7 | async-start | bytes 4866048 | tf_op jit(solution)/shard_map/all_gather | solution.py:38
  10.0 679.9 %reduce-scatter.7.cloned.1.call-start = ((), (), s32[]{:S(2)}) async-start(), calls=%async_computation.9 | async-start | bytes 2433024 | tf_op jit(solution)/shard_map/reduce_scatter | solution.py:47
  56.7 17.2 %copy-start.39 = (f32[768]{0:T(1024)}, f32[768]{0:T(1024)S(1)}, u32[]{:S(2)}) copy-start(f32[768]{0:T(1024)S(1)} %convert_element_type.74) | copy-start | bytes 9220
  56.7 17.2 %copy-start.24 = (f32[768]{0:T(1024)}, f32[768]{0:T(1024)S(1)}, u32[]{:S(2)}) copy-start(f32[768]{0:T(1024)S(1)} %convert_element_type.73) | copy-start | bytes 9220
  59.7 14.3 %copy-start.1 = (bf16[1024,768]{0,1:T(8,128)(2,1)}, bf16[1024,768]{0,1:T(8,128)(2,1)S(1)}, u32[]{:S(2)}) copy-start(bf16[1024,768]{0,1:T(8,128)(2,1)S(1)} %copy.50) | copy-start | bytes 4718596
  223.8 69.5 %copy-start.22 = (f32[1024]{0:T(1024)}, f32[1024]{0:T(1024)S(1)}, u32[]{:S(2)}) copy-start(f32[1024]{0:T(1024)S(1)} %broadcast_multiply_fusion) | copy-start | bytes 12292
  225.8 67.5 %copy-start.30 = (f32[1024]{0:T(1024)}, f32[1024]{0:T(1024)S(1)}, u32[]{:S(2)}) copy-start(f32[1024]{0:T(1024)S(1)} %fusion.100) | copy-start | bytes 12292
  225.8 34.8 %copy-start.42 = (pred[1024]{0:T(1024)(128)(4,1)S(1)}, pred[1024]{0:T(1024)(128)(4,1)}, u32[]{:S(2)}) copy-start(pred[1024]{0:T(1024)(128)(4,1)} %iota_compare_fusion.4) | copy-start | bytes 3076
  260.6 17.3 %copy-start.44 = (bf16[768,3072]{0,1:T(8,128)(2,1)S(1)}, bf16[768,3072]{0,1:T(8,128)(2,1)}, u32[]{:S(2)}) copy-start(bf16[768,3072]{0,1:T(8,128)(2,1)} %all-gather.9.cloned.1.call-done) | copy-start | bytes 14155780
  300.6 395.7 %reduce-scatter.5.cloned.1.call-start = ((), (), s32[]{:S(2)}) async-start(), calls=%async_computation.8 | async-start | bytes 7299072 | tf_op jit(solution)/shard_map/reduce_scatter | solution.py:46
  349.9 14.1 %copy-start = (bf16[6,512,1024]{2,1,0:T(8,128)(2,1)S(1)}, bf16[6,512,1024]{2,1,0:T(8,128)(2,1)}, u32[]{:S(2)}) copy-start(bf16[6,512,1024]{2,1,0:T(8,128)(2,1)} %multiply_convert_fusion.15) | copy-start | bytes 18874372 | tf_op jit(solution)/shard_map/while
  350.0 14.1 %copy-start.13 = (bf16[4,512,6,64]{1,3,2,0:T(8,128)(2,1)S(1)}, bf16[4,512,6,64]{1,3,2,0:T(8,128)(2,1)}, u32[]{:S(2)}) copy-start(bf16[4,512,6,64]{1,3,2,0:T(8,128)(2,1)} %get-tuple-element.562) | copy-start | bytes 4718596 | tf_op jit(solution)/shard_map/while
  413.1 14.1 %copy-start = (bf16[6,512,1024]{2,1,0:T(8,128)(2,1)S(1)}, bf16[6,512,1024]{2,1,0:T(8,128)(2,1)}, u32[]{:S(2)}) copy-start(bf16[6,512,1024]{2,1,0:T(8,128)(2,1)} %multiply_convert_fusion.15) | copy-start | bytes 18874372 | tf_op jit(solution)/shard_map/while
  413.1 14.1 %copy-start.13 = (bf16[4,512,6,64]{1,3,2,0:T(8,128)(2,1)S(1)}, bf16[4,512,6,64]{1,3,2,0:T(8,128)(2,1)}, u32[]{:S(2)}) copy-start(bf16[4,512,6,64]{1,3,2,0:T(8,128)(2,1)} %get-tuple-element.562) | copy-start | bytes 4718596 | tf_op jit(solution)/shard_map/while
  476.0 14.1 %copy-start = (bf16[6,512,1024]{2,1,0:T(8,128)(2,1)S(1)}, bf16[6,512,1024]{2,1,0:T(8,128)(2,1)}, u32[]{:S(2)}) copy-start(bf16[6,512,1024]{2,1,0:T(8,128)(2,1)} %multiply_convert_fusion.15) | copy-start | bytes 18874372 | tf_op jit(solution)/shard_map/while
  476.0 14.1 %copy-start.13 = (bf16[4,512,6,64]{1,3,2,0:T(8,128)(2,1)S(1)}, bf16[4,512,6,64]{1,3,2,0:T(8,128)(2,1)}, u32[]{:S(2)}) copy-start(bf16[4,512,6,64]{1,3,2,0:T(8,128)(2,1)} %get-tuple-element.562) | copy-start | bytes 4718596 | tf_op jit(solution)/shard_map/while
  539.2 14.1 %copy-start = (bf16[6,512,1024]{2,1,0:T(8,128)(2,1)S(1)}, bf16[6,512,1024]{2,1,0:T(8,128)(2,1)}, u32[]{:S(2)}) copy-start(bf16[6,512,1024]{2,1,0:T(8,128)(2,1)} %multiply_convert_fusion.15) | copy-start | bytes 18874372 | tf_op jit(solution)/shard_map/while
  539.2 14.1 %copy-start.13 = (bf16[4,512,6,64]{1,3,2,0:T(8,128)(2,1)S(1)}, bf16[4,512,6,64]{1,3,2,0:T(8,128)(2,1)}, u32[]{:S(2)}) copy-start(bf16[4,512,6,64]{1,3,2,0:T(8,128)(2,1)} %get-tuple-element.562) | copy-start | bytes 4718596 | tf_op jit(solution)/shard_map/while
  577.5 260.2 %reduce-scatter.11.cloned.1.call-start = ((), (), s32[]{:S(2)}) async-start(), calls=%async_computation.11 | async-start | bytes 9732096 | tf_op jit(solution)/shard_map/reduce_scatter | solution.py:47
  592.6 387.1 %reduce-scatter.9.cloned.1.call-start = ((), (), s32[]{:S(2)}) async-start(), calls=%async_computation.10 | async-start | bytes 9732096 | tf_op jit(solution)/shard_map/reduce_scatter | solution.py:46
  634.9 44.3 %copy-start.35 = (f32[1024]{0:T(1024)S(1)}, f32[1024]{0:T(1024)}, u32[]{:S(2)}) copy-start(f32[1024]{0:T(1024)} %copy-done.34) | copy-start | bytes 12292
  (42 other events, 151.0 us)
Sparse Core Ops, SparseCore 0:
  10.9 62.9 all-gather.4
  76.9 52.8 all-gather.6
  132.7 62.5 all-gather.8
  198.1 62.5 all-gather.10
  300.8 97.8 reduce-scatter.6
  577.7 118.6 reduce-scatter.4
  702.8 134.8 reduce-scatter.10
  845.2 134.4 reduce-scatter.8
where the time goes:
time: 993 us; the launch traced here: 987 us
  matrix products  413 us (42%)
  waiting for transfers between devices  326 us (33%)
  blocking collectives  82.5 us (8%)
  other arithmetic  76.1 us (8%)
  local copies, waits for them, and re-layouts  50.6 us (5%)
  loops' own time  22.6 us (2%)
  between operations  15.6 us (2%)
    reduce_scatter x2, waiting for transfers between devices, spread(): lax.psum_scatter(grad_left, ('dp', 'fsdp'), scatter_dimension=1, tiled=True)  148 us
    reduce_scatter x2, waiting for transfers between devices, spread(): lax.psum_scatter(grad_right, ('dp', 'fsdp'), scatter_dimension=0, tiled=T...  141 us
    sub x4, matrix products, one_item(): grad_weights * signed - delta  132 us
    unnamed x2, blocking collectives  82.5 us
    dot_general x8, matrix products, masked_scores(): jnp.einsum('qhe,khe->hqk', query_rows, keys_seq, preferred_element_type=j...  59.4 us
    dot_general x4, matrix products, one_item(): jnp.einsum('hqk,qhe->khe', weights_low, grad_rows, preferred_element_type...  56.3 us
    dot_general x4, matrix products, one_item(): jnp.einsum('hqk,khe->qhe', weights_low, values_seq, preferred_element_typ...  40.6 us
    dot_general x4, matrix products, contract_cols(): lax.dot_general(left_mat, right_mat, (((1,), (1,)), ((), ())), preferred_...  37.6 us
  transfers between devices with their start and end apart: 8, of which 5 were waited for; matrix products, arithmetic and copies ran while one was open for 50% of the time, Pallas kernels for 0%

commit v1 on v0

v1 whole, which is shorter than its diff:
```python
import functools
import math

import jax
import jax.numpy as jnp
from jax import lax
from jax.experimental import pallas as pl
from jax.experimental.pallas import tpu as pltpu
from jax.sharding import PartitionSpec as P

F32 = jnp.float32
BF16 = jnp.bfloat16
HEAD = 64
PAIR = 2 * HEAD
EPSILON = 1e-05
NEGATIVE = -1e30
TILE = 256
AXES = ("dp", "fsdp")
VMEM_LIMIT = 56 << 20
GELU_A = math.sqrt(2.0 / math.pi)
GELU_B = GELU_A * 0.044715


def mm_nn(left, right):
    return jnp.dot(left, right, preferred_element_type=F32)


def mm_nt(left, right):
    return lax.dot_general(left, right, (((1,), (1,)), ((), ())), preferred_element_type=F32)


def mm_tn(left, right):
    return lax.dot_general(left, right, (((0,), (0,)), ((), ())), preferred_element_type=F32)


def norm_stats(values):
    average = jnp.mean(values, axis=-1, keepdims=True)
    centred = values - average
    variance = jnp.mean(centred * centred, axis=-1, keepdims=True)
    rinv = lax.rsqrt(variance + EPSILON)
    return centred * rinv, rinv


def params(**kw):
    return pltpu.CompilerParams(vmem_limit_bytes=VMEM_LIMIT, **kw)


class Plan:
    def __init__(self, mesh):
        self.n = mesh.shape["dp"] * mesh.shape["fsdp"]
        self.bits = self.n.bit_length() - 1
        self.direct = self.n == 1 << self.bits and 4 <= self.bits <= 5
        self.stages = [tuple(range(3, self.bits)), (1, 2)]

    @staticmethod
    def masks_of(bits):
        found = [0]
        for bit in bits:
            found = found + [m | 1 << bit for m in found]
        return found

    def slot_masks(self):
        masks = [0]
        for stage in self.stages:
            masks = [m ^ k for m in self.masks_of(stage) for k in masks]
        return masks

    def swap(self, value, mask):
        return lax.ppermute(value, AXES, [(i, i ^ mask) for i in range(self.n)])

    def gather(self, piece):
        held = piece[None]
        for stage in self.stages:
            masks = self.masks_of(stage)
            held = jnp.concatenate([held] + [self.swap(held, m) for m in masks[1:]], axis=0)
        return held, self.swap(held, 1)

    def scatter(self, keep, send):
        held = add_low(keep, [self.swap(send, 1)])
        for stage in reversed(self.stages):
            masks = self.masks_of(stage)
            parts = jnp.split(held, len(masks), axis=0)
            held = add_low(parts[0], [self.swap(p, m) for p, m in zip(parts[1:], masks[1:])])
        return held[0]


def add_low(first, others):
    total = first.astype(F32)
    for other in others:
        total = total + other.astype(F32)
    return total.astype(first.dtype)


def slot_of(masks, me, piece_pair):
    wanted = piece_pair ^ lax.div(me, 2)
    slot = jnp.int32(0)
    for s, m in enumerate(masks):
        slot = jnp.where(wanted == m // 2, s, slot)
    return slot


def qkv_kernel(masks, ppr, me_ref, x_ref, own_ref, sib_ref, e_ref, m_ref, mixed_ref, n1_ref, w_ref, vec_ref):
    me = me_ref[0]

    @pl.when(pl.program_id(0) == 0)
    def _():
        core = lax.rem(me, 2)
        for s, m in enumerate(masks):
            pair = lax.div(me, 2) ^ (m // 2)
            at = pl.ds(pl.multiple_of(pair * (2 * ppr), 16), 2 * ppr)

            @pl.when(core == 0)
            def _():
                w_ref[at, :] = jnp.concatenate([own_ref[s, :ppr, :], sib_ref[s, :ppr, :]], axis=0)

            @pl.when(core == 1)
            def _():
                w_ref[at, :] = jnp.concatenate([sib_ref[s, :ppr, :], own_ref[s, :ppr, :]], axis=0)

        packed = jnp.concatenate(
            [own_ref[:, ppr, :128].astype(F32), sib_ref[:, ppr, :128].astype(F32)], axis=0
        )
        for v in range(4):
            spread = jnp.dot(packed, e_ref[v], preferred_element_type=F32, precision=lax.Precision.HIGHEST)
            vec_ref[v : v + 1, :] = jnp.sum(spread * m_ref[...], axis=0, keepdims=True)

    xhat, rinv = norm_stats(x_ref[...].astype(F32))
    n1 = (xhat * vec_ref[0:1, :] + vec_ref[1:2, :]).astype(BF16)
    n1_ref[...] = n1
    mixed_ref[...] = mm_nt(n1, w_ref[...]).astype(BF16)


def qkv_project(plan, me, tokens, own, sib, spread, place, out_cols, rows_block=256):
    rows, width = tokens.shape
    masks = plan.slot_masks()
    full = lambda a: pl.BlockSpec(a.shape, lambda r, *_: (0,) * a.ndim)
    whole = lambda shape: pl.BlockSpec(shape, lambda r, *_: (0,) * len(shape))
    return pl.pallas_call(
        functools.partial(qkv_kernel, masks, out_cols // plan.n),
        grid_spec=pltpu.PrefetchScalarGridSpec(
            num_scalar_prefetch=1,
            grid=(rows // rows_block,),
            in_specs=[
                pl.BlockSpec((rows_block, width), lambda r, *_: (r, 0)),
                full(own), full(sib), full(spread), full(place),
            ],
            out_specs=[
                pl.BlockSpec((rows_block, out_cols), lambda r, *_: (r, 0)),
                pl.BlockSpec((rows_block, width), lambda r, *_: (r, 0)),
                whole((out_cols, width)), whole((8, width)),
            ],
        ),
        out_shape=[
            jax.ShapeDtypeStruct((rows, out_cols), BF16),
            jax.ShapeDtypeStruct((rows, width), BF16),
            jax.ShapeDtypeStruct((out_cols, width), BF16),
            jax.ShapeDtypeStruct((8, width), F32),
        ],
        compiler_params=params(),
        name="qkv_project",
    )(me, tokens, own, sib, spread, place)


def qkv_plain_kernel(x_ref, w_ref, vec_ref, mixed_ref, n1_ref):
    xhat, rinv = norm_stats(x_ref[...].astype(F32))
    n1 = (xhat * vec_ref[0:1, :] + vec_ref[1:2, :]).astype(BF16)
    n1_ref[...] = n1
    mixed_ref[...] = mm_nt(n1, w_ref[...]).astype(BF16)


def qkv_plain(tokens, w_abs, vecs, rows_block=256):
    rows, width = tokens.shape
    out_cols = w_abs.shape[0]
    full = lambda a: pl.BlockSpec(a.shape, lambda r: (0,) * a.ndim)
    return pl.pallas_call(
        qkv_plain_kernel,
        grid=(rows // rows_block,),
        in_specs=[pl.BlockSpec((rows_block, width), lambda r: (r, 0)), full(w_abs), full(vecs)],
        out_specs=[
            pl.BlockSpec((rows_block, out_cols), lambda r: (r, 0)),
            pl.BlockSpec((rows_block, width), lambda r: (r, 0)),
        ],
        out_shape=[
            jax.ShapeDtypeStruct((rows, out_cols), BF16),
            jax.ShapeDtypeStruct((rows, width), BF16),
        ],
        compiler_params=params(),
        name="qkv_plain",
    )(tokens, w_abs, vecs)


def attend_kernel(maxlen, len_ref, q_ref, k_ref, v_ref, att_ref, attT_ref, lse_ref):
    length = len_ref[pl.program_id(0)]
    qT = (q_ref[...].astype(F32) * HEAD**-0.5).T.astype(BF16)
    vT = v_ref[...].astype(F32).T.astype(BF16)
    k = k_ref[...]
    for i in range(maxlen // TILE):
        lo, hi = i * TILE, (i + 1) * TILE
        qpos = lo + lax.broadcasted_iota(jnp.int32, (1, TILE), 1)
        limit = jnp.minimum(qpos, length - 1)
        kpos = lax.broadcasted_iota(jnp.int32, (hi, TILE), 0)
        blank = jnp.zeros((HEAD, TILE), BF16)
        outs = []
        for h in range(2):
            own = qT[h * HEAD : (h + 1) * HEAD, lo:hi]
            own = jnp.concatenate([own, blank] if h == 0 else [blank, own], axis=0)
            s = mm_nn(k[:hi], own)
            t = s * s + 1.0
            magnitude = jnp.where(kpos <= limit, t * lax.rsqrt(t), NEGATIVE)
            top = jnp.max(magnitude, axis=0, keepdims=True)
            e = jnp.exp(magnitude - top)
            total = jnp.sum(e, axis=0, keepdims=True)
            weights = (jnp.tanh(s) * e).astype(BF16)
            outs.append(mm_nn(vT[h * HEAD : (h + 1) * HEAD, :hi], weights) / total)
            lse_ref[0, h : h + 1, lo:hi] = jnp.where(qpos >= length, -NEGATIVE, top + jnp.log(total))
        outT = jnp.concatenate(outs, axis=0)
        attT_ref[:, lo:hi] = outT.astype(BF16)
        att_ref[lo:hi, :] = outT.T.astype(BF16)


def attend_forward(mixed, lengths):
    rows, width = mixed.shape[0], mixed.shape[1] // 3
    seqs = lengths.shape[0]
    maxlen, pairs = rows // seqs, width // PAIR
    col = lambda part: pl.BlockSpec((maxlen, PAIR), lambda s, p, *_: (s, part * pairs + p))
    return pl.pallas_call(
        functools.partial(attend_kernel, maxlen),
        grid_spec=pltpu.PrefetchScalarGridSpec(
            num_scalar_prefetch=1,
            grid=(seqs, pairs),
            in_specs=[col(0), col(1), col(2)],
            out_specs=[
                col(0),
                pl.BlockSpec((PAIR, maxlen), lambda s, p, *_: (p, s)),
                pl.BlockSpec((1, 8, maxlen), lambda s, p, *_: (s * pairs + p, 0, 0)),
            ],
        ),
        out_shape=[
            jax.ShapeDtypeStruct((rows, width), BF16),
            jax.ShapeDtypeStruct((width, rows), BF16),
            jax.ShapeDtypeStruct((seqs * pairs, 8, maxlen), F32),
        ],
        compiler_params=params(),
        name="attend_forward",
    )(lengths, mixed, mixed, mixed)


def attend_back_kernel(maxlen, q_ref, k_ref, v_ref, ga_ref, attT_ref, lse_ref, dq_ref, dk_ref, dv_ref, dqT):
    qs = q_ref[...] * jnp.asarray(HEAD**-0.5, BF16)
    k, v, ga = k_ref[...], v_ref[...], ga_ref[...]
    qT = qs.astype(F32).T.astype(BF16)
    kT = k.astype(F32).T.astype(BF16)
    gaT32 = ga.astype(F32).T
    gaT = gaT32.astype(BF16)
    prod = gaT32 * attT_ref[...].astype(F32)
    lane = lax.broadcasted_iota(jnp.int32, (maxlen, PAIR), 1)
    blank = jnp.zeros((HEAD, maxlen), BF16)
    nil = jnp.zeros((), BF16)
    heads = []
    for h in range(2):
        mine = (lane < HEAD) if h == 0 else (lane >= HEAD)
        at = slice(h * HEAD, (h + 1) * HEAD)
        pad = lambda a: jnp.concatenate([a, blank] if h == 0 else [blank, a], axis=0)
        heads.append(
            (
                jnp.where(mine, ga, nil), jnp.where(mine, qs, nil), pad(qT[at]), pad(gaT[at]), kT[at],
                jnp.sum(prod[at], axis=0, keepdims=True), lse_ref[0, h : h + 1, :],
            )
        )
    for j in range(maxlen // TILE):
        lo, hi = j * TILE, (j + 1) * TILE
        dv = dk = None
        for h in range(2):
            ga_h, q_h, qT_h, gaT_h, kT_h, delta, lse = heads[h]
            s = mm_nn(k[lo:hi], qT_h[:, lo:])
            gw = mm_nn(v[lo:hi], gaT_h[:, lo:])
            t = s * s + 1.0
            r = lax.rsqrt(t)
            p = jnp.exp(t * r - lse[:, lo:])
            kpos = lax.broadcasted_iota(jnp.int32, s.shape, 0)
            qpos = lax.broadcasted_iota(jnp.int32, s.shape, 1)
            p = jnp.where(kpos <= qpos, p, 0.0)
            g = jnp.tanh(s)
            w = g * p
            c = p * (s * r)
            a = p + g * (c - w)
            ds = (gw * a - c * delta[:, lo:]).astype(BF16)
            dv_h = mm_nn(w.astype(BF16), ga_h[lo:])
            dk_h = mm_nn(ds, q_h[lo:])
            dv = dv_h if dv is None else dv + dv_h
            dk = dk_h if dk is None else dk + dk_h
            dq_h = mm_nn(kT_h[:, lo:hi], ds)
            if j == 0:
                dqT[h * HEAD : (h + 1) * HEAD, :] = dq_h
            else:
                dqT[h * HEAD : (h + 1) * HEAD, lo:] += dq_h
        dv_ref[lo:hi, :] = dv.astype(BF16)
        dk_ref[lo:hi, :] = dk.astype(BF16)
    dq_ref[...] = (dqT[...] * HEAD**-0.5).T.astype(BF16)


def attend_backward(mixed, ga, attT, lse, seqs):
    rows, width = mixed.shape[0], mixed.shape[1] // 3
    maxlen, pairs = rows // seqs, width // PAIR
    col = lambda part: pl.BlockSpec((maxlen, PAIR), lambda s, p: (s, part * pairs + p))
    return pl.pallas_call(
        functools.partial(attend_back_kernel, maxlen),
        grid=(seqs, pairs),
        in_specs=[
            col(0), col(1), col(2), col(0),
            pl.BlockSpec((PAIR, maxlen), lambda s, p: (p, s)),
            pl.BlockSpec((1, 8, maxlen), lambda s, p: (s * pairs + p, 0, 0)),
        ],
        out_specs=[col(0)] * 3,
        out_shape=[jax.ShapeDtypeStruct((rows, width), BF16)] * 3,
        scratch_shapes=[pltpu.VMEM((PAIR, maxlen), F32)],
        compiler_params=params(),
        name="attend_backward",
    )(mixed, mixed, mixed, ga, attT, lse)


def project_kernel(att_ref, x_ref, wo_ref, vec_ref, res_ref, n2_ref):
    residual = x_ref[...].astype(F32) + mm_nn(att_ref[...], wo_ref[...])
    res_ref[...] = residual
    xhat, rinv = norm_stats(residual)
    n2_ref[...] = (xhat * vec_ref[2:3, :] + vec_ref[3:4, :]).astype(BF16)


def project_out(att, tokens, wo, vecs, rows_block=256):
    rows, width = tokens.shape
    block = pl.BlockSpec((rows_block, width), lambda r: (r, 0))
    full = lambda a: pl.BlockSpec(a.shape, lambda r: (0,) * a.ndim)
    return pl.pallas_call(
        project_kernel,
        grid=(rows // rows_block,),
        in_specs=[block, block, full(wo), full(vecs)],
        out_specs=[block, block],
        out_shape=[jax.ShapeDtypeStruct((rows, width), F32), jax.ShapeDtypeStruct((rows, width), BF16)],
        compiler_params=params(),
        name="project_out",
    )(att, tokens, wo, vecs)


def live_grad(cot, lengths_ref, maxlen, first_row):
    rows = cot.shape[0]
    at = first_row + lax.broadcasted_iota(jnp.int32, (rows, 1), 0)
    seq = first_row // maxlen
    return jnp.where(at - seq * maxlen < lengths_ref[seq], cot, 0.0)


def mlp_kernel(maxlen, len_ref, n2_ref, res_ref, cot_ref, w_ref, out_ref, gn_ref, gw_ref, gl_s, acc_s):
    step = pl.program_id(0)
    units = w_ref.shape[2]
    rows, width = n2_ref.shape

    @pl.when(step == 0)
    def _():
        for first in range(0, rows, maxlen):
            at = slice(first, first + maxlen)
            gl_s[at, :] = live_grad(cot_ref[at, :], len_ref, maxlen, first).astype(BF16)

    pieces = w_ref.shape[0]
    wu = w_ref[:, 0].reshape(pieces * units, width)
    wd = w_ref[:, 1].reshape(pieces * units, width)
    n2, gl = n2_ref[...], gl_s[...]
    u = mm_nt(n2, wu)
    uu = u * u
    th = jnp.tanh(u * (GELU_A + GELU_B * uu))
    half = 0.5 * u
    act = (half + half * th).astype(BF16)
    slope = 0.5 + 0.5 * th + (half - half * (th * th)) * (GELU_A + (3.0 * GELU_B) * uu)
    gp = (mm_nt(gl, wd) * slope).astype(BF16)
    out = mm_nn(act, wd)
    gn = mm_nn(gp, wu)

    @pl.when(step == 0)
    def _():
        acc_s[...] = out + res_ref[...]
        gn_ref[...] = gn

    @pl.when(step > 0)
    def _():
        acc_s[...] += out
        gn_ref[...] += gn

    gw_ref[:, 0] = mm_tn(gp, n2).astype(BF16).reshape(pieces, units, width)
    gw_ref[:, 1] = mm_tn(act, gl).astype(BF16).reshape(pieces, units, width)

    @pl.when(step == pl.num_programs(0) - 1)
    def _():
        out_ref[...] = acc_s[...].astype(BF16)


def feed_forward(lengths, n2, residual, cot, w):
    rows, width = n2.shape
    pieces, _, units, _ = w.shape
    take = max(1, 768 // units)
    full = lambda: pl.BlockSpec((rows, width), lambda f, *_: (0, 0))
    chunk = pl.BlockSpec((take, 2, units, width), lambda f, *_: (f, 0, 0, 0))
    return pl.pallas_call(
        functools.partial(mlp_kernel, rows // lengths.shape[0]),
        grid_spec=pltpu.PrefetchScalarGridSpec(
            num_scalar_prefetch=1,
            grid=(pieces // take,),
            in_specs=[full(), full(), full(), chunk],
            out_specs=[full(), full(), chunk],
            scratch_shapes=[pltpu.VMEM((rows, width), BF16), pltpu.VMEM((rows, width), F32)],
        ),
        out_shape=[
            jax.ShapeDtypeStruct((rows, width), BF16),
            jax.ShapeDtypeStruct((rows, width), F32),
            jax.ShapeDtypeStruct(w.shape, BF16),
        ],
        compiler_params=params(),
        name="feed_forward",
    )(lengths, n2, residual, cot, w)


def norm_back(grad, xhat, rinv, gain):
    dh = grad * gain
    first = jnp.mean(dh, axis=-1, keepdims=True)
    second = jnp.mean(dh * xhat, axis=-1, keepdims=True)
    return rinv * (dh - first - xhat * second)


def middle_kernel(maxlen, len_ref, gn_ref, res_ref, cot_ref, att_ref, wo_ref, vec_ref, gres_ref, ga_ref, gwo_ref, gvec_ref, acc_s):
    step = pl.program_id(0)
    rows = gn_ref.shape[0]
    gn = gn_ref[...]
    xhat, rinv = norm_stats(res_ref[...])
    gres = live_grad(cot_ref[...], len_ref, maxlen, step * rows) + norm_back(gn, xhat, rinv, vec_ref[2:3, :])
    gres_ref[...] = gres
    low = gres.astype(BF16)
    ga_ref[...] = mm_nt(low, wo_ref[...]).astype(BF16)
    gwo = mm_tn(att_ref[...], low)
    ggain = jnp.sum(gn * xhat, axis=0, keepdims=True)
    gshift = jnp.sum(gn, axis=0, keepdims=True)

    @pl.when(step == 0)
    def _():
        acc_s[...] = gwo
        gvec_ref[...] = jnp.zeros_like(gvec_ref)

    @pl.when(step > 0)
    def _():
        acc_s[...] += gwo

    gvec_ref[0:1, :] += ggain
    gvec_ref[1:2, :] += gshift

    @pl.when(step == pl.num_programs(0) - 1)
    def _():
        gwo_ref[...] = acc_s[...].astype(BF16)


def middle_back(lengths, gn, residual, cot, att, wo, vecs, rows_block=256):
    rows, width = gn.shape
    block = pl.BlockSpec((rows_block, width), lambda r, *_: (r, 0))
    full = lambda shape: pl.BlockSpec(shape, lambda r, *_: (0,) * len(shape))
    return pl.pallas_call(
        functools.partial(middle_kernel, rows // lengths.shape[0]),
        grid_spec=pltpu.PrefetchScalarGridSpec(
            num_scalar_prefetch=1,
            grid=(rows // rows_block,),
            in_specs=[block, block, block, block, full(wo.shape), full(vecs.shape)],
            out_specs=[block, block, full(wo.shape), full((8, width))],
            scratch_shapes=[pltpu.VMEM(wo.shape, F32)],
        ),
        out_shape=[
            jax.ShapeDtypeStruct((rows, width), F32),
            jax.ShapeDtypeStruct((rows, width), BF16),
            jax.ShapeDtypeStruct(wo.shape, BF16),
            jax.ShapeDtypeStruct((8, width), F32),
        ],
        compiler_params=params(),
        name="middle_back",
    )(lengths, gn, residual, cot, att, wo, vecs)


def qkv_grad_kernel(masks, ppr, opr, me_ref, dq_ref, dk_ref, dv_ref, n1_ref, gwo_ref, keep_ref, send_ref, low_s):
    width = n1_ref.shape[1]
    n1 = n1_ref[...]
    for part, ref in enumerate((dq_ref, dk_ref, dv_ref)):
        low_s[part * width : (part + 1) * width, :] = mm_tn(ref[...], n1).astype(BF16)
    me = me_ref[0]
    core = lax.rem(me, 2)
    for pair in range(len(masks)):
        slot = slot_of(masks, me, pair)
        w0 = low_s[2 * pair * ppr : (2 * pair + 1) * ppr, :]
        w1 = low_s[(2 * pair + 1) * ppr : (2 * pair + 2) * ppr, :]
        o0 = gwo_ref[2 * pair * opr : (2 * pair + 1) * opr, :]
        o1 = gwo_ref[(2 * pair + 1) * opr : (2 * pair + 2) * opr, :]
        for side, (own_w, own_o, sib_w, sib_o) in enumerate(((w0, o0, w1, o1), (w1, o1, w0, o0))):

            @pl.when(core == side)
            def _():
                keep_ref[slot] = jnp.concatenate([own_w, own_o], axis=0)
                send_ref[slot] = jnp.concatenate([sib_w, sib_o], axis=0)


def qkv_grad(plan, me, dq, dk, dv, n1, gwo):
    rows, width = n1.shape
    masks = plan.slot_masks()
    ppr, opr = 3 * width // plan.n, width // plan.n
    vm = pl.BlockSpec(memory_space=pltpu.VMEM)
    shape = jax.ShapeDtypeStruct((len(masks), ppr + opr, width), BF16)
    return pl.pallas_call(
        functools.partial(qkv_grad_kernel, masks, ppr, opr),
        in_specs=[pl.BlockSpec(memory_space=pltpu.SMEM)] + [vm] * 5,
        out_specs=[vm, vm],
        out_shape=[shape, shape],
        scratch_shapes=[pltpu.VMEM((3 * width, width), BF16)],
        compiler_params=params(),
        name="qkv_grad",
    )(me, dq, dk, dv, n1, gwo)


def qkv_grad_plain_kernel(d_ref, n1_ref, out_ref):
    out_ref[...] = mm_tn(d_ref[...], n1_ref[...]).astype(BF16)


def qkv_grad_plain(dq, dk, dv, n1):
    rows, width = n1.shape
    vm = pl.BlockSpec(memory_space=pltpu.VMEM)
    call = pl.pallas_call(
        qkv_grad_plain_kernel,
        in_specs=[vm, vm],
        out_specs=vm,
        out_shape=jax.ShapeDtypeStruct((width, width), BF16),
        compiler_params=params(),
        name="qkv_grad_plain",
    )
    return jnp.concatenate([call(d, n1) for d in (dq, dk, dv)], axis=0)


def first_kernel(dq_ref, dk_ref, dv_ref, w_ref, x_ref, gres_ref, vec_ref, gtok_ref, gvec_ref):
    width = x_ref.shape[1]
    gn = mm_nn(dq_ref[...], w_ref[:width, :])
    gn += mm_nn(dk_ref[...], w_ref[width : 2 * width, :])
    gn += mm_nn(dv_ref[...], w_ref[2 * width :, :])
    xhat, rinv = norm_stats(x_ref[...].astype(F32))
    gtok_ref[...] = gres_ref[...] + norm_back(gn, xhat, rinv, vec_ref[0:1, :])

    @pl.when(pl.program_id(0) == 0)
    def _():
        gvec_ref[...] = jnp.zeros_like(gvec_ref)

    gvec_ref[0:1, :] += jnp.sum(gn * xhat, axis=0, keepdims=True)
    gvec_ref[1:2, :] += jnp.sum(gn, axis=0, keepdims=True)


def first_back(dq, dk, dv, w_abs, tokens, gres, vecs, rows_block=256):
    rows, width = tokens.shape
    block = pl.BlockSpec((rows_block, width), lambda r: (r, 0))
    full = lambda shape: pl.BlockSpec(shape, lambda r: (0,) * len(shape))
    return pl.pallas_call(
        first_kernel,
        grid=(rows // rows_block,),
        in_specs=[block, block, block, full(w_abs.shape), block, block, full(vecs.shape)],
        out_specs=[block, full((8, width))],
        out_shape=[jax.ShapeDtypeStruct((rows, width), F32), jax.ShapeDtypeStruct((8, width), F32)],
        compiler_params=params(),
        name="first_back",
    )(dq, dk, dv, w_abs, tokens, gres, vecs)


def body(plan, tokens, lengths, ln1_gain, ln1_shift, w_qkv, w_out, ln2_gain, ln2_shift, w_up, w_down, cot):
    rows, width = tokens.shape
    n = plan.n
    seqs = lengths.shape[0]
    me = lax.axis_index(AXES).astype(jnp.int32)
    me_arr = me[None]
    vec_piece = jnp.stack([ln1_gain, ln1_shift, ln2_gain, ln2_shift])
    per = vec_piece.shape[1]
    qkv_piece = w_qkv.T
    ppr, units = qkv_piece.shape[0], w_down.shape[0]
    ff = units * n

    mlp_piece = jnp.concatenate([w_up.T, w_down, w_out], axis=0)
    mlp_all = lax.all_gather(mlp_piece, AXES, axis=0, tiled=True).reshape(n, -1, width)
    wo = mlp_all[:, 2 * units :].reshape(width, width)
    w_ff = mlp_all[:, : 2 * units].reshape(n, 2, units, width)
    if units % 16 or 768 % units:
        w_ff = w_ff.transpose(1, 0, 2, 3).reshape(2, ff // 768, 768, width).transpose(1, 0, 2, 3)

    if plan.direct:
        flat = jnp.pad(vec_piece.reshape(1, -1), ((0, 7), (0, width - 4 * per)))
        own, sib = plan.gather(jnp.concatenate([qkv_piece, flat], axis=0))
        slots = jnp.array(plan.slot_masks() + [m ^ 1 for m in plan.slot_masks()], jnp.int32)
        column = jnp.arange(width, dtype=jnp.int32)
        place = ((slots ^ me)[:, None] == (column // per)[None]).astype(F32)
        lane = jnp.arange(128, dtype=jnp.int32)
        spread = jnp.stack([(lane[:, None] == v * per + (column % per)[None]).astype(F32) for v in range(4)])
        mixed, n1, w_abs, vecs = qkv_project(plan, me_arr, tokens, own, sib, spread, place, ppr * n)
    else:
        w_abs = lax.all_gather(qkv_piece, AXES, axis=0, tiled=True)
        vecs = lax.all_gather(vec_piece, AXES, axis=1, tiled=True).astype(F32)
        vecs = jnp.pad(vecs, ((0, 4), (0, 0)))
        mixed, n1 = qkv_plain(tokens, w_abs, vecs)

    att, attT, lse = attend_forward(mixed, lengths)
    residual, n2 = project_out(att, tokens, wo, vecs)
    output, gn2, gw_ff = feed_forward(lengths, n2, residual, cot, w_ff)
    if units % 16 or 768 % units:
        gw_ff = gw_ff.transpose(1, 0, 2, 3).reshape(2, n, units, width).transpose(1, 0, 2, 3)
    g_ff = lax.psum_scatter(gw_ff.reshape(n * 2 * units, width), AXES, scatter_dimension=0, tiled=True)
    gres, ga, gwo, gvec2 = middle_back(lengths, gn2, residual, cot, att, wo, vecs)
    dq, dk, dv = attend_backward(mixed, ga, attT, lse, seqs)
    if plan.direct:
        keep, send = qkv_grad(plan, me_arr, dq, dk, dv, n1, gwo)
        g_attn = plan.scatter(keep, send).astype(F32)
        g_qkv, g_out = g_attn[:ppr], g_attn[ppr:]
    else:
        g_qkv = lax.psum_scatter(qkv_grad_plain(dq, dk, dv, n1), AXES, scatter_dimension=0, tiled=True)
        g_out = lax.psum_scatter(gwo, AXES, scatter_dimension=0, tiled=True)
    gtok, gvec1 = first_back(dq, dk, dv, w_abs, tokens, gres, vecs)
    gvec = jnp.concatenate([gvec1[:2], gvec2[:2]], axis=0)
    if plan.direct:
        by_piece = gvec.reshape(4, n, per).transpose(1, 0, 2)
        by_slot = by_piece[slots ^ me]
        half = n // 2
        g_vec = plan.scatter(by_slot[:half], by_slot[half:])
    else:
        g_vec = lax.psum_scatter(gvec, AXES, scatter_dimension=1, tiled=True)
    g_ff = g_ff.astype(F32)
    return (
        output, gtok, g_vec[0], g_vec[1], g_qkv.astype(F32).T, g_out.astype(F32), g_vec[2], g_vec[3],
        g_ff[:units].T, g_ff[units:],
    )


def solution(mesh):
    both = AXES
    rows2, vec, cols2 = P(both, None), P(both), P(None, both)
    in_specs = (rows2, vec, vec, vec, cols2, rows2, vec, vec, cols2, rows2, rows2)
    out_specs = (rows2, rows2, vec, vec, cols2, rows2, vec, vec, cols2, rows2)
    return jax.shard_map(
        functools.partial(body, Plan(mesh)), mesh=mesh, in_specs=in_specs, out_specs=out_specs, check_vma=False
    )
```

time: 993 us -> 334 us (0.34)
  matrix products: 413 us -> 0 us
  waiting for transfers between devices: 326 us -> 105 us
  Pallas kernels: 0 us -> 159 us
  blocking collectives: 82.5 us -> 0 us
  other arithmetic: 76.1 us -> 9.51 us
  local copies, waits for them, and re-layouts: 50.6 us -> 17.4 us
  starting transfers between devices: 0.31 us -> 26.7 us
  loops' own time: 22.6 us -> 0 us
    dot_general x36 -> x0, matrix products: 281 us -> none  [the longest x8 59.4 us: masked_scores(): jnp.einsum('qhe,khe->hqk', query_rows, keys_seq, preferred_element_type=j...]
    reduce_scatter x4 -> x1, waiting for transfers between devices: 290 us -> 17.1 us  [body(): lax.psum_scatter(gw_ff.reshape(n * 2 * units, width), AXES, scatter_dimen...]
    pallas_call x0 -> x8, Pallas kernels: none -> 159 us  [the longest x1 42.1 us: feed_forward(): pl.pallas_call(functools.partial(mlp_kernel, rows // lengths.shape[0]), g...]
    sub x4 -> x0, matrix products: 132 us -> none  [one_item(): grad_weights * signed - delta]
    ppermute x0 -> x21, waiting for transfers between devices: none -> 83.1 us  [swap(): return lax.ppermute(value, AXES, [(i, i ^ mask) for i in range(self.n)])]
    unnamed x2 -> x0, blocking collectives: 82.5 us -> none
    reduce_sum x13 -> x0, other arithmetic: 54.6 us -> none  [the longest x4 34.1 us: one_item(): row_total = jnp.sum(exp_terms, axis=-1, keepdims=True)]
    all_gather x4 -> x1, waiting for transfers between devices: 33.3 us -> 4.68 us  [body(): lax.all_gather(mlp_piece, AXES, axis=0, tiled=True).reshape(n, -1, width)]
  transfers between devices with their start and end apart: 8 -> 23, of which waited for: 5 -> 17; matrix products, arithmetic and copies ran while one was open for 50% -> 3% of each run, Pallas kernels for 0% -> 33%
where the time goes in v1:
time: 334 us; the launch traced here: 333 us
  Pallas kernels  159 us (48%)
  waiting for transfers between devices  105 us (31%)
  starting transfers between devices  26.7 us (8%)
  local copies, waits for them, and re-layouts  17.4 us (5%)
  between operations  15 us (4%)
  other arithmetic  9.51 us (3%)
    ppermute x21, waiting for transfers between devices, swap(): return lax.ppermute(value, AXES, [(i, i ^ mask) for i in range(self.n)])  83.1 us
    pallas_call x1, Pallas kernels, feed_forward(): pl.pallas_call(functools.partial(mlp_kernel, rows // lengths.shape[0]), g...  42.1 us
    pallas_call x1, Pallas kernels, attend_backward(): pl.pallas_call(functools.partial(attend_back_kernel, maxlen), grid=(seqs,...  38.4 us
    pallas_call x1, Pallas kernels, attend_forward(): pl.pallas_call(functools.partial(attend_kernel, maxlen), grid_spec=pltpu....  31.3 us
    ppermute x21, starting transfers between devices, swap(): return lax.ppermute(value, AXES, [(i, i ^ mask) for i in range(self.n)])  26.6 us
    reduce_scatter x1, waiting for transfers between devices, body(): lax.psum_scatter(gw_ff.reshape(n * 2 * units, width), AXES, scatter_dimen...  17.1 us
    pallas_call x1, Pallas kernels, middle_back(): pl.pallas_call(functools.partial(middle_kernel, rows // lengths.shape[0])...  10.8 us
    pallas_call x1, Pallas kernels, qkv_project(): pl.pallas_call(functools.partial(qkv_kernel, masks, out_cols // plan.n),...  10.7 us
  transfers between devices with their start and end apart: 23, of which 17 were waited for; matrix products, arithmetic and copies ran while one was open for 3% of the time, Pallas kernels for 33%

profile of v1, /device:TPU:0, one launch (start us, length us, event | category | flops | bytes accessed | tf_op | source)
XLA Modules:
  0.0 332.8 jit_solution(8241379029904518208)
XLA Ops:
  10.8 3.1 collective-permute-start
  13.9 2.6 collective-permute-start.1
  18.5 7.7 %collective-permute-done.1 = bf16[1,80,768]{2,1,0:T(8,128)(2,1)S(1)} collective-permute-done((bf16[1,80,768]{2,1,0:T(8,128)(2,1)S(1)}, bf16[1,80,768]{2,1,0:T(8,128)(2,1)S(1)}, u32[]{:S(2)}, u32[]{:S(2)}) %collective-permute-start.1) | collective-permute-done | bytes 122912 | tf_op jit(solution)/shard_map/ppermute | solution.py:69
  30.0 10.3 %collective-permute-done.3 = bf16[4,80,768]{2,1,0:T(8,128)(2,1)S(1)} collective-permute-done((bf16[4,80,768]{2,1,0:T(8,128)(2,1)S(1)}, bf16[4,80,768]{2,1,0:T(8,128)(2,1)S(1)}, u32[]{:S(2)}, u32[]{:S(2)}) %collective-permute-start.3) | collective-permute-done | bytes 491552 | tf_op jit(solution)/shard_map/ppermute | solution.py:69
  42.1 15.1 %collective-permute-done.5 = bf16[4,80,768]{2,1,0:T(8,128)(2,1)S(1)} collective-permute-done((bf16[4,80,768]{2,1,0:T(8,128)(2,1)S(1)}, bf16[4,80,768]{2,1,0:T(8,128)(2,1)S(1)}, u32[]{:S(2)}, u32[]{:S(2)}) %collective-permute-start.5) | collective-permute-done | bytes 491552 | tf_op jit(solution)/shard_map/ppermute | solution.py:69
  61.4 10.7 %qkv_project.1 = (bf16[1024,2304]{1,0:T(8,128)(2,1)}, bf16[1024,768]{1,0:T(8,128)(2,1)}, bf16[2304,768]{1,0:T(8,128)(2,1)}, f32[8,768]{1,0:T(8,128)}) custom-call(s32[1]{0:T(128)} %bitcast.me_ref, bf16[1024,768]{1,0:T(8,128)(2,1)} %x_ref.5, bf16[16,80,768]{2,1,0:T(8,128)(2,1)} %copy-done.1, bf16[16,80,768]{2,1,0:T(8,128)(2,1)} %collective-permute-done.6.sib_ref, ...), custom_call_target="tpu_custom_call" | custom-call | tf_op jit(solution)/shard_map/qkv_project/pallas_call | solution.py:138
  72.1 31.3 %attend_forward.1 = (bf16[1024,768]{1,0:T(8,128)(2,1)}, bf16[768,1024]{1,0:T(8,128)(2,1)}, f32[6,8,1024]{2,1,0:T(8,128)}) custom-call(s32[1]{0:T(128)S(6)} %copy.31.len_ref, bf16[1024,2304]{1,0:T(8,128)(2,1)} %get-tuple-element.33.q_ref.k_ref.v_ref, bf16[1024,2304]{1,0:T(8,128)(2,1)} %get-tuple-element.33.q_ref.k_ref.v_ref, ...), custom_call_target="tpu_custom_call" | custom-call | tf_op jit(solution)/shard_map/attend_forward/pallas_call | solution.py:226
  103.5 4.7 %all-gather.2.cloned.1.call-done = bf16[6912,768]{1,0:T(8,128)(2,1)} async-done(((bf16[216,768]{1,0:T(8,128)(2,1)}), bf16[6912,768]{1,0:T(8,128)(2,1)}) %all-gather.2.cloned.1.call-update) | async-done | bytes 10616848 | tf_op jit(solution)/shard_map/all_gather | solution.py:580
  108.1 2.4 slice.70
  110.5 8.2 %slice.71 = bf16[32,192,768]{2,1,0:T(8,128)(2,1)} slice(bf16[32,216,768]{2,1,0:T(8,128)(2,1)} %bitcast.36), slice={[0:32], [0:192], [0:768]} | slice | bytes 18874368 | tf_op jit(solution)/shard_map/slice | solution.py:582
  118.7 5.8 %project_out.1 = (f32[1024,768]{1,0:T(8,128)}, bf16[1024,768]{1,0:T(8,128)(2,1)}) custom-call(bf16[1024,768]{1,0:T(8,128)(2,1)} %get-tuple-element.34.att_ref, bf16[1024,768]{1,0:T(8,128)(2,1)} %x_ref.5, bf16[768,768]{1,0:T(8,128)(2,1)} %bitcast.37, f32[8,768]{1,0:T(8,128)} %get-tuple-element.35.vec_ref), custom_call_target="tpu_custom_call" | custom-call | tf_op jit(solution)/shard_map/project_out/pallas_call | solution.py:333
  124.5 42.1 %feed_forward.1 = (bf16[1024,768]{1,0:T(8,128)(2,1)}, f32[1024,768]{1,0:T(8,128)}, bf16[32,2,96,768]{3,2,1,0:T(8,128)(2,1)}) custom-call(s32[1]{0:T(128)S(6)} %copy.31.len_ref, bf16[1024,768]{1,0:T(8,128)(2,1)} %get-tuple-element.36.n2_ref, f32[1024,768]{1,0:T(8,128)} %get-tuple-element.37.res_ref, f32[1024,768]{1,0:T(8,128)} %cot_ref.3, ...), custom_call_target="tpu_custom_call" | custom-call | tf_op jit(solution)/shard_map/feed_forward/pallas_call | solution.py:400
  166.6 10.8 %middle_back.1 = (f32[1024,768]{1,0:T(8,128)}, bf16[1024,768]{1,0:T(8,128)(2,1)}, bf16[768,768]{1,0:T(8,128)(2,1)}, f32[8,768]{1,0:T(8,128)}) custom-call(s32[1]{0:T(128)S(6)} %copy.31.len_ref, f32[1024,768]{1,0:T(8,128)} %get-tuple-element.39.gn_ref, f32[1024,768]{1,0:T(8,128)} %get-tuple-element.37.res_ref, f32[1024,768]{1,0:T(8,128)} %cot_ref.3, ...), custom_call_target="tpu_custom_call" | custom-call | tf_op jit(solution)/shard_map/middle_back/pallas_call | solution.py:460
  177.4 38.4 %attend_backward.1 = (bf16[1024,768]{1,0:T(8,128)(2,1)}, bf16[1024,768]{1,0:T(8,128)(2,1)}, bf16[1024,768]{1,0:T(8,128)(2,1)}) custom-call(bf16[1024,2304]{1,0:T(8,128)(2,1)} %get-tuple-element.33.q_ref.k_ref.v_ref, bf16[1024,2304]{1,0:T(8,128)(2,1)} %get-tuple-element.33.q_ref.k_ref.v_ref, bf16[1024,2304]{1,0:T(8,128)(2,1)} %get-tuple-element.33.q_ref.k_ref.v_ref, ...), custom_call_target="tpu_custom_call" | custom-call | tf_op jit(solution)/shard_map/attend_backward/pallas_call | solution.py:306
  215.8 9.7 %qkv_grad.1 = (bf16[16,96,768]{2,1,0:T(8,128)(2,1)}, bf16[16,96,768]{2,1,0:T(8,128)(2,1)}) custom-call(s32[1]{0:T(128)} %bitcast.me_ref, bf16[1024,768]{1,0:T(8,128)(2,1)} %get-tuple-element.43.dq_ref, bf16[1024,768]{1,0:T(8,128)(2,1)} %get-tuple-element.44.dk_ref, bf16[1024,768]{1,0:T(8,128)(2,1)} %get-tuple-element.45.dv_ref, ...), custom_call_target="tpu_custom_call" | custom-call | tf_op jit(solution)/shard_map/qkv_grad/pallas_call | solution.py:507
  225.8 10.5 %first_back.1 = (f32[1024,768]{1,0:T(8,128)}, f32[8,768]{1,0:T(8,128)}) custom-call(bf16[1024,768]{1,0:T(8,128)(2,1)} %get-tuple-element.43.dq_ref, bf16[1024,768]{1,0:T(8,128)(2,1)} %get-tuple-element.44.dk_ref, bf16[1024,768]{1,0:T(8,128)(2,1)} %get-tuple-element.45.dv_ref, bf16[2304,768]{1,0:T(8,128)(2,1)} %get-tuple-element.46.w_ref, ...), custom_call_target="tpu_custom_call" | custom-call | tf_op jit(solution)/shard_map/first_back/pallas_call | solution.py:556
  243.5 2.4 add_convert_fusion
  253.2 2.2 collective-permute-start.13
  255.6 3.0 collective-permute-done.13
  258.6 6.7 %collective-permute-done.15 = bf16[4,96,768]{2,1,0:T(8,128)(2,1)S(1)} collective-permute-done((bf16[4,96,768]{2,1,0:T(8,128)(2,1)S(1)}, bf16[4,96,768]{2,1,0:T(8,128)(2,1)S(1)}, u32[]{:S(2)}, u32[]{:S(2)}) %collective-permute-start.15) | collective-permute-done | bytes 589856 | tf_op jit(solution)/shard_map/ppermute | solution.py:69
  265.9 17.3 %collective-permute-done.17 = bf16[4,96,768]{2,1,0:T(8,128)(2,1)S(1)} collective-permute-done((bf16[4,96,768]{2,1,0:T(8,128)(2,1)S(1)}, bf16[4,96,768]{2,1,0:T(8,128)(2,1)S(1)}, u32[]{:S(2)}, u32[]{:S(2)}) %collective-permute-start.17) | collective-permute-done | bytes 589856 | tf_op jit(solution)/shard_map/ppermute | solution.py:69
  288.5 7.8 %collective-permute-done.18 = bf16[1,96,768]{2,1,0:T(8,128)(2,1)S(1)} collective-permute-done((bf16[1,96,768]{2,1,0:T(8,128)(2,1)S(1)}, bf16[1,96,768]{2,1,0:T(8,128)(2,1)S(1)}, u32[]{:S(2)}, u32[]{:S(2)}) %collective-permute-start.18) | collective-permute-done | bytes 147488 | tf_op jit(solution)/shard_map/ppermute | solution.py:69
  296.4 7.8 %collective-permute-done.19 = bf16[1,96,768]{2,1,0:T(8,128)(2,1)S(1)} collective-permute-done((bf16[1,96,768]{2,1,0:T(8,128)(2,1)S(1)}, bf16[1,96,768]{2,1,0:T(8,128)(2,1)S(1)}, u32[]{:S(2)}, u32[]{:S(2)}) %collective-permute-start.19) | collective-permute-done | bytes 147488 | tf_op jit(solution)/shard_map/ppermute | solution.py:69
  305.6 17.1 %reduce-scatter.2.cloned.1.call-done = bf16[192,768]{1,0:T(8,128)(2,1)} async-done(((bf16[6144,768]{1,0:T(8,128)(2,1)}), bf16[192,768]{1,0:T(8,128)(2,1)}) %reduce-scatter.2.cloned.1.call-update) | async-done | bytes 294928 | tf_op jit(solution)/shard_map/reduce_scatter | solution.py:606
  (88 shorter events, 40.3 us)
Async XLA Ops:
  7.2 22.2 %copy-start.2 = (bf16[768,72]{0,1:T(8,128)(2,1)S(1)}, bf16[768,72]{0,1:T(8,128)(2,1)}, u32[]{:S(2)}) copy-start(bf16[768,72]{0,1:T(8,128)(2,1)} %param.16) | copy-start | bytes 331780
  7.2 101.0 %all-gather.2.cloned.1.call-start = ((), (), s32[]{:S(2)}) async-start(), calls=%async_computation.1 | async-start | bytes 10948608 | tf_op jit(solution)/shard_map/all_gather | solution.py:580
  9.0 313.6 %reduce-scatter.2.cloned.1.call-start = ((), (), s32[]{:S(2)}) async-start(), calls=%async_computation.2 | async-start | bytes 9732096 | tf_op jit(solution)/shard_map/reduce_scatter | solution.py:606
  10.8 7.7 %collective-permute-start = (bf16[1,80,768]{2,1,0:T(8,128)(2,1)S(1)}, bf16[1,80,768]{2,1,0:T(8,128)(2,1)S(1)}, u32[]{:S(2)}, u32[]{:S(2)}) collective-permute-start(bf16[1,80,768]{2,1,0:T(8,128)(2,1)S(1)} %fusion.3), channel_id=1, source_target_pairs={{0,8},{1,9},{2,10},{3,11},{4,12},{5,13},{6,14},{7,15},{8,0},{9,1},... | collective-permute-start | bytes 368648 | tf_op jit(solution)/shard_map/ppermute | solution.py:69
  13.9 12.3 %collective-permute-start.1 = (bf16[1,80,768]{2,1,0:T(8,128)(2,1)S(1)}, bf16[1,80,768]{2,1,0:T(8,128)(2,1)S(1)}, u32[]{:S(2)}, u32[]{:S(2)}) collective-permute-start(bf16[1,80,768]{2,1,0:T(8,128)(2,1)S(1)} %fusion.3), channel_id=1, source_target_pairs={{0,16},{1,17},{2,18},{3,19},{4,20},{5,21},{6,22},{7,23},{8,24},{9,... | collective-permute-start | bytes 368648 | tf_op jit(solution)/shard_map/ppermute | solution.py:69
  16.5 9.7 %collective-permute-start.2 = (bf16[1,80,768]{2,1,0:T(8,128)(2,1)S(1)}, bf16[1,80,768]{2,1,0:T(8,128)(2,1)S(1)}, u32[]{:S(2)}, u32[]{:S(2)}) collective-permute-start(bf16[1,80,768]{2,1,0:T(8,128)(2,1)S(1)} %fusion.3), channel_id=1, source_target_pairs={{0,24},{1,25},{2,26},{3,27},{4,28},{5,29},{6,30},{7,31},{8,16},{9,... | collective-permute-start | bytes 368648 | tf_op jit(solution)/shard_map/ppermute | solution.py:69
  26.3 14.0 %collective-permute-start.3 = (bf16[4,80,768]{2,1,0:T(8,128)(2,1)S(1)}, bf16[4,80,768]{2,1,0:T(8,128)(2,1)S(1)}, u32[]{:S(2)}, u32[]{:S(2)}) collective-permute-start(bf16[4,80,768]{2,1,0:T(8,128)(2,1)S(1)} %pad_maximum_fusion), channel_id=1, source_target_pairs={{0,2},{1,3},{2,0},{3,1},{4,6},{5,7},{6,4},{7,5},{8,10},{9,11},{10,... | collective-permute-start | bytes 1474568 | tf_op jit(solution)/shard_map/ppermute | solution.py:69
  27.9 14.2 %collective-permute-start.4 = (bf16[4,80,768]{2,1,0:T(8,128)(2,1)S(1)}, bf16[4,80,768]{2,1,0:T(8,128)(2,1)S(1)}, u32[]{:S(2)}, u32[]{:S(2)}) collective-permute-start(bf16[4,80,768]{2,1,0:T(8,128)(2,1)S(1)} %pad_maximum_fusion), channel_id=1, source_target_pairs={{0,4},{1,5},{2,6},{3,7},{4,0},{5,1},{6,2},{7,3},{8,12},{9,13},{10,... | collective-permute-start | bytes 1474568 | tf_op jit(solution)/shard_map/ppermute | solution.py:69
  29.4 27.8 %collective-permute-start.5 = (bf16[4,80,768]{2,1,0:T(8,128)(2,1)S(1)}, bf16[4,80,768]{2,1,0:T(8,128)(2,1)S(1)}, u32[]{:S(2)}, u32[]{:S(2)}) collective-permute-start(bf16[4,80,768]{2,1,0:T(8,128)(2,1)S(1)} %pad_maximum_fusion), channel_id=1, source_target_pairs={{0,6},{1,7},{2,4},{3,5},{4,2},{5,3},{6,0},{7,1},{8,14},{9,15},{10,... | collective-permute-start | bytes 1474568 | tf_op jit(solution)/shard_map/ppermute | solution.py:69
  57.2 4.2 %collective-permute-start.6 = (bf16[16,80,768]{2,1,0:T(8,128)(2,1)S(1)}, bf16[16,80,768]{2,1,0:T(8,128)(2,1)}, u32[]{:S(2)}, u32[]{:S(2)}) collective-permute-start(bf16[16,80,768]{2,1,0:T(8,128)(2,1)S(1)} %constant_dynamic-update-slice_fusion.own_ref), channel_id=1, source_target_pairs={{0,1},{1,0},{2,3},{3,2},{4,5},{5,4},{6,7},{7,6},{8,9},{9,8},{10,11... | collective-permute-start | bytes 5898248 | tf_op jit(solution)/shard_map/ppermute | solution.py:69
  225.5 18.0 %collective-permute-start.14 = (bf16[16,96,768]{2,1,0:T(8,128)(2,1)}, bf16[16,96,768]{2,1,0:T(8,128)(2,1)}, u32[]{:S(2)}, u32[]{:S(2)}) collective-permute-start(bf16[16,96,768]{2,1,0:T(8,128)(2,1)} %get-tuple-element.54), channel_id=1, source_target_pairs={{0,1},{1,0},{2,3},{3,2},{4,5},{5,4},{6,7},{7,6},{8,9},{9,8},{10,11... | collective-permute-start | bytes 7077896 | tf_op jit(solution)/shard_map/ppermute | solution.py:69
  238.6 1.3 collective-permute-start.7
  239.9 8.3 %collective-permute-start.10 = (f32[4,4,24]{2,1,0:T(4,128)S(1)}, f32[4,4,24]{2,1,0:T(4,128)S(1)}, u32[]{:S(2)}, u32[]{:S(2)}) collective-permute-start(f32[4,4,24]{2,1,0:T(4,128)S(1)} %get-tuple-element.63), channel_id=1, source_target_pairs={{0,6},{1,7},{2,4},{3,5},{4,2},{5,3},{6,0},{7,1},{8,14},{9,15},{10,... | collective-permute-start | bytes 4616 | tf_op jit(solution)/shard_map/ppermute | solution.py:69
  241.5 8.0 %collective-permute-start.8 = (f32[4,4,24]{2,1,0:T(4,128)S(1)}, f32[4,4,24]{2,1,0:T(4,128)S(1)}, u32[]{:S(2)}, u32[]{:S(2)}) collective-permute-start(f32[4,4,24]{2,1,0:T(4,128)S(1)} %get-tuple-element.62), channel_id=1, source_target_pairs={{0,2},{1,3},{2,0},{3,1},{4,6},{5,7},{6,4},{7,5},{8,10},{9,11},{10,... | collective-permute-start | bytes 4616 | tf_op jit(solution)/shard_map/ppermute | solution.py:69
  242.8 6.7 %collective-permute-start.9 = (f32[4,4,24]{2,1,0:T(4,128)S(1)}, f32[4,4,24]{2,1,0:T(4,128)S(1)}, u32[]{:S(2)}, u32[]{:S(2)}) collective-permute-start(f32[4,4,24]{2,1,0:T(4,128)S(1)} %get-tuple-element.64), channel_id=1, source_target_pairs={{0,4},{1,5},{2,6},{3,7},{4,0},{5,1},{6,2},{7,3},{8,12},{9,13},{10,... | collective-permute-start | bytes 4616 | tf_op jit(solution)/shard_map/ppermute | solution.py:69
  246.0 19.3 %collective-permute-start.15 = (bf16[4,96,768]{2,1,0:T(8,128)(2,1)S(1)}, bf16[4,96,768]{2,1,0:T(8,128)(2,1)S(1)}, u32[]{:S(2)}, u32[]{:S(2)}) collective-permute-start(bf16[4,96,768]{2,1,0:T(8,128)(2,1)S(1)} %get-tuple-element.56), channel_id=1, source_target_pairs={{0,2},{1,3},{2,0},{3,1},{4,6},{5,7},{6,4},{7,5},{8,10},{9,11},{10,... | collective-permute-start | bytes 1769480 | tf_op jit(solution)/shard_map/ppermute | solution.py:69
  247.5 18.4 %collective-permute-start.16 = (bf16[4,96,768]{2,1,0:T(8,128)(2,1)S(1)}, bf16[4,96,768]{2,1,0:T(8,128)(2,1)S(1)}, u32[]{:S(2)}, u32[]{:S(2)}) collective-permute-start(bf16[4,96,768]{2,1,0:T(8,128)(2,1)S(1)} %get-tuple-element.58), channel_id=1, source_target_pairs={{0,4},{1,5},{2,6},{3,7},{4,0},{5,1},{6,2},{7,3},{8,12},{9,13},{10,... | collective-permute-start | bytes 1769480 | tf_op jit(solution)/shard_map/ppermute | solution.py:69
  248.2 35.0 %collective-permute-start.17 = (bf16[4,96,768]{2,1,0:T(8,128)(2,1)S(1)}, bf16[4,96,768]{2,1,0:T(8,128)(2,1)S(1)}, u32[]{:S(2)}, u32[]{:S(2)}) collective-permute-start(bf16[4,96,768]{2,1,0:T(8,128)(2,1)S(1)} %get-tuple-element.57), channel_id=1, source_target_pairs={{0,6},{1,7},{2,4},{3,5},{4,2},{5,3},{6,0},{7,1},{8,14},{9,15},{10,... | collective-permute-start | bytes 1769480 | tf_op jit(solution)/shard_map/ppermute | solution.py:69
  249.5 3.7 %collective-permute-start.11 = (f32[1,4,24]{2,1,0:T(4,128)S(1)}, f32[1,4,24]{2,1,0:T(4,128)S(1)}, u32[]{:S(2)}, u32[]{:S(2)}) collective-permute-start(f32[1,4,24]{2,1,0:T(4,128)S(1)} %get-tuple-element.65), channel_id=1, source_target_pairs={{0,8},{1,9},{2,10},{3,11},{4,12},{5,13},{6,14},{7,15},{8,0},{9,1},... | collective-permute-start | bytes 1160 | tf_op jit(solution)/shard_map/ppermute | solution.py:69
  251.1 4.5 %collective-permute-start.12 = (f32[1,4,24]{2,1,0:T(4,128)S(1)}, f32[1,4,24]{2,1,0:T(4,128)S(1)}, u32[]{:S(2)}, u32[]{:S(2)}) collective-permute-start(f32[1,4,24]{2,1,0:T(4,128)S(1)} %get-tuple-element.67), channel_id=1, source_target_pairs={{0,16},{1,17},{2,18},{3,19},{4,20},{5,21},{6,22},{7,23},{8,24},{9,... | collective-permute-start | bytes 1160 | tf_op jit(solution)/shard_map/ppermute | solution.py:69
  253.2 5.4 %collective-permute-start.13 = (f32[1,4,24]{2,1,0:T(4,128)S(1)}, f32[1,4,24]{2,1,0:T(4,128)S(1)}, u32[]{:S(2)}, u32[]{:S(2)}) collective-permute-start(f32[1,4,24]{2,1,0:T(4,128)S(1)} %get-tuple-element.66), channel_id=1, source_target_pairs={{0,24},{1,25},{2,26},{3,27},{4,28},{5,29},{6,30},{7,31},{8,16},{9,... | collective-permute-start | bytes 1160 | tf_op jit(solution)/shard_map/ppermute | solution.py:69
  283.5 12.8 %collective-permute-start.18 = (bf16[1,96,768]{2,1,0:T(8,128)(2,1)S(1)}, bf16[1,96,768]{2,1,0:T(8,128)(2,1)S(1)}, u32[]{:S(2)}, u32[]{:S(2)}) collective-permute-start(bf16[1,96,768]{2,1,0:T(8,128)(2,1)S(1)} %get-tuple-element.59), channel_id=1, source_target_pairs={{0,8},{1,9},{2,10},{3,11},{4,12},{5,13},{6,14},{7,15},{8,0},{9,1},... | collective-permute-start | bytes 442376 | tf_op jit(solution)/shard_map/ppermute | solution.py:69
  284.2 19.9 %collective-permute-start.19 = (bf16[1,96,768]{2,1,0:T(8,128)(2,1)S(1)}, bf16[1,96,768]{2,1,0:T(8,128)(2,1)S(1)}, u32[]{:S(2)}, u32[]{:S(2)}) collective-permute-start(bf16[1,96,768]{2,1,0:T(8,128)(2,1)S(1)} %get-tuple-element.61), channel_id=1, source_target_pairs={{0,16},{1,17},{2,18},{3,19},{4,20},{5,21},{6,22},{7,23},{8,24},{9,... | collective-permute-start | bytes 442376 | tf_op jit(solution)/shard_map/ppermute | solution.py:69
  286.0 18.1 %collective-permute-start.20 = (bf16[1,96,768]{2,1,0:T(8,128)(2,1)S(1)}, bf16[1,96,768]{2,1,0:T(8,128)(2,1)S(1)}, u32[]{:S(2)}, u32[]{:S(2)}) collective-permute-start(bf16[1,96,768]{2,1,0:T(8,128)(2,1)S(1)} %get-tuple-element.60), channel_id=1, source_target_pairs={{0,24},{1,25},{2,26},{3,27},{4,28},{5,29},{6,30},{7,31},{8,16},{9,... | collective-permute-start | bytes 442376 | tf_op jit(solution)/shard_map/ppermute | solution.py:69
  (3 other events, 41.2 us)
Sparse Core Ops, SparseCore 0:
  10.9 97.1 all-gather.1
  166.7 155.8 reduce-scatter.1

commit v2 on v1

--- a/solution.py
+++ b/solution.py
@@ -45,12 +45,17 @@
     return pltpu.CompilerParams(vmem_limit_bytes=VMEM_LIMIT, **kw)
 
 
+def cost(flops, moved):
+    return pl.CostEstimate(flops=int(flops), bytes_accessed=int(moved), transcendentals=0)
+
+
 class Plan:
     def __init__(self, mesh):
         self.n = mesh.shape["dp"] * mesh.shape["fsdp"]
         self.bits = self.n.bit_length() - 1
-        self.direct = self.n == 1 << self.bits and 4 <= self.bits <= 5
-        self.stages = [tuple(range(3, self.bits)), (1, 2)]
+        self.direct = self.n == 1 << self.bits and self.bits == 5 and mesh.shape["fsdp"] == 4
+        self.along = (3, 4)
+        self.across = (1, 2)
 
     @staticmethod
     def masks_of(bits):
@@ -60,28 +65,61 @@
         return found
 
     def slot_masks(self):
-        masks = [0]
-        for stage in self.stages:
-            masks = [m ^ k for m in self.masks_of(stage) for k in masks]
-        return masks
+        return [m ^ k for m in self.masks_of(self.across) for k in self.masks_of(self.along)]
 
     def swap(self, value, mask):
         return lax.ppermute(value, AXES, [(i, i ^ mask) for i in range(self.n)])
 
+    def spread_stage(self, held, bits):
+        return jnp.concatenate([held] + [self.swap(held, m) for m in self.masks_of(bits)[1:]], axis=0)
+
     def gather(self, piece):
-        held = piece[None]
-        for stage in self.stages:
-            masks = self.masks_of(stage)
-            held = jnp.concatenate([held] + [self.swap(held, m) for m in masks[1:]], axis=0)
+        held = self.spread_stage(self.spread_stage(piece[None], self.along), self.across)
         return held, self.swap(held, 1)
 
-    def scatter(self, keep, send):
-        held = add_low(keep, [self.swap(send, 1)])
-        for stage in reversed(self.stages):
-            masks = self.masks_of(stage)
-            parts = jnp.split(held, len(masks), axis=0)
-            held = add_low(parts[0], [self.swap(p, m) for p, m in zip(parts[1:], masks[1:])])
-        return held[0]
+    def scatter_first(self, keep, send, cut):
+        got = self.swap(send, 1)
+        outer, inner = len(self.masks_of(self.across)), len(self.masks_of(self.along))
+        grid = (outer, inner) + keep.shape[1:]
+        keep, got = keep.reshape(grid), got.reshape(grid)
+        pair = lambda at: add_low(keep[at], [got[at]])
+        head, tail = slice(None, cut), slice(cut, None)
+        first = [pair((slice(None), z, head)) for z in range(inner)]
+        second = [pair((x, slice(None), tail)) for x in range(outer)]
+        return first, second
+
+    def scatter_rest(self, first, second):
+        outer, inner = self.masks_of(self.across), self.masks_of(self.along)
+        second = add_low(second[0], [self.swap(v, m) for v, m in zip(second[1:], outer[1:])])
+        first = add_low(first[0], [self.swap(v, m) for v, m in zip(first[1:], inner[1:])])
+        second = add_low(second[0], [self.swap(second[z], m) for z, m in list(enumerate(inner))[1:]])
+        first = add_low(first[0], [self.swap(first[x], m) for x, m in list(enumerate(outer))[1:]])
+        return jnp.concatenate([first, second], axis=0)
+
+    def view(self, held):
+        pieces, rows, width = held.shape
+        return held.reshape(pieces // 4, 2, 2, 2, rows // 2, width)
+
+    def first_away(self, keep, got):
+        k, g = self.view(keep), self.view(got)
+        return add_low(k[:, :, 1, 0], [g[:, :, 1, 0]]), add_low(k[:, 1, :, 1], [g[:, 1, :, 1]])
+
+    def second_away(self, keep, got, back):
+        k, g = self.view(keep), self.view(got)
+        return (
+            add_low(k[:, 1, 0, 0], [g[:, 1, 0, 0], back[0][:, 1]]),
+            add_low(k[:, 0, 1, 1], [g[:, 0, 1, 1], back[1][:, 1]]),
+        )
+
+    def last_sum(self, keep, got, back, again):
+        k, g = self.view(keep), self.view(got)
+        both = [
+            add_low(k[:, 0, 0, half], [g[:, 0, 0, half], back[half][:, 0], again[half]]) for half in range(2)
+        ]
+        whole = jnp.concatenate(both, axis=1)
+        line = [[r + 8 * z for z in range(self.n // 8)] for r in range(8)]
+        whole = whole.reshape(-1, whole.shape[-1])
+        return lax.psum_scatter(whole, AXES, scatter_dimension=0, tiled=True, axis_index_groups=line)
 
 
 def add_low(first, others):
@@ -108,21 +146,16 @@
         for s, m in enumerate(masks):
             pair = lax.div(me, 2) ^ (m // 2)
             at = pl.ds(pl.multiple_of(pair * (2 * ppr), 16), 2 * ppr)
-
-            @pl.when(core == 0)
-            def _():
-                w_ref[at, :] = jnp.concatenate([own_ref[s, :ppr, :], sib_ref[s, :ppr, :]], axis=0)
-
-            @pl.when(core == 1)
-            def _():
-                w_ref[at, :] = jnp.concatenate([sib_ref[s, :ppr, :], own_ref[s, :ppr, :]], axis=0)
-
-        packed = jnp.concatenate(
-            [own_ref[:, ppr, :128].astype(F32), sib_ref[:, ppr, :128].astype(F32)], axis=0
-        )
+            both = [own_ref[s, :ppr, :], sib_ref[s, :ppr, :]]
+            for side in range(2):
+
+                @pl.when(core == side)
+                def _():
+                    w_ref[at, :] = jnp.concatenate([both[side], both[1 - side]], axis=0)
+
+        packed = jnp.concatenate([own_ref[:, ppr, :128], sib_ref[:, ppr, :128]], axis=0)
         for v in range(4):
-            spread = jnp.dot(packed, e_ref[v], preferred_element_type=F32, precision=lax.Precision.HIGHEST)
-            vec_ref[v : v + 1, :] = jnp.sum(spread * m_ref[...], axis=0, keepdims=True)
+            vec_ref[v : v + 1, :] = jnp.sum(mm_nn(packed, e_ref[v]) * m_ref[...], axis=0, keepdims=True)
 
     xhat, rinv = norm_stats(x_ref[...].astype(F32))
     n1 = (xhat * vec_ref[0:1, :] + vec_ref[1:2, :]).astype(BF16)
@@ -130,7 +163,7 @@
     mixed_ref[...] = mm_nt(n1, w_ref[...]).astype(BF16)
 
 
-def qkv_project(plan, me, tokens, own, sib, spread, place, out_cols, rows_block=256):
+def qkv_project(plan, me, tokens, gathered, spread, place, out_cols, rows_block=256):
     rows, width = tokens.shape
     masks = plan.slot_masks()
     full = lambda a: pl.BlockSpec(a.shape, lambda r, *_: (0,) * a.ndim)
@@ -142,8 +175,8 @@
             grid=(rows // rows_block,),
             in_specs=[
                 pl.BlockSpec((rows_block, width), lambda r, *_: (r, 0)),
-                full(own), full(sib), full(spread), full(place),
-            ],
+            ]
+            + [full(a) for a in (*gathered, spread, place)],
             out_specs=[
                 pl.BlockSpec((rows_block, out_cols), lambda r, *_: (r, 0)),
                 pl.BlockSpec((rows_block, width), lambda r, *_: (r, 0)),
@@ -157,8 +190,9 @@
             jax.ShapeDtypeStruct((8, width), F32),
         ],
         compiler_params=params(),
+        cost_estimate=cost(2 * rows * width * out_cols, 20e6),
         name="qkv_project",
-    )(me, tokens, own, sib, spread, place)
+    )(me, tokens, *gathered, spread, place)
 
 
 def qkv_plain_kernel(x_ref, w_ref, vec_ref, mixed_ref, n1_ref):
@@ -241,11 +275,12 @@
             jax.ShapeDtypeStruct((seqs * pairs, 8, maxlen), F32),
         ],
         compiler_params=params(),
+        cost_estimate=cost(20e9, 10e6),
         name="attend_forward",
     )(lengths, mixed, mixed, mixed)
 
 
-def attend_back_kernel(maxlen, q_ref, k_ref, v_ref, ga_ref, attT_ref, lse_ref, dq_ref, dk_ref, dv_ref, dqT):
+def attend_back_kernel(maxlen, q_ref, k_ref, v_ref, ga_ref, attT_ref, lse_ref, d_ref, sum_ref, dqT):
     qs = q_ref[...] * jnp.asarray(HEAD**-0.5, BF16)
     k, v, ga = k_ref[...], v_ref[...], ga_ref[...]
     qT = qs.astype(F32).T.astype(BF16)
@@ -294,51 +329,78 @@
                 dqT[h * HEAD : (h + 1) * HEAD, :] = dq_h
             else:
                 dqT[h * HEAD : (h + 1) * HEAD, lo:] += dq_h
-        dv_ref[lo:hi, :] = dv.astype(BF16)
-        dk_ref[lo:hi, :] = dk.astype(BF16)
-    dq_ref[...] = (dqT[...] * HEAD**-0.5).T.astype(BF16)
-
-
-def attend_backward(mixed, ga, attT, lse, seqs):
+        d_ref[2, lo:hi, :] = dv.astype(BF16)
+        d_ref[1, lo:hi, :] = dk.astype(BF16)
+        sums = [jnp.sum(d, axis=0, keepdims=True) for d in (dk, dv)]
+        total = sums if j == 0 else [t + d for t, d in zip(total, sums)]
+    dq = (dqT[...] * HEAD**-0.5).T
+    d_ref[0] = dq.astype(BF16)
+    total = [jnp.sum(dq, axis=0, keepdims=True)] + total
+    sum_ref[0] = jnp.concatenate(total + [jnp.zeros((5, PAIR), F32)], axis=0)
+
+
+def attend_backward(mixed, ga, attT, lse, seqs, first, count):
     rows, width = mixed.shape[0], mixed.shape[1] // 3
     maxlen, pairs = rows // seqs, width // PAIR
-    col = lambda part: pl.BlockSpec((maxlen, PAIR), lambda s, p: (s, part * pairs + p))
+    col = lambda part: pl.BlockSpec((maxlen, PAIR), lambda s, p: (s, part * pairs + p + first))
     return pl.pallas_call(
         functools.partial(attend_back_kernel, maxlen),
-        grid=(seqs, pairs),
+        grid=(seqs, count),
         in_specs=[
             col(0), col(1), col(2), col(0),
-            pl.BlockSpec((PAIR, maxlen), lambda s, p: (p, s)),
-            pl.BlockSpec((1, 8, maxlen), lambda s, p: (s * pairs + p, 0, 0)),
-        ],
-        out_specs=[col(0)] * 3,
-        out_shape=[jax.ShapeDtypeStruct((rows, width), BF16)] * 3,
+            pl.BlockSpec((PAIR, maxlen), lambda s, p: (p + first, s)),
+            pl.BlockSpec((1, 8, maxlen), lambda s, p: (s * pairs + p + first, 0, 0)),
+        ],
+        out_specs=[
+            pl.BlockSpec((3, maxlen, PAIR), lambda s, p: (0, s, p)),
+            pl.BlockSpec((1, 8, PAIR), lambda s, p: (s, 0, p)),
+        ],
+        out_shape=[
+            jax.ShapeDtypeStruct((3, rows, count * PAIR), BF16),
+            jax.ShapeDtypeStruct((seqs, 8, count * PAIR), F32),
+        ],
         scratch_shapes=[pltpu.VMEM((PAIR, maxlen), F32)],
         compiler_params=params(),
+        cost_estimate=cost(5e9 * count, 2e6 * count),
         name="attend_backward",
     )(mixed, mixed, mixed, ga, attT, lse)
 
 
-def project_kernel(att_ref, x_ref, wo_ref, vec_ref, res_ref, n2_ref):
+def project_kernel(att_ref, x_ref, wp_ref, vec_ref, res_ref, n2_ref, wo_ref):
+    pieces, per, _ = wp_ref.shape
+
+    @pl.when(pl.program_id(0) == 0)
+    def _():
+        for p in range(pieces):
+            wo_ref[p * per : (p + 1) * per, :] = wp_ref[p]
+
     residual = x_ref[...].astype(F32) + mm_nn(att_ref[...], wo_ref[...])
     res_ref[...] = residual
     xhat, rinv = norm_stats(residual)
     n2_ref[...] = (xhat * vec_ref[2:3, :] + vec_ref[3:4, :]).astype(BF16)
 
 
-def project_out(att, tokens, wo, vecs, rows_block=256):
+def project_out(att, tokens, wo_pieces, at, vecs, rows_block=256):
     rows, width = tokens.shape
+    pieces = wo_pieces.shape[0]
     block = pl.BlockSpec((rows_block, width), lambda r: (r, 0))
     full = lambda a: pl.BlockSpec(a.shape, lambda r: (0,) * a.ndim)
     return pl.pallas_call(
         project_kernel,
         grid=(rows // rows_block,),
-        in_specs=[block, block, full(wo), full(vecs)],
-        out_specs=[block, block],
-        out_shape=[jax.ShapeDtypeStruct((rows, width), F32), jax.ShapeDtypeStruct((rows, width), BF16)],
-        compiler_params=params(),
+        in_specs=[
+            block, block, pl.BlockSpec((pieces, width // pieces, width), lambda r: (0, at, 0)), full(vecs),
+        ],
+        out_specs=[block, block, pl.BlockSpec((width, width), lambda r: (0, 0))],
+        out_shape=[
+            jax.ShapeDtypeStruct((rows, width), F32),
+            jax.ShapeDtypeStruct((rows, width), BF16),
+            jax.ShapeDtypeStruct((width, width), BF16),
+        ],
+        compiler_params=params(),
+        cost_estimate=cost(2 * rows * width * width, 10e6),
         name="project_out",
-    )(att, tokens, wo, vecs)
+    )(att, tokens, wo_pieces, vecs)
 
 
 def live_grad(cot, lengths_ref, maxlen, first_row):
@@ -348,9 +410,9 @@
     return jnp.where(at - seq * maxlen < lengths_ref[seq], cot, 0.0)
 
 
-def mlp_kernel(maxlen, len_ref, n2_ref, res_ref, cot_ref, w_ref, out_ref, gn_ref, gw_ref, gl_s, acc_s):
+def mlp_kernel(maxlen, units, len_ref, me_ref, n2_ref, res_ref, cot_ref, w_ref, out_ref, gn_ref, *rest):
+    *gw_refs, gl_s, acc_s = rest
     step = pl.program_id(0)
-    units = w_ref.shape[2]
     rows, width = n2_ref.shape
 
     @pl.when(step == 0)
@@ -360,8 +422,8 @@
             gl_s[at, :] = live_grad(cot_ref[at, :], len_ref, maxlen, first).astype(BF16)
 
     pieces = w_ref.shape[0]
-    wu = w_ref[:, 0].reshape(pieces * units, width)
-    wd = w_ref[:, 1].reshape(pieces * units, width)
+    wu = w_ref[:, :units, :].reshape(pieces * units, width)
+    wd = w_ref[:, units : 2 * units, :].reshape(pieces * units, width)
     n2, gl = n2_ref[...], gl_s[...]
     u = mm_nt(n2, wu)
     uu = u * u
@@ -383,37 +445,50 @@
         acc_s[...] += out
         gn_ref[...] += gn
 
-    gw_ref[:, 0] = mm_tn(gp, n2).astype(BF16).reshape(pieces, units, width)
-    gw_ref[:, 1] = mm_tn(act, gl).astype(BF16).reshape(pieces, units, width)
+    for at, grad in ((0, mm_tn(gp, n2)), (units, mm_tn(act, gl))):
+        grad = grad.astype(BF16)
+        if len(gw_refs) == 1:
+            gw_refs[0][:, at : at + units, :] = grad.reshape(pieces, units, width)
+            continue
+        grad = grad.reshape(pieces // 2, 2, units, width)
+        core = lax.rem(me_ref[0], 2)
+        near = lax.rem(lax.div(me_ref[0], 2), 4)
+        for side in range(2):
+
+            @pl.when(core == side)
+            def _():
+                for place in range(pieces // 2):
+                    slot = (place // 4) * 4 + ((place % 4) ^ near)
+                    gw_refs[0][slot, at : at + units, :] = grad[place, side]
+                    gw_refs[1][slot, at : at + units, :] = grad[place, 1 - side]
 
     @pl.when(step == pl.num_programs(0) - 1)
     def _():
         out_ref[...] = acc_s[...].astype(BF16)
 
 
-def feed_forward(lengths, n2, residual, cot, w):
+def feed_forward(lengths, me, n2, residual, cot, w, units, split):
     rows, width = n2.shape
-    pieces, _, units, _ = w.shape
+    pieces, held, _ = w.shape
     take = max(1, 768 // units)
     full = lambda: pl.BlockSpec((rows, width), lambda f, *_: (0, 0))
-    chunk = pl.BlockSpec((take, 2, units, width), lambda f, *_: (f, 0, 0, 0))
-    return pl.pallas_call(
-        functools.partial(mlp_kernel, rows // lengths.shape[0]),
+    outs = 2 if split else 1
+    grads = [pl.BlockSpec((take // outs, 2 * units, width), lambda f, *_: (f, 0, 0))] * outs
+    return pl.pallas_call(
+        functools.partial(mlp_kernel, rows // lengths.shape[0], units),
         grid_spec=pltpu.PrefetchScalarGridSpec(
-            num_scalar_prefetch=1,
+            num_scalar_prefetch=2,
             grid=(pieces // take,),
-            in_specs=[full(), full(), full(), chunk],
-            out_specs=[full(), full(), chunk],
+            in_specs=[full(), full(), full(), pl.BlockSpec((take, held, width), lambda f, *_: (f, 0, 0))],
+            out_specs=[full(), full()] + grads,
             scratch_shapes=[pltpu.VMEM((rows, width), BF16), pltpu.VMEM((rows, width), F32)],
         ),
-        out_shape=[
-            jax.ShapeDtypeStruct((rows, width), BF16),
-            jax.ShapeDtypeStruct((rows, width), F32),
-            jax.ShapeDtypeStruct(w.shape, BF16),
-        ],
-        compiler_params=params(),
+        out_shape=[jax.ShapeDtypeStruct((rows, width), BF16), jax.ShapeDtypeStruct((rows, width), F32)]
+        + [jax.ShapeDtypeStruct((pieces // outs, 2 * units, width), BF16)] * outs,
+        compiler_params=params(),
+        cost_estimate=cost(12 * rows * width * pieces * units, 40e6),
         name="feed_forward",
-    )(lengths, n2, residual, cot, w)
+    )(lengths, me, n2, residual, cot, w)
 
 
 def norm_back(grad, xhat, rinv, gain):
@@ -423,7 +498,7 @@
     return rinv * (dh - first - xhat * second)
 
 
-def middle_kernel(maxlen, len_ref, gn_ref, res_ref, cot_ref, att_ref, wo_ref, vec_ref, gres_ref, ga_ref, gwo_ref, gvec_ref, acc_s):
+def middle_kernel(maxlen, len_ref, gn_ref, res_ref, cot_ref, att_ref, wo_ref, vec_ref, gres_ref, ga_ref, gwo_ref, gvec_ref, low_s):
     step = pl.program_id(0)
     rows = gn_ref.shape[0]
     gn = gn_ref[...]
@@ -431,26 +506,19 @@
     gres = live_grad(cot_ref[...], len_ref, maxlen, step * rows) + norm_back(gn, xhat, rinv, vec_ref[2:3, :])
     gres_ref[...] = gres
     low = gres.astype(BF16)
+    low_s[pl.ds(pl.multiple_of(step * rows, rows), rows), :] = low
     ga_ref[...] = mm_nt(low, wo_ref[...]).astype(BF16)
-    gwo = mm_tn(att_ref[...], low)
-    ggain = jnp.sum(gn * xhat, axis=0, keepdims=True)
-    gshift = jnp.sum(gn, axis=0, keepdims=True)
 
     @pl.when(step == 0)
     def _():
-        acc_s[...] = gwo
         gvec_ref[...] = jnp.zeros_like(gvec_ref)
 
-    @pl.when(step > 0)
-    def _():
-        acc_s[...] += gwo
-
-    gvec_ref[0:1, :] += ggain
-    gvec_ref[1:2, :] += gshift
+    gvec_ref[0:1, :] += jnp.sum(gn * xhat, axis=0, keepdims=True)
+    gvec_ref[1:2, :] += jnp.sum(gn, axis=0, keepdims=True)
 
     @pl.when(step == pl.num_programs(0) - 1)
     def _():
-        gwo_ref[...] = acc_s[...].astype(BF16)
+        gwo_ref[...] = mm_tn(att_ref[...], low_s[...]).astype(BF16)
 
 
 def middle_back(lengths, gn, residual, cot, att, wo, vecs, rows_block=256):
@@ -462,9 +530,9 @@
         grid_spec=pltpu.PrefetchScalarGridSpec(
             num_scalar_prefetch=1,
             grid=(rows // rows_block,),
-            in_specs=[block, block, block, block, full(wo.shape), full(vecs.shape)],
+            in_specs=[block, block, block, full(att.shape), full(wo.shape), full(vecs.shape)],
             out_specs=[block, block, full(wo.shape), full((8, width))],
-            scratch_shapes=[pltpu.VMEM(wo.shape, F32)],
+            scratch_shapes=[pltpu.VMEM((rows, width), BF16)],
         ),
         out_shape=[
             jax.ShapeDtypeStruct((rows, width), F32),
@@ -473,71 +541,124 @@
             jax.ShapeDtypeStruct((8, width), F32),
         ],
         compiler_params=params(),
+        cost_estimate=cost(4 * rows * width * width, 30e6),
         name="middle_back",
     )(lengths, gn, residual, cot, att, wo, vecs)
 
 
-def qkv_grad_kernel(masks, ppr, opr, me_ref, dq_ref, dk_ref, dv_ref, n1_ref, gwo_ref, keep_ref, send_ref, low_s):
-    width = n1_ref.shape[1]
+def qkv_grad_kernel(masks, ppr, opr, me_ref, *refs):
+    d1_ref, d2_ref, sum1_ref, sum2_ref, n1_ref, w_ref, gwo_ref, vec_ref, gvec2_ref, e_ref, keep_ref, send_ref, low_s, acc_s = refs
+    rows, width = n1_ref.shape
+    part = pl.program_id(0)
     n1 = n1_ref[...]
-    for part, ref in enumerate((dq_ref, dk_ref, dv_ref)):
-        low_s[part * width : (part + 1) * width, :] = mm_tn(ref[...], n1).astype(BF16)
+    paired, gshift, at = jnp.zeros((1, width), F32), jnp.zeros((8, width), F32), 0
+    for d_ref, sum_ref in ((d1_ref, sum1_ref), (d2_ref, sum2_ref)):
+        cols = d_ref.shape[2]
+        gw = mm_tn(d_ref[0], n1)
+        low_s[pl.ds(pl.multiple_of(part * width + at, PAIR), cols), :] = gw.astype(BF16)
+        w = w_ref[at : at + cols, :]
+        paired += jnp.sum(gw * w.astype(F32), axis=0, keepdims=True)
+        total = jnp.sum(sum_ref[...], axis=0)
+        pick = lax.broadcasted_iota(jnp.int32, (8, 1), 0) == part
+        total = jnp.sum(jnp.where(pick, total, 0.0), axis=0, keepdims=True)
+        high = total.astype(BF16).astype(F32)
+        low = jnp.concatenate([high, total - high, jnp.zeros((6, cols), F32)], axis=0)
+        gshift += mm_nn(low.astype(BF16), w)
+        at += cols
+
+    @pl.when(part == 0)
+    def _():
+        acc_s[...] = jnp.zeros_like(acc_s)
+
+    acc_s[0:1, :] += paired
+    acc_s[1:2, :] += gshift[0:1, :] + gshift[1:2, :]
+
+    @pl.when(part == 2)
+    def _():
+        qkv_grad_pieces(masks, ppr, opr, me_ref, acc_s, gwo_ref, vec_ref, gvec2_ref, e_ref, keep_ref, send_ref, low_s)
+
+
+def qkv_grad_pieces(masks, ppr, opr, me_ref, acc_s, gwo_ref, vec_ref, gvec2_ref, e_ref, keep_ref, send_ref, low_s):
+    width = acc_s.shape[1]
+    paired, gshift = acc_s[0:1, :], acc_s[1:2, :]
+    ggain = (paired - vec_ref[1:2, :] * gshift) / vec_ref[0:1, :]
+    n = 2 * len(masks)
+    owner = lax.broadcasted_iota(jnp.int32, (n, width), 1) // opr == lax.broadcasted_iota(jnp.int32, (n, width), 0)
+    packed = jnp.zeros((n, 128), F32)
+    for v, row in enumerate((ggain, gshift, gvec2_ref[0:1, :], gvec2_ref[1:2, :])):
+        packed += mm_nt(jnp.where(owner, row, 0.0).astype(BF16), e_ref[v])
     me = me_ref[0]
     core = lax.rem(me, 2)
     for pair in range(len(masks)):
         slot = slot_of(masks, me, pair)
-        w0 = low_s[2 * pair * ppr : (2 * pair + 1) * ppr, :]
-        w1 = low_s[(2 * pair + 1) * ppr : (2 * pair + 2) * ppr, :]
-        o0 = gwo_ref[2 * pair * opr : (2 * pair + 1) * opr, :]
-        o1 = gwo_ref[(2 * pair + 1) * opr : (2 * pair + 2) * opr, :]
-        for side, (own_w, own_o, sib_w, sib_o) in enumerate(((w0, o0, w1, o1), (w1, o1, w0, o0))):
+        sides = []
+        for j in (2 * pair, 2 * pair + 1):
+            extra = jnp.concatenate([packed[j : j + 1, :], jnp.zeros((1, width - 128), F32)], axis=1)
+            extra = jnp.concatenate([extra, jnp.zeros((7, width), F32)], axis=0)
+            sides.append((low_s[j * ppr : (j + 1) * ppr, :], gwo_ref[j * opr : (j + 1) * opr, :], extra.astype(BF16)))
+        for side in range(2):
 
             @pl.when(core == side)
             def _():
-                keep_ref[slot] = jnp.concatenate([own_w, own_o], axis=0)
-                send_ref[slot] = jnp.concatenate([sib_w, sib_o], axis=0)
-
-
-def qkv_grad(plan, me, dq, dk, dv, n1, gwo):
+                for out, part in ((keep_ref, sides[side]), (send_ref, sides[1 - side])):
+                    out[slot] = jnp.concatenate(part, axis=0)
+
+
+def qkv_grad(plan, me, grads, sums, n1, w_abs, gwo, vecs, gvec2, spread):
     rows, width = n1.shape
     masks = plan.slot_masks()
     ppr, opr = 3 * width // plan.n, width // plan.n
-    vm = pl.BlockSpec(memory_space=pltpu.VMEM)
-    shape = jax.ShapeDtypeStruct((len(masks), ppr + opr, width), BF16)
+    full = lambda a: pl.BlockSpec(a.shape, lambda p, *_: (0,) * len(a.shape))
+    shape = jax.ShapeDtypeStruct((len(masks), ppr + opr + 8, width), BF16)
     return pl.pallas_call(
         functools.partial(qkv_grad_kernel, masks, ppr, opr),
-        in_specs=[pl.BlockSpec(memory_space=pltpu.SMEM)] + [vm] * 5,
-        out_specs=[vm, vm],
+        grid_spec=pltpu.PrefetchScalarGridSpec(
+            num_scalar_prefetch=1,
+            grid=(3,),
+            in_specs=[pl.BlockSpec((1, rows, d.shape[2]), lambda p, *_: (p, 0, 0)) for d in grads]
+            + [full(a) for a in (*sums, n1)]
+            + [pl.BlockSpec((width, width), lambda p, *_: (p, 0))]
+            + [full(a) for a in (gwo, vecs, gvec2, spread)],
+            out_specs=[full(shape), full(shape)],
+            scratch_shapes=[pltpu.VMEM((3 * width, width), BF16), pltpu.VMEM((8, width), F32)],
+        ),
         out_shape=[shape, shape],
-        scratch_shapes=[pltpu.VMEM((3 * width, width), BF16)],
-        compiler_params=params(),
+        compiler_params=params(),
+        cost_estimate=cost(6 * rows * width * width, 25e6),
         name="qkv_grad",
-    )(me, dq, dk, dv, n1, gwo)
+    )(me, *grads, *sums, n1, w_abs, gwo, vecs, gvec2, spread)
 
 
 def qkv_grad_plain_kernel(d_ref, n1_ref, out_ref):
     out_ref[...] = mm_tn(d_ref[...], n1_ref[...]).astype(BF16)
 
 
-def qkv_grad_plain(dq, dk, dv, n1):
+def qkv_grad_plain(grads, n1):
     rows, width = n1.shape
     vm = pl.BlockSpec(memory_space=pltpu.VMEM)
-    call = pl.pallas_call(
-        qkv_grad_plain_kernel,
-        in_specs=[vm, vm],
-        out_specs=vm,
-        out_shape=jax.ShapeDtypeStruct((width, width), BF16),
-        compiler_params=params(),
-        name="qkv_grad_plain",
-    )
-    return jnp.concatenate([call(d, n1) for d in (dq, dk, dv)], axis=0)
-
-
-def first_kernel(dq_ref, dk_ref, dv_ref, w_ref, x_ref, gres_ref, vec_ref, gtok_ref, gvec_ref):
+    found = []
+    for part in range(3):
+        for d in grads:
+            call = pl.pallas_call(
+                qkv_grad_plain_kernel,
+                in_specs=[vm, vm],
+                out_specs=vm,
+                out_shape=jax.ShapeDtypeStruct((d.shape[2], width), BF16),
+                compiler_params=params(),
+                name="qkv_grad_plain",
+            )
+            found.append(call(d[part], n1))
+    return jnp.concatenate(found, axis=0)
+
+
+def first_kernel(d1_ref, d2_ref, w_ref, x_ref, gres_ref, vec_ref, gtok_ref, gvec_ref):
     width = x_ref.shape[1]
-    gn = mm_nn(dq_ref[...], w_ref[:width, :])
-    gn += mm_nn(dk_ref[...], w_ref[width : 2 * width, :])
-    gn += mm_nn(dv_ref[...], w_ref[2 * width :, :])
+    gn = jnp.zeros(x_ref.shape, F32)
+    for part in range(3):
+        at = part * width
+        for ref in (d1_ref, d2_ref):
+            gn += mm_nn(ref[part], w_ref[at : at + ref.shape[2], :])
+            at += ref.shape[2]
     xhat, rinv = norm_stats(x_ref[...].astype(F32))
     gtok_ref[...] = gres_ref[...] + norm_back(gn, xhat, rinv, vec_ref[0:1, :])
 
@@ -549,19 +670,21 @@
     gvec_ref[1:2, :] += jnp.sum(gn, axis=0, keepdims=True)
 
 
-def first_back(dq, dk, dv, w_abs, tokens, gres, vecs, rows_block=256):
+def first_back(grads, w_abs, tokens, gres, vecs, rows_block=256):
     rows, width = tokens.shape
     block = pl.BlockSpec((rows_block, width), lambda r: (r, 0))
     full = lambda shape: pl.BlockSpec(shape, lambda r: (0,) * len(shape))
     return pl.pallas_call(
         first_kernel,
         grid=(rows // rows_block,),
-        in_specs=[block, block, block, full(w_abs.shape), block, block, full(vecs.shape)],
+        in_specs=[pl.BlockSpec((3, rows_block, d.shape[2]), lambda r: (0, r, 0)) for d in grads]
+        + [full(w_abs.shape), block, block, full(vecs.shape)],
         out_specs=[block, full((8, width))],
         out_shape=[jax.ShapeDtypeStruct((rows, width), F32), jax.ShapeDtypeStruct((8, width), F32)],
         compiler_params=params(),
+        cost_estimate=cost(6 * rows * width * width, 25e6),
         name="first_back",
-    )(dq, dk, dv, w_abs, tokens, gres, vecs)
+    )(*grads, w_abs, tokens, gres, vecs)
 
 
 def body(plan, tokens, lengths, ln1_gain, ln1_shift, w_qkv, w_out, ln2_gain, ln2_shift, w_up, w_down, cot):
@@ -578,20 +701,23 @@
 
     mlp_piece = jnp.concatenate([w_up.T, w_down, w_out], axis=0)
     mlp_all = lax.all_gather(mlp_piece, AXES, axis=0, tiled=True).reshape(n, -1, width)
-    wo = mlp_all[:, 2 * units :].reshape(width, width)
-    w_ff = mlp_all[:, : 2 * units].reshape(n, 2, units, width)
-    if units % 16 or 768 % units:
-        w_ff = w_ff.transpose(1, 0, 2, 3).reshape(2, ff // 768, 768, width).transpose(1, 0, 2, 3)
+    if plan.direct:
+        w_ff, ff_units, wo_pieces, wo_at = mlp_all, units, mlp_all, 2 * units // per
+    else:
+        ff_units = 768
+        wo_pieces, wo_at = mlp_all[:, 2 * units :].reshape(1, width, width), 0
+        w_ff = mlp_all[:, : 2 * units].reshape(n, 2, units, width).transpose(1, 0, 2, 3)
+        w_ff = w_ff.reshape(2, ff // 768, 768, width).transpose(1, 0, 2, 3).reshape(ff // 768, 2 * 768, width)
 
     if plan.direct:
         flat = jnp.pad(vec_piece.reshape(1, -1), ((0, 7), (0, width - 4 * per)))
-        own, sib = plan.gather(jnp.concatenate([qkv_piece, flat], axis=0))
+        gathered = plan.gather(jnp.concatenate([qkv_piece, flat], axis=0))
         slots = jnp.array(plan.slot_masks() + [m ^ 1 for m in plan.slot_masks()], jnp.int32)
         column = jnp.arange(width, dtype=jnp.int32)
         place = ((slots ^ me)[:, None] == (column // per)[None]).astype(F32)
         lane = jnp.arange(128, dtype=jnp.int32)
-        spread = jnp.stack([(lane[:, None] == v * per + (column % per)[None]).astype(F32) for v in range(4)])
-        mixed, n1, w_abs, vecs = qkv_project(plan, me_arr, tokens, own, sib, spread, place, ppr * n)
+        spread = jnp.stack([(lane[:, None] == v * per + (column % per)[None]).astype(BF16) for v in range(4)])
+        mixed, n1, w_abs, vecs = qkv_project(plan, me_arr, tokens, gathered, spread, place, ppr * n)
     else:
         w_abs = lax.all_gather(qkv_piece, AXES, axis=0, tiled=True)
         vecs = lax.all_gather(vec_piece, AXES, axis=1, tiled=True).astype(F32)
@@ -599,28 +725,48 @@
         mixed, n1 = qkv_plain(tokens, w_abs, vecs)
 
     att, attT, lse = attend_forward(mixed, lengths)
-    residual, n2 = project_out(att, tokens, wo, vecs)
-    output, gn2, gw_ff = feed_forward(lengths, n2, residual, cot, w_ff)
-    if units % 16 or 768 % units:
-        gw_ff = gw_ff.transpose(1, 0, 2, 3).reshape(2, n, units, width).transpose(1, 0, 2, 3)
-    g_ff = lax.psum_scatter(gw_ff.reshape(n * 2 * units, width), AXES, scatter_dimension=0, tiled=True)
+    residual, n2, wo = project_out(att, tokens, wo_pieces, wo_at, vecs)
+    output, gn2, *gw_ff = feed_forward(lengths, me_arr, n2, residual, cot, w_ff, ff_units, plan.direct)
+    if plan.direct:
+        got = plan.swap(gw_ff[1], 1)
+    else:
+        gw_ff = gw_ff[0].reshape(ff // 768, 2, 768, width).transpose(1, 0, 2, 3)
+        gw_ff = gw_ff.reshape(2, n, units, width).transpose(1, 0, 2, 3).reshape(-1, width)
+        g_ff = lax.psum_scatter(gw_ff, AXES, scatter_dimension=0, tiled=True)
     gres, ga, gwo, gvec2 = middle_back(lengths, gn2, residual, cot, att, wo, vecs)
-    dq, dk, dv = attend_backward(mixed, ga, attT, lse, seqs)
+    pairs = width // PAIR
+    late = pairs // 3
     if plan.direct:
-        keep, send = qkv_grad(plan, me_arr, dq, dk, dv, n1, gwo)
-        g_attn = plan.scatter(keep, send).astype(F32)
-        g_qkv, g_out = g_attn[:ppr], g_attn[ppr:]
+        ga, got, keep = lax.optimization_barrier((ga, got, gw_ff[0]))
+        away = plan.first_away(keep, got)
+        back = (plan.swap(away[0], 2), plan.swap(away[1], 4))
+        ga, away = lax.optimization_barrier((ga, away))
+    grads, sums = attend_backward(mixed, ga, attT, lse, seqs, 0, pairs - late)
+    if plan.direct:
+        back, grads, ga, sums = lax.optimization_barrier((back, grads, ga, sums))
+        away = plan.second_away(keep, got, back)
+        again = (plan.swap(away[0], 4), plan.swap(away[1], 2))
+        ga, away = lax.optimization_barrier((ga, away))
+    more, late_sums = attend_backward(mixed, ga, attT, lse, seqs, pairs - late, late)
+    if plan.direct:
+        again, more, n1 = lax.optimization_barrier((again, more, n1))
+        g_ff = plan.last_sum(keep, got, back, again)
+    grads, sums = [grads, more], [sums, late_sums]
+    if plan.direct:
+        keep, send = qkv_grad(plan, me_arr, grads, sums, n1, w_abs, gwo, vecs, gvec2, spread)
+        summed = plan.scatter_first(keep, send, 32)
+        gres, summed = lax.optimization_barrier((gres, summed))
+        g_attn = plan.scatter_rest(*summed)
+        g_attn, g_ff = lax.optimization_barrier((g_attn, g_ff))
+        g_attn = g_attn.astype(F32)
+        g_qkv, g_out = g_attn[:ppr], g_attn[ppr : ppr + per]
+        g_vec = g_attn[ppr + per, : 4 * per].reshape(4, per)
     else:
-        g_qkv = lax.psum_scatter(qkv_grad_plain(dq, dk, dv, n1), AXES, scatter_dimension=0, tiled=True)
+        g_qkv = lax.psum_scatter(qkv_grad_plain(grads, n1), AXES, scatter_dimension=0, tiled=True)
         g_out = lax.psum_scatter(gwo, AXES, scatter_dimension=0, tiled=True)
-    gtok, gvec1 = first_back(dq, dk, dv, w_abs, tokens, gres, vecs)
-    gvec = jnp.concatenate([gvec1[:2], gvec2[:2]], axis=0)
-    if plan.direct:
-        by_piece = gvec.reshape(4, n, per).transpose(1, 0, 2)
-        by_slot = by_piece[slots ^ me]
-        half = n // 2
-        g_vec = plan.scatter(by_slot[:half], by_slot[half:])
-    else:
+    gtok, gvec1 = first_back(grads, w_abs, tokens, gres, vecs)
+    if not plan.direct:
+        gvec = jnp.concatenate([gvec1[:2], gvec2[:2]], axis=0)
         g_vec = lax.psum_scatter(gvec, AXES, scatter_dimension=1, tiled=True)
     g_ff = g_ff.astype(F32)
     return (

time: 334 us -> 320 us (0.958)
  waiting for transfers between devices: 105 us -> 66.3 us
  Pallas kernels: 159 us -> 177 us
  local copies, waits for them, and re-layouts: 17.4 us -> 4.59 us
  other arithmetic: 9.51 us -> 20.9 us
  starting transfers between devices: 26.7 us -> 35.2 us
    ppermute x21 -> x25, waiting for transfers between devices: 83.1 us -> 63.7 us  [swap(): return lax.ppermute(value, AXES, [(i, i ^ mask) for i in range(self.n)])]
    reduce_scatter x1, waiting for transfers between devices: 17.1 us -> 0.02 us  [last_sum(): lax.psum_scatter(whole, AXES, scatter_dimension=0, tiled=True, axis_index...]
    pallas_call x1 -> x2, Pallas kernels: 38.4 us -> 53.6 us  [attend_backward(): pl.pallas_call(functools.partial(attend_back_kernel, maxlen), grid=(seqs,...]
    slice x6 -> x1, local copies, waits for them, and re-layouts: 12.7 us -> 0.64 us  [body(): g_qkv, g_out = (g_attn[:ppr], g_attn[ppr:ppr + per])]
    convert_element_type x2 -> x11, other arithmetic: 2.66 us -> 13.2 us  [add_low(): return total.astype(first.dtype)]
    ppermute x21 -> x25, starting transfers between devices: 26.6 us -> 35.2 us  [swap(): return lax.ppermute(value, AXES, [(i, i ^ mask) for i in range(self.n)])]
  transfers between devices with their start and end apart: 23 -> 27, of which waited for: 17 -> 14; matrix products, arithmetic and copies ran while one was open for 3% -> 4% of each run, Pallas kernels for 33% -> 36%
where the time goes in v2:
time: 320 us; the launch traced here: 319 us
  Pallas kernels  177 us (55%)
  waiting for transfers between devices  66.3 us (21%)
  starting transfers between devices  35.2 us (11%)
  other arithmetic  20.9 us (7%)
  between operations  15.2 us (5%)
  local copies, waits for them, and re-layouts  4.59 us (1%)
    ppermute x25, waiting for transfers between devices, swap(): return lax.ppermute(value, AXES, [(i, i ^ mask) for i in range(self.n)])  63.7 us
    pallas_call x2, Pallas kernels, attend_backward(): pl.pallas_call(functools.partial(attend_back_kernel, maxlen), grid=(seqs,...  53.6 us
    pallas_call x1, Pallas kernels, feed_forward(): pl.pallas_call(functools.partial(mlp_kernel, rows // lengths.shape[0], un...  43.2 us
    ppermute x25, starting transfers between devices, swap(): return lax.ppermute(value, AXES, [(i, i ^ mask) for i in range(self.n)])  35.2 us
    pallas_call x1, Pallas kernels, attend_forward(): pl.pallas_call(functools.partial(attend_kernel, maxlen), grid_spec=pltpu....  31.1 us
    convert_element_type x11, other arithmetic, add_low(): return total.astype(first.dtype)  13.2 us
    pallas_call x1, Pallas kernels, qkv_grad(): pl.pallas_call(functools.partial(qkv_grad_kernel, masks, ppr, opr), grid_...  11.4 us
    pallas_call x1, Pallas kernels, middle_back(): pl.pallas_call(functools.partial(middle_kernel, rows // lengths.shape[0])...  11.2 us
  transfers between devices with their start and end apart: 27, of which 14 were waited for; matrix products, arithmetic and copies ran while one was open for 4% of the time, Pallas kernels for 36%

profile of v2, /device:TPU:0, one launch (start us, length us, event | category | flops | bytes accessed | tf_op | source)
XLA Modules:
  0.0 319.1 jit_solution(16394396350130377665)
XLA Ops:
  10.8 5.1 %collective-permute-start.2 = (bf16[1,80,768]{2,1,0:T(8,128)(2,1)S(1)}, bf16[1,80,768]{2,1,0:T(8,128)(2,1)S(1)}, u32[]{:S(2)}, u32[]{:S(2)}) collective-permute-start(bf16[1,80,768]{2,1,0:T(8,128)(2,1)S(1)} %fusion.21), channel_id=1, source_target_pairs={{0,24},{1,25},{2,26},{3,27},{4,28},{5,29},{6,30},{7,31},{8,16},{9,... | collective-permute-start | bytes 368648 | tf_op jit(solution)/shard_map/ppermute | solution.py:71
  16.5 3.6 %collective-permute-done.2 = bf16[1,80,768]{2,1,0:T(8,128)(2,1)S(1)} collective-permute-done((bf16[1,80,768]{2,1,0:T(8,128)(2,1)S(1)}, bf16[1,80,768]{2,1,0:T(8,128)(2,1)S(1)}, u32[]{:S(2)}, u32[]{:S(2)}) %collective-permute-start.2) | collective-permute-done | bytes 122912 | tf_op jit(solution)/shard_map/ppermute | solution.py:71
  20.1 6.2 %collective-permute-done.1 = bf16[1,80,768]{2,1,0:T(8,128)(2,1)S(1)} collective-permute-done((bf16[1,80,768]{2,1,0:T(8,128)(2,1)S(1)}, bf16[1,80,768]{2,1,0:T(8,128)(2,1)S(1)}, u32[]{:S(2)}, u32[]{:S(2)}) %collective-permute-start.1) | collective-permute-done | bytes 122912 | tf_op jit(solution)/shard_map/ppermute | solution.py:71
  30.1 9.6 %collective-permute-done.3 = bf16[4,80,768]{2,1,0:T(8,128)(2,1)S(1)} collective-permute-done((bf16[4,80,768]{2,1,0:T(8,128)(2,1)S(1)}, bf16[4,80,768]{2,1,0:T(8,128)(2,1)S(1)}, u32[]{:S(2)}, u32[]{:S(2)}) %collective-permute-start.3) | collective-permute-done | bytes 491552 | tf_op jit(solution)/shard_map/ppermute | solution.py:71
  39.7 2.4 collective-permute-done.4
  42.2 16.8 %collective-permute-done.5 = bf16[4,80,768]{2,1,0:T(8,128)(2,1)S(1)} collective-permute-done((bf16[4,80,768]{2,1,0:T(8,128)(2,1)S(1)}, bf16[4,80,768]{2,1,0:T(8,128)(2,1)S(1)}, u32[]{:S(2)}, u32[]{:S(2)}) %collective-permute-start.5) | collective-permute-done | bytes 491552 | tf_op jit(solution)/shard_map/ppermute | solution.py:71
  63.2 10.7 %qkv_project.1 = (bf16[1024,2304]{1,0:T(8,128)(2,1)}, bf16[1024,768]{1,0:T(8,128)(2,1)}, bf16[2304,768]{1,0:T(8,128)(2,1)}, f32[8,768]{1,0:T(8,128)}) custom-call(s32[1]{0:T(128)} %bitcast.me_ref, bf16[1024,768]{1,0:T(8,128)(2,1)} %x_ref.5, bf16[16,80,768]{2,1,0:T(8,128)(2,1)} %copy-done.3, bf16[16,80,768]{2,1,0:T(8,128)(2,1)} %collective-permute-done.6.sib_ref, ...), custom_call_target="tpu_custom_call" | custom-call | flops 3623878656 | bytes 20000000 | tf_op jit(solution)/shard_map/qkv_project/pallas_call | solution.py:171
  73.8 31.1 %attend_forward.1 = (bf16[1024,768]{1,0:T(8,128)(2,1)}, bf16[768,1024]{1,0:T(8,128)(2,1)}, f32[6,8,1024]{2,1,0:T(8,128)}) custom-call(s32[1]{0:T(128)S(6)} %copy.64.len_ref, bf16[1024,2304]{1,0:T(8,128)(2,1)} %get-tuple-element.60.q_ref.k_ref.v_ref, bf16[1024,2304]{1,0:T(8,128)(2,1)} %get-tuple-element.60.q_ref.k_ref.v_ref, ...), custom_call_target="tpu_custom_call" | custom-call | flops 20000000000 | bytes 10000000 | tf_op jit(solution)/shard_map/attend_forward/pallas_call | solution.py:260
  104.9 2.5 all-gather.2.cloned.1.call-done
  107.4 5.9 %project_out.1 = (f32[1024,768]{1,0:T(8,128)}, bf16[1024,768]{1,0:T(8,128)(2,1)}, bf16[768,768]{1,0:T(8,128)(2,1)}) custom-call(bf16[1024,768]{1,0:T(8,128)(2,1)} %get-tuple-element.61.att_ref, bf16[1024,768]{1,0:T(8,128)(2,1)} %x_ref.5, bf16[32,216,768]{2,1,0:T(8,128)(2,1)} %bitcast.139, f32[8,768]{1,0:T(8,128)} %get-tuple-element.62.vec_ref.refs_7_), custom_call_target="tpu_custom_call" | custom-call | flops 1207959552 | bytes 10000000 | tf_op jit(solution)/shard_map/project_out/pallas_call | solution.py:388
  113.3 43.2 %feed_forward.1 = (bf16[1024,768]{1,0:T(8,128)(2,1)}, f32[1024,768]{1,0:T(8,128)}, bf16[16,192,768]{2,1,0:T(8,128)(2,1)}, bf16[16,192,768]{2,1,0:T(8,128)(2,1)}) custom-call(s32[1]{0:T(128)S(6)} %copy.64.len_ref, s32[1]{0:T(128)} %bitcast.me_ref, bf16[1024,768]{1,0:T(8,128)(2,1)} %get-tuple-element.63.n2_ref, f32[1024,768]{1,0:T(8,128)} %get-tuple-element.64.res_ref, ...), custom_call_target="tpu_custom_call" | custom-call | flops 28991029248 | bytes 40000000 | tf_op jit(solution)/shard_map/feed_forward/pallas_call | solution.py:477
  156.9 11.2 %middle_back.1 = (f32[1024,768]{1,0:T(8,128)}, bf16[1024,768]{1,0:T(8,128)(2,1)}, bf16[768,768]{1,0:T(8,128)(2,1)}, f32[8,768]{1,0:T(8,128)}) custom-call(s32[1]{0:T(128)S(6)} %copy.64.len_ref, f32[1024,768]{1,0:T(8,128)} %get-tuple-element.66.gn_ref, f32[1024,768]{1,0:T(8,128)} %get-tuple-element.64.res_ref, f32[1024,768]{1,0:T(8,128)} %cot_ref.3, ...), custom_call_target="tpu_custom_call" | custom-call | flops 2415919104 | bytes 30000000 | tf_op jit(solution)/shard_map/middle_back/pallas_call | solution.py:528
  169.7 2.6 fusion
  174.3 39.4 %attend_backward.2 = (bf16[3,1024,512]{2,1,0:T(8,128)(2,1)}, f32[1,8,512]{2,1,0:T(8,128)}) custom-call(bf16[1024,2304]{1,0:T(8,128)(2,1)} %get-tuple-element.60.q_ref.k_ref.v_ref, bf16[1024,2304]{1,0:T(8,128)(2,1)} %get-tuple-element.60.q_ref.k_ref.v_ref, bf16[1024,2304]{1,0:T(8,128)(2,1)} %get-tuple-element.60.q_ref.k_ref.v_ref, ...), custom_call_target="tpu_custom_call" | custom-call | flops 20000000000 | bytes 8000000 | tf_op jit(solution)/shard_map/attend_backward/pallas_call | solution.py:346
  213.8 2.7 fusion.6
  218.5 14.2 %attend_backward.3 = (bf16[3,1024,256]{2,1,0:T(8,128)(2,1)}, f32[1,8,256]{2,1,0:T(8,128)}) custom-call(bf16[1024,2304]{1,0:T(8,128)(2,1)} %get-tuple-element.60.q_ref.k_ref.v_ref, bf16[1024,2304]{1,0:T(8,128)(2,1)} %get-tuple-element.60.q_ref.k_ref.v_ref, bf16[1024,2304]{1,0:T(8,128)(2,1)} %get-tuple-element.60.q_ref.k_ref.v_ref, ...), custom_call_target="tpu_custom_call" | custom-call | flops 10000000000 | bytes 4000000 | tf_op jit(solution)/shard_map/attend_backward/pallas_call | solution.py:346
  232.7 11.4 %qkv_grad.1 = (bf16[16,104,768]{2,1,0:T(8,128)(2,1)}, bf16[16,104,768]{2,1,0:T(8,128)(2,1)}) custom-call(s32[1]{0:T(128)} %bitcast.me_ref, bf16[3,1024,512]{2,1,0:T(8,128)(2,1)} %get-tuple-element.79.refs_0_.d1_ref, bf16[3,1024,256]{2,1,0:T(8,128)(2,1)} %get-tuple-element.86.refs_1_.d2_ref, f32[1,8,512]{2,1,0:T(8,128)} %get-tuple-element.89.refs_2_, ...), custom_call_target="tpu_custom_call" | custom-call | flops 3623878656 | bytes 25000000 | tf_op jit(solution)/shard_map/qkv_grad/pallas_call | solution.py:613
  259.9 9.8 %first_back.1 = (f32[1024,768]{1,0:T(8,128)}, f32[8,768]{1,0:T(8,128)}) custom-call(bf16[3,1024,512]{2,1,0:T(8,128)(2,1)} %get-tuple-element.79.refs_0_.d1_ref, bf16[3,1024,256]{2,1,0:T(8,128)(2,1)} %get-tuple-element.86.refs_1_.d2_ref, bf16[2304,768]{1,0:T(8,128)(2,1)} %get-tuple-element.87.refs_5_.w_ref, bf16[1024,768]{1,0:T(8,128)(2,1)} %x_ref.5, ...), custom_call_target="tpu_custom_call" | custom-call | flops 3623878656 | bytes 25000000 | tf_op jit(solution)/shard_map/first_back/pallas_call | solution.py:677
  269.6 3.7 %collective-permute-done.13 = bf16[4,32,768]{2,1,0:T(8,128)(2,1)S(1)} collective-permute-done((bf16[4,32,768]{2,1,0:T(8,128)(2,1)S(1)}, bf16[4,32,768]{2,1,0:T(8,128)(2,1)S(1)}, u32[]{:S(2)}, u32[]{:S(2)}) %collective-permute-start.13) | collective-permute-done | bytes 196640 | tf_op jit(solution)/shard_map/ppermute | solution.py:71
  274.9 2.9 collective-permute-done.14
  277.8 5.2 %collective-permute-done.15 = bf16[4,32,768]{2,1,0:T(8,128)(2,1)S(1)} collective-permute-done((bf16[4,32,768]{2,1,0:T(8,128)(2,1)S(1)}, bf16[4,32,768]{2,1,0:T(8,128)(2,1)S(1)}, u32[]{:S(2)}, u32[]{:S(2)}) %collective-permute-start.15) | collective-permute-done | bytes 196640 | tf_op jit(solution)/shard_map/ppermute | solution.py:71
  287.0 8.2 %collective-permute-start.22 = (bf16[72,768]{1,0:T(8,128)(2,1)S(1)}, bf16[72,768]{1,0:T(8,128)(2,1)S(1)}, u32[]{:S(2)}, u32[]{:S(2)}) collective-permute-start(bf16[72,768]{1,0:T(8,128)(2,1)S(1)} %get-tuple-element.121), channel_id=1, source_target_pairs={{0,8},{1,9},{2,10},{3,11},{4,12},{5,13},{6,14},{7,15},{8,0},{9,1},... | collective-permute-start | bytes 331784 | tf_op jit(solution)/shard_map/ppermute | solution.py:71
  298.7 4.3 %collective-permute-done.24 = bf16[72,768]{1,0:T(8,128)(2,1)S(1)} collective-permute-done((bf16[72,768]{1,0:T(8,128)(2,1)S(1)}, bf16[72,768]{1,0:T(8,128)(2,1)S(1)}, u32[]{:S(2)}, u32[]{:S(2)}) %collective-permute-start.24) | collective-permute-done | bytes 110624 | tf_op jit(solution)/shard_map/ppermute | solution.py:71
  303.0 3.6 %collective-permute-done.23 = bf16[72,768]{1,0:T(8,128)(2,1)S(1)} collective-permute-done((bf16[72,768]{1,0:T(8,128)(2,1)S(1)}, bf16[72,768]{1,0:T(8,128)(2,1)S(1)}, u32[]{:S(2)}, u32[]{:S(2)}) %collective-permute-start.23) | collective-permute-done | bytes 110624 | tf_op jit(solution)/shard_map/ppermute | solution.py:71
  (95 shorter events, 47.5 us)
Async XLA Ops:
  7.2 100.2 %all-gather.2.cloned.1.call-start = ((), (), s32[]{:S(2)}) async-start(), calls=%async_computation.1 | async-start | bytes 10948608 | tf_op jit(solution)/shard_map/all_gather | solution.py:703
  9.0 297.7 %reduce-scatter.2.cloned.1.call-start = ((), (), s32[]{:S(2)}) async-start(), calls=%async_computation.2 | async-start | bytes 1474560 | tf_op jit(solution)/shard_map/reduce_scatter | solution.py:122
  10.8 9.4 %collective-permute-start.2 = (bf16[1,80,768]{2,1,0:T(8,128)(2,1)S(1)}, bf16[1,80,768]{2,1,0:T(8,128)(2,1)S(1)}, u32[]{:S(2)}, u32[]{:S(2)}) collective-permute-start(bf16[1,80,768]{2,1,0:T(8,128)(2,1)S(1)} %fusion.21), channel_id=1, source_target_pairs={{0,24},{1,25},{2,26},{3,27},{4,28},{5,29},{6,30},{7,31},{8,16},{9,... | collective-permute-start | bytes 368648 | tf_op jit(solution)/shard_map/ppermute | solution.py:71
  15.9 10.4 %collective-permute-start.1 = (bf16[1,80,768]{2,1,0:T(8,128)(2,1)S(1)}, bf16[1,80,768]{2,1,0:T(8,128)(2,1)S(1)}, u32[]{:S(2)}, u32[]{:S(2)}) collective-permute-start(bf16[1,80,768]{2,1,0:T(8,128)(2,1)S(1)} %fusion.21), channel_id=1, source_target_pairs={{0,16},{1,17},{2,18},{3,19},{4,20},{5,21},{6,22},{7,23},{8,24},{9,... | collective-permute-start | bytes 368648 | tf_op jit(solution)/shard_map/ppermute | solution.py:71
  15.9 10.4 %collective-permute-start = (bf16[1,80,768]{2,1,0:T(8,128)(2,1)S(1)}, bf16[1,80,768]{2,1,0:T(8,128)(2,1)S(1)}, u32[]{:S(2)}, u32[]{:S(2)}) collective-permute-start(bf16[1,80,768]{2,1,0:T(8,128)(2,1)S(1)} %fusion.21), channel_id=1, source_target_pairs={{0,8},{1,9},{2,10},{3,11},{4,12},{5,13},{6,14},{7,15},{8,0},{9,1},... | collective-permute-start | bytes 368648 | tf_op jit(solution)/shard_map/ppermute | solution.py:71
  26.4 13.3 %collective-permute-start.3 = (bf16[4,80,768]{2,1,0:T(8,128)(2,1)S(1)}, bf16[4,80,768]{2,1,0:T(8,128)(2,1)S(1)}, u32[]{:S(2)}, u32[]{:S(2)}) collective-permute-start(bf16[4,80,768]{2,1,0:T(8,128)(2,1)S(1)} %pad_maximum_fusion.1), channel_id=1, source_target_pairs={{0,2},{1,3},{2,0},{3,1},{4,6},{5,7},{6,4},{7,5},{8,10},{9,11},{10,... | collective-permute-start | bytes 1474568 | tf_op jit(solution)/shard_map/ppermute | solution.py:71
  28.0 14.2 %collective-permute-start.4 = (bf16[4,80,768]{2,1,0:T(8,128)(2,1)S(1)}, bf16[4,80,768]{2,1,0:T(8,128)(2,1)S(1)}, u32[]{:S(2)}, u32[]{:S(2)}) collective-permute-start(bf16[4,80,768]{2,1,0:T(8,128)(2,1)S(1)} %pad_maximum_fusion.1), channel_id=1, source_target_pairs={{0,4},{1,5},{2,6},{3,7},{4,0},{5,1},{6,2},{7,3},{8,12},{9,13},{10,... | collective-permute-start | bytes 1474568 | tf_op jit(solution)/shard_map/ppermute | solution.py:71
  29.5 29.4 %collective-permute-start.5 = (bf16[4,80,768]{2,1,0:T(8,128)(2,1)S(1)}, bf16[4,80,768]{2,1,0:T(8,128)(2,1)S(1)}, u32[]{:S(2)}, u32[]{:S(2)}) collective-permute-start(bf16[4,80,768]{2,1,0:T(8,128)(2,1)S(1)} %pad_maximum_fusion.1), channel_id=1, source_target_pairs={{0,6},{1,7},{2,4},{3,5},{4,2},{5,3},{6,0},{7,1},{8,14},{9,15},{10,... | collective-permute-start | bytes 1474568 | tf_op jit(solution)/shard_map/ppermute | solution.py:71
  156.6 11.5 %collective-permute-start.7 = (bf16[16,192,768]{2,1,0:T(8,128)(2,1)}, bf16[16,192,768]{2,1,0:T(8,128)(2,1)}, u32[]{:S(2)}, u32[]{:S(2)}) collective-permute-start(bf16[16,192,768]{2,1,0:T(8,128)(2,1)} %get-tuple-element.69), channel_id=1, source_target_pairs={{0,1},{1,0},{2,3},{3,2},{4,5},{5,4},{6,7},{7,6},{8,9},{9,8},{10,11... | collective-permute-start | bytes 14155784 | tf_op jit(solution)/shard_map/ppermute | solution.py:71
  172.2 41.5 %collective-permute-start.8 = (bf16[4,2,96,768]{3,2,0,1:T(8,128)(2,1)}, bf16[4,2,96,768]{3,2,0,1:T(8,128)(2,1)S(1)}, u32[]{:S(2)}, u32[]{:S(2)}) collective-permute-start(bf16[4,2,96,768]{3,2,0,1:T(8,128)(2,1)} %fusion), channel_id=1, source_target_pairs={{0,2},{1,3},{2,0},{3,1},{4,6},{5,7},{6,4},{7,5},{8,10},{9,11},{10,... | collective-permute-start | bytes 3538952 | tf_op jit(solution)/shard_map/ppermute | solution.py:71
  173.6 40.1 %collective-permute-start.9 = (bf16[4,2,96,768]{3,2,0,1:T(8,128)(2,1)S(1)}, bf16[4,2,96,768]{3,2,0,1:T(8,128)(2,1)S(1)}, u32[]{:S(2)}, u32[]{:S(2)}) collective-permute-start(bf16[4,2,96,768]{3,2,0,1:T(8,128)(2,1)S(1)} %fusion.1), channel_id=1, source_target_pairs={{0,4},{1,5},{2,6},{3,7},{4,0},{5,1},{6,2},{7,3},{8,12},{9,13},{10,... | collective-permute-start | bytes 3538952 | tf_op jit(solution)/shard_map/ppermute | solution.py:71
  216.5 16.2 %collective-permute-start.11 = (bf16[4,96,768]{2,1,0:T(8,128)(2,1)}, bf16[4,96,768]{2,1,0:T(8,128)(2,1)S(1)}, u32[]{:S(2)}, u32[]{:S(2)}) collective-permute-start(bf16[4,96,768]{2,1,0:T(8,128)(2,1)} %get-tuple-element.112), channel_id=1, source_target_pairs={{0,2},{1,3},{2,0},{3,1},{4,6},{5,7},{6,4},{7,5},{8,10},{9,11},{10,... | collective-permute-start | bytes 1769480 | tf_op jit(solution)/shard_map/ppermute | solution.py:71
  217.8 14.9 %collective-permute-start.10 = (bf16[4,96,768]{2,1,0:T(8,128)(2,1)}, bf16[4,96,768]{2,1,0:T(8,128)(2,1)S(1)}, u32[]{:S(2)}, u32[]{:S(2)}) collective-permute-start(bf16[4,96,768]{2,1,0:T(8,128)(2,1)} %get-tuple-element.113), channel_id=1, source_target_pairs={{0,4},{1,5},{2,6},{3,7},{4,0},{5,1},{6,2},{7,3},{8,12},{9,13},{10,... | collective-permute-start | bytes 1769480 | tf_op jit(solution)/shard_map/ppermute | solution.py:71
  253.3 20.0 %collective-permute-start.13 = (bf16[4,32,768]{2,1,0:T(8,128)(2,1)S(1)}, bf16[4,32,768]{2,1,0:T(8,128)(2,1)S(1)}, u32[]{:S(2)}, u32[]{:S(2)}) collective-permute-start(bf16[4,32,768]{2,1,0:T(8,128)(2,1)S(1)} %get-tuple-element.99), channel_id=1, source_target_pairs={{0,8},{1,9},{2,10},{3,11},{4,12},{5,13},{6,14},{7,15},{8,0},{9,1},... | collective-permute-start | bytes 589832 | tf_op jit(solution)/shard_map/ppermute | solution.py:71
  254.8 23.1 %collective-permute-start.14 = (bf16[4,32,768]{2,1,0:T(8,128)(2,1)S(1)}, bf16[4,32,768]{2,1,0:T(8,128)(2,1)S(1)}, u32[]{:S(2)}, u32[]{:S(2)}) collective-permute-start(bf16[4,32,768]{2,1,0:T(8,128)(2,1)S(1)} %get-tuple-element.100), channel_id=1, source_target_pairs={{0,16},{1,17},{2,18},{3,19},{4,20},{5,21},{6,22},{7,23},{8,24},{9,... | collective-permute-start | bytes 589832 | tf_op jit(solution)/shard_map/ppermute | solution.py:71
  255.7 27.3 %collective-permute-start.15 = (bf16[4,32,768]{2,1,0:T(8,128)(2,1)S(1)}, bf16[4,32,768]{2,1,0:T(8,128)(2,1)S(1)}, u32[]{:S(2)}, u32[]{:S(2)}) collective-permute-start(bf16[4,32,768]{2,1,0:T(8,128)(2,1)S(1)} %fusion.19), channel_id=1, source_target_pairs={{0,24},{1,25},{2,26},{3,27},{4,28},{5,29},{6,30},{7,31},{8,16},{9,... | collective-permute-start | bytes 589832 | tf_op jit(solution)/shard_map/ppermute | solution.py:71
  257.8 28.3 %collective-permute-start.19 = (bf16[4,72,768]{2,1,0:T(8,128)(2,1)S(1)}, bf16[4,72,768]{2,1,0:T(8,128)(2,1)S(1)}, u32[]{:S(2)}, u32[]{:S(2)}) collective-permute-start(bf16[4,72,768]{2,1,0:T(8,128)(2,1)S(1)} %get-tuple-element.103), channel_id=1, source_target_pairs={{0,2},{1,3},{2,0},{3,1},{4,6},{5,7},{6,4},{7,5},{8,10},{9,11},{10,... | collective-permute-start | bytes 1327112 | tf_op jit(solution)/shard_map/ppermute | solution.py:71
  259.3 27.4 %collective-permute-start.20 = (bf16[4,72,768]{2,1,0:T(8,128)(2,1)S(1)}, bf16[4,72,768]{2,1,0:T(8,128)(2,1)S(1)}, u32[]{:S(2)}, u32[]{:S(2)}) collective-permute-start(bf16[4,72,768]{2,1,0:T(8,128)(2,1)S(1)} %get-tuple-element.104), channel_id=1, source_target_pairs={{0,4},{1,5},{2,6},{3,7},{4,0},{5,1},{6,2},{7,3},{8,12},{9,13},{10,... | collective-permute-start | bytes 1327112 | tf_op jit(solution)/shard_map/ppermute | solution.py:71
  273.4 13.4 %collective-permute-start.21 = (bf16[4,72,768]{2,1,0:T(8,128)(2,1)S(1)}, bf16[4,72,768]{2,1,0:T(8,128)(2,1)S(1)}, u32[]{:S(2)}, u32[]{:S(2)}) collective-permute-start(bf16[4,72,768]{2,1,0:T(8,128)(2,1)S(1)} %get-tuple-element.105), channel_id=1, source_target_pairs={{0,6},{1,7},{2,4},{3,5},{4,2},{5,3},{6,0},{7,1},{8,14},{9,15},{10,... | collective-permute-start | bytes 1327112 | tf_op jit(solution)/shard_map/ppermute | solution.py:71
  283.2 13.5 %collective-permute-start.16 = (bf16[32,768]{1,0:T(8,128)(2,1)S(1)}, bf16[32,768]{1,0:T(8,128)(2,1)S(1)}, u32[]{:S(2)}, u32[]{:S(2)}) collective-permute-start(bf16[32,768]{1,0:T(8,128)(2,1)S(1)} %get-tuple-element.128), channel_id=1, source_target_pairs={{0,2},{1,3},{2,0},{3,1},{4,6},{5,7},{6,4},{7,5},{8,10},{9,11},{10,... | collective-permute-start | bytes 147464 | tf_op jit(solution)/shard_map/ppermute | solution.py:71
  284.7 12.1 %collective-permute-start.18 = (bf16[32,768]{1,0:T(8,128)(2,1)S(1)}, bf16[32,768]{1,0:T(8,128)(2,1)S(1)}, u32[]{:S(2)}, u32[]{:S(2)}) collective-permute-start(bf16[32,768]{1,0:T(8,128)(2,1)S(1)} %get-tuple-element.129), channel_id=1, source_target_pairs={{0,6},{1,7},{2,4},{3,5},{4,2},{5,3},{6,0},{7,1},{8,14},{9,15},{10,... | collective-permute-start | bytes 147464 | tf_op jit(solution)/shard_map/ppermute | solution.py:71
  286.1 10.7 %collective-permute-start.17 = (bf16[32,768]{1,0:T(8,128)(2,1)S(1)}, bf16[32,768]{1,0:T(8,128)(2,1)S(1)}, u32[]{:S(2)}, u32[]{:S(2)}) collective-permute-start(bf16[32,768]{1,0:T(8,128)(2,1)S(1)} %get-tuple-element.130), channel_id=1, source_target_pairs={{0,4},{1,5},{2,6},{3,7},{4,0},{5,1},{6,2},{7,3},{8,12},{9,13},{10,... | collective-permute-start | bytes 147464 | tf_op jit(solution)/shard_map/ppermute | solution.py:71
  287.0 11.8 %collective-permute-start.22 = (bf16[72,768]{1,0:T(8,128)(2,1)S(1)}, bf16[72,768]{1,0:T(8,128)(2,1)S(1)}, u32[]{:S(2)}, u32[]{:S(2)}) collective-permute-start(bf16[72,768]{1,0:T(8,128)(2,1)S(1)} %get-tuple-element.121), channel_id=1, source_target_pairs={{0,8},{1,9},{2,10},{3,11},{4,12},{5,13},{6,14},{7,15},{8,0},{9,1},... | collective-permute-start | bytes 331784 | tf_op jit(solution)/shard_map/ppermute | solution.py:71
  296.7 9.9 %collective-permute-start.23 = (bf16[72,768]{1,0:T(8,128)(2,1)S(1)}, bf16[72,768]{1,0:T(8,128)(2,1)S(1)}, u32[]{:S(2)}, u32[]{:S(2)}) collective-permute-start(bf16[72,768]{1,0:T(8,128)(2,1)S(1)} %get-tuple-element.123), channel_id=1, source_target_pairs={{0,16},{1,17},{2,18},{3,19},{4,20},{5,21},{6,22},{7,23},{8,24},{9,... | collective-permute-start | bytes 331784 | tf_op jit(solution)/shard_map/ppermute | solution.py:71
  (8 other events, 79.5 us)
Sparse Core Ops, SparseCore 0:
  11.5 95.8 all-gather.1
  247.3 40.4 reduce-scatter.1

commit v3 on v2

--- a/solution.py
+++ b/solution.py
@@ -15,6 +15,7 @@
 EPSILON = 1e-05
 NEGATIVE = -1e30
 TILE = 256
+CHUNK = 32
 AXES = ("dp", "fsdp")
 VMEM_LIMIT = 56 << 20
 GELU_A = math.sqrt(2.0 / math.pi)
@@ -77,24 +78,17 @@
         held = self.spread_stage(self.spread_stage(piece[None], self.along), self.across)
         return held, self.swap(held, 1)
 
-    def scatter_first(self, keep, send, cut):
+    def scatter_first(self, keep, send):
         got = self.swap(send, 1)
-        outer, inner = len(self.masks_of(self.across)), len(self.masks_of(self.along))
-        grid = (outer, inner) + keep.shape[1:]
+        grid = (len(self.masks_of(self.across)), -1) + keep.shape[1:]
         keep, got = keep.reshape(grid), got.reshape(grid)
-        pair = lambda at: add_low(keep[at], [got[at]])
-        head, tail = slice(None, cut), slice(cut, None)
-        first = [pair((slice(None), z, head)) for z in range(inner)]
-        second = [pair((x, slice(None), tail)) for x in range(outer)]
-        return first, second
-
-    def scatter_rest(self, first, second):
+        return [add_low(keep[x], [got[x]]) for x in range(grid[0])]
+
+    def scatter_rest(self, held, beside):
         outer, inner = self.masks_of(self.across), self.masks_of(self.along)
-        second = add_low(second[0], [self.swap(v, m) for v, m in zip(second[1:], outer[1:])])
-        first = add_low(first[0], [self.swap(v, m) for v, m in zip(first[1:], inner[1:])])
-        second = add_low(second[0], [self.swap(second[z], m) for z, m in list(enumerate(inner))[1:]])
-        first = add_low(first[0], [self.swap(first[x], m) for x, m in list(enumerate(outer))[1:]])
-        return jnp.concatenate([first, second], axis=0)
+        held = add_low(held[0], [self.swap(v, m) for v, m in zip(held[1:], outer[1:])])
+        held, beside = lax.optimization_barrier((held, beside))
+        return add_low(held[0], [self.swap(held[z], m) for z, m in list(enumerate(inner))[1:]]), beside
 
     def view(self, held):
         pieces, rows, width = held.shape
@@ -117,8 +111,10 @@
             add_low(k[:, 0, 0, half], [g[:, 0, 0, half], back[half][:, 0], again[half]]) for half in range(2)
         ]
         whole = jnp.concatenate(both, axis=1)
+        return whole.reshape(-1, whole.shape[-1])
+
+    def along_sum(self, whole):
         line = [[r + 8 * z for z in range(self.n // 8)] for r in range(8)]
-        whole = whole.reshape(-1, whole.shape[-1])
         return lax.psum_scatter(whole, AXES, scatter_dimension=0, tiled=True, axis_index_groups=line)
 
 
@@ -223,39 +219,82 @@
     )(tokens, w_abs, vecs)
 
 
-def attend_kernel(maxlen, len_ref, q_ref, k_ref, v_ref, att_ref, attT_ref, lse_ref):
+def tile_at(i, j):
+    return i * (i + 1) // 2 + j
+
+def attend_kernel(maxlen, len_ref, q_ref, k_ref, v_ref, att_ref, attT_ref, inv_ref, keep_ref):
     length = len_ref[pl.program_id(0)]
-    qT = (q_ref[...].astype(F32) * HEAD**-0.5).T.astype(BF16)
+    q, k = q_ref[...], k_ref[...]
+    qT = (q.astype(F32) * HEAD**-0.5).T.astype(BF16)
     vT = v_ref[...].astype(F32).T.astype(BF16)
-    k = k_ref[...]
-    for i in range(maxlen // TILE):
+    same = lax.broadcasted_iota(jnp.int32, (PAIR, PAIR), 0) // HEAD == lax.broadcasted_iota(jnp.int32, (PAIR, PAIR), 1) // HEAD
+    same = jnp.where(same, 1.0, 0.0).astype(BF16)
+    square = lambda a: jnp.max(mm_nn((a.astype(F32) * a.astype(F32)).astype(BF16), same))
+    small = square(q) * square(k) * (1.03 / HEAD) < 70.0**2
+
+    def block(i, plain):
         lo, hi = i * TILE, (i + 1) * TILE
         qpos = lo + lax.broadcasted_iota(jnp.int32, (1, TILE), 1)
         limit = jnp.minimum(qpos, length - 1)
-        kpos = lax.broadcasted_iota(jnp.int32, (hi, TILE), 0)
         blank = jnp.zeros((HEAD, TILE), BF16)
         outs = []
         for h in range(2):
             own = qT[h * HEAD : (h + 1) * HEAD, lo:hi]
             own = jnp.concatenate([own, blank] if h == 0 else [blank, own], axis=0)
-            s = mm_nn(k[:hi], own)
-            t = s * s + 1.0
-            magnitude = jnp.where(kpos <= limit, t * lax.rsqrt(t), NEGATIVE)
-            top = jnp.max(magnitude, axis=0, keepdims=True)
-            e = jnp.exp(magnitude - top)
-            total = jnp.sum(e, axis=0, keepdims=True)
-            weights = (jnp.tanh(s) * e).astype(BF16)
-            outs.append(mm_nn(vT[h * HEAD : (h + 1) * HEAD, :hi], weights) / total)
-            lse_ref[0, h : h + 1, lo:hi] = jnp.where(qpos >= length, -NEGATIVE, top + jnp.log(total))
+
+            def piece(at):
+                s = mm_nn(k[at : at + CHUNK], own)
+                t = s * s + 1.0
+                r = lax.rsqrt(t)
+                kpos = at + lax.broadcasted_iota(jnp.int32, (CHUNK, TILE), 0)
+                return s, r, t * r, (kpos <= limit if at >= lo else kpos < length)
+
+            top = None
+            if not plain:
+                for at in range(0, hi, CHUNK):
+                    s, r, smooth, allowed = piece(at)
+                    here = jnp.max(jnp.where(allowed, smooth, NEGATIVE), axis=0, keepdims=True)
+                    top = here if top is None else jnp.maximum(top, here)
+            total, weights = None, []
+            for at in range(0, hi, CHUNK):
+                s, r, smooth, allowed = piece(at)
+                e = jnp.exp(smooth) if plain else jnp.exp(jnp.minimum(smooth - top, 0.0))
+                e = jnp.where(allowed, e, 0.0)
+                part = e.reshape(CHUNK // 8, 8, TILE).sum(axis=0)
+                total = part if total is None else total + part
+                g = jnp.tanh(s)
+                w = g * e
+                c = e * (s * r)
+                a = e + g * (c - w)
+                w = w.astype(BF16)
+                weights.append(w)
+                tile, row = tile_at(i, at // TILE), at % TILE
+                keep_ref[0, h, 0, tile, row : row + CHUNK, :] = w
+                keep_ref[0, h, 1, tile, row : row + CHUNK, :] = a.astype(BF16)
+                keep_ref[0, h, 2, tile, row : row + CHUNK, :] = c.astype(BF16)
+            inv = 1.0 / jnp.sum(total, axis=0, keepdims=True)
+            inv_ref[0, h : h + 1, lo:hi] = inv
+            outs.append(mm_nn(vT[h * HEAD : (h + 1) * HEAD, :hi], jnp.concatenate(weights, axis=0)) * inv)
         outT = jnp.concatenate(outs, axis=0)
         attT_ref[:, lo:hi] = outT.astype(BF16)
         att_ref[lo:hi, :] = outT.T.astype(BF16)
+
+    @pl.when(small)
+    def _():
+        for i in range(maxlen // TILE):
+            block(i, True)
+
+    @pl.when(jnp.logical_not(small))
+    def _():
+        for i in range(maxlen // TILE):
+            block(i, False)
 
 
 def attend_forward(mixed, lengths):
     rows, width = mixed.shape[0], mixed.shape[1] // 3
     seqs = lengths.shape[0]
     maxlen, pairs = rows // seqs, width // PAIR
+    tiles = tile_at(maxlen // TILE, 0)
     col = lambda part: pl.BlockSpec((maxlen, PAIR), lambda s, p, *_: (s, part * pairs + p))
     return pl.pallas_call(
         functools.partial(attend_kernel, maxlen),
@@ -267,68 +306,64 @@
                 col(0),
                 pl.BlockSpec((PAIR, maxlen), lambda s, p, *_: (p, s)),
                 pl.BlockSpec((1, 8, maxlen), lambda s, p, *_: (s * pairs + p, 0, 0)),
+                pl.BlockSpec((1, 2, 3, tiles, TILE, TILE), lambda s, p, *_: (s * pairs + p, 0, 0, 0, 0, 0)),
             ],
         ),
         out_shape=[
             jax.ShapeDtypeStruct((rows, width), BF16),
             jax.ShapeDtypeStruct((width, rows), BF16),
             jax.ShapeDtypeStruct((seqs * pairs, 8, maxlen), F32),
+            jax.ShapeDtypeStruct((seqs * pairs, 2, 3, tiles, TILE, TILE), BF16),
         ],
         compiler_params=params(),
-        cost_estimate=cost(20e9, 10e6),
+        cost_estimate=cost(20e9, 60e6),
         name="attend_forward",
     )(lengths, mixed, mixed, mixed)
 
 
-def attend_back_kernel(maxlen, q_ref, k_ref, v_ref, ga_ref, attT_ref, lse_ref, d_ref, sum_ref, dqT):
+def attend_back_kernel(maxlen, q_ref, k_ref, v_ref, ga_ref, attT_ref, inv_ref, keep_ref, d_ref, sum_ref, dqT):
     qs = q_ref[...] * jnp.asarray(HEAD**-0.5, BF16)
-    k, v, ga = k_ref[...], v_ref[...], ga_ref[...]
-    qT = qs.astype(F32).T.astype(BF16)
-    kT = k.astype(F32).T.astype(BF16)
-    gaT32 = ga.astype(F32).T
-    gaT = gaT32.astype(BF16)
-    prod = gaT32 * attT_ref[...].astype(F32)
+    v = v_ref[...]
+    kT = k_ref[...].astype(F32).T.astype(BF16)
+    gaT = ga_ref[...].astype(F32).T
+    prod = gaT * attT_ref[...].astype(F32)
+    half = lambda h: slice(h * HEAD, (h + 1) * HEAD)
+    inv = [inv_ref[0, h : h + 1, :] for h in range(2)]
+    gaT = jnp.concatenate([gaT[half(h)] * inv[h] for h in range(2)], axis=0)
+    ga = gaT.T.astype(BF16)
+    gaT = gaT.astype(BF16)
     lane = lax.broadcasted_iota(jnp.int32, (maxlen, PAIR), 1)
     blank = jnp.zeros((HEAD, maxlen), BF16)
     nil = jnp.zeros((), BF16)
     heads = []
     for h in range(2):
         mine = (lane < HEAD) if h == 0 else (lane >= HEAD)
-        at = slice(h * HEAD, (h + 1) * HEAD)
-        pad = lambda a: jnp.concatenate([a, blank] if h == 0 else [blank, a], axis=0)
+        own = gaT[half(h)]
         heads.append(
             (
-                jnp.where(mine, ga, nil), jnp.where(mine, qs, nil), pad(qT[at]), pad(gaT[at]), kT[at],
-                jnp.sum(prod[at], axis=0, keepdims=True), lse_ref[0, h : h + 1, :],
+                jnp.where(mine, ga, nil), jnp.where(mine, qs, nil),
+                jnp.concatenate([own, blank] if h == 0 else [blank, own], axis=0), kT[half(h)],
+                jnp.sum(prod[half(h)], axis=0, keepdims=True) * inv[h],
             )
         )
-    for j in range(maxlen // TILE):
+    blocks = maxlen // TILE
+    for j in range(blocks):
         lo, hi = j * TILE, (j + 1) * TILE
         dv = dk = None
         for h in range(2):
-            ga_h, q_h, qT_h, gaT_h, kT_h, delta, lse = heads[h]
-            s = mm_nn(k[lo:hi], qT_h[:, lo:])
+            ga_h, q_h, gaT_h, kT_h, delta = heads[h]
+            side = lambda part: jnp.concatenate([keep_ref[0, h, part, tile_at(i, j)] for i in range(j, blocks)], axis=1)
             gw = mm_nn(v[lo:hi], gaT_h[:, lo:])
-            t = s * s + 1.0
-            r = lax.rsqrt(t)
-            p = jnp.exp(t * r - lse[:, lo:])
-            kpos = lax.broadcasted_iota(jnp.int32, s.shape, 0)
-            qpos = lax.broadcasted_iota(jnp.int32, s.shape, 1)
-            p = jnp.where(kpos <= qpos, p, 0.0)
-            g = jnp.tanh(s)
-            w = g * p
-            c = p * (s * r)
-            a = p + g * (c - w)
-            ds = (gw * a - c * delta[:, lo:]).astype(BF16)
-            dv_h = mm_nn(w.astype(BF16), ga_h[lo:])
+            ds = (gw * side(1).astype(F32) - side(2).astype(F32) * delta[:, lo:]).astype(BF16)
+            dv_h = mm_nn(side(0), ga_h[lo:])
             dk_h = mm_nn(ds, q_h[lo:])
             dv = dv_h if dv is None else dv + dv_h
             dk = dk_h if dk is None else dk + dk_h
             dq_h = mm_nn(kT_h[:, lo:hi], ds)
             if j == 0:
-                dqT[h * HEAD : (h + 1) * HEAD, :] = dq_h
+                dqT[half(h), :] = dq_h
             else:
-                dqT[h * HEAD : (h + 1) * HEAD, lo:] += dq_h
+                dqT[half(h), lo:] += dq_h
         d_ref[2, lo:hi, :] = dv.astype(BF16)
         d_ref[1, lo:hi, :] = dk.astype(BF16)
         sums = [jnp.sum(d, axis=0, keepdims=True) for d in (dk, dv)]
@@ -339,7 +374,7 @@
     sum_ref[0] = jnp.concatenate(total + [jnp.zeros((5, PAIR), F32)], axis=0)
 
 
-def attend_backward(mixed, ga, attT, lse, seqs, first, count):
+def attend_backward(mixed, ga, attT, inv, keep, seqs, first, count):
     rows, width = mixed.shape[0], mixed.shape[1] // 3
     maxlen, pairs = rows // seqs, width // PAIR
     col = lambda part: pl.BlockSpec((maxlen, PAIR), lambda s, p: (s, part * pairs + p + first))
@@ -350,6 +385,7 @@
             col(0), col(1), col(2), col(0),
             pl.BlockSpec((PAIR, maxlen), lambda s, p: (p + first, s)),
             pl.BlockSpec((1, 8, maxlen), lambda s, p: (s * pairs + p + first, 0, 0)),
+            pl.BlockSpec((1,) + keep.shape[1:], lambda s, p: (s * pairs + p + first, 0, 0, 0, 0, 0)),
         ],
         out_specs=[
             pl.BlockSpec((3, maxlen, PAIR), lambda s, p: (0, s, p)),
@@ -361,9 +397,9 @@
         ],
         scratch_shapes=[pltpu.VMEM((PAIR, maxlen), F32)],
         compiler_params=params(),
-        cost_estimate=cost(5e9 * count, 2e6 * count),
+        cost_estimate=cost(5e9 * count, 10e6 * count),
         name="attend_backward",
-    )(mixed, mixed, mixed, ga, attT, lse)
+    )(mixed, mixed, mixed, ga, attT, inv, keep)
 
 
 def project_kernel(att_ref, x_ref, wp_ref, vec_ref, res_ref, n2_ref, wo_ref):
@@ -724,7 +760,7 @@
         vecs = jnp.pad(vecs, ((0, 4), (0, 0)))
         mixed, n1 = qkv_plain(tokens, w_abs, vecs)
 
-    att, attT, lse = attend_forward(mixed, lengths)
+    att, attT, inv, kept = attend_forward(mixed, lengths)
     residual, n2, wo = project_out(att, tokens, wo_pieces, wo_at, vecs)
     output, gn2, *gw_ff = feed_forward(lengths, me_arr, n2, residual, cot, w_ff, ff_units, plan.direct)
     if plan.direct:
@@ -735,29 +771,28 @@
         g_ff = lax.psum_scatter(gw_ff, AXES, scatter_dimension=0, tiled=True)
     gres, ga, gwo, gvec2 = middle_back(lengths, gn2, residual, cot, att, wo, vecs)
     pairs = width // PAIR
-    late = pairs // 3
+    late = pairs // 6
     if plan.direct:
         ga, got, keep = lax.optimization_barrier((ga, got, gw_ff[0]))
         away = plan.first_away(keep, got)
         back = (plan.swap(away[0], 2), plan.swap(away[1], 4))
         ga, away = lax.optimization_barrier((ga, away))
-    grads, sums = attend_backward(mixed, ga, attT, lse, seqs, 0, pairs - late)
+    grads, sums = attend_backward(mixed, ga, attT, inv, kept, seqs, 0, pairs - late)
     if plan.direct:
         back, grads, ga, sums = lax.optimization_barrier((back, grads, ga, sums))
         away = plan.second_away(keep, got, back)
         again = (plan.swap(away[0], 4), plan.swap(away[1], 2))
         ga, away = lax.optimization_barrier((ga, away))
-    more, late_sums = attend_backward(mixed, ga, attT, lse, seqs, pairs - late, late)
-    if plan.direct:
-        again, more, n1 = lax.optimization_barrier((again, more, n1))
-        g_ff = plan.last_sum(keep, got, back, again)
+    more, late_sums = attend_backward(mixed, ga, attT, inv, kept, seqs, pairs - late, late)
     grads, sums = [grads, more], [sums, late_sums]
     if plan.direct:
-        keep, send = qkv_grad(plan, me_arr, grads, sums, n1, w_abs, gwo, vecs, gvec2, spread)
-        summed = plan.scatter_first(keep, send, 32)
+        q_keep, q_send = qkv_grad(plan, me_arr, grads, sums, n1, w_abs, gwo, vecs, gvec2, spread)
+        again, q_keep, q_send = lax.optimization_barrier((again, q_keep, q_send))
+        whole, q_keep = lax.optimization_barrier((plan.last_sum(keep, got, back, again), q_keep))
+        g_ff = plan.along_sum(whole)
+        summed = plan.scatter_first(q_keep, q_send)
         gres, summed = lax.optimization_barrier((gres, summed))
-        g_attn = plan.scatter_rest(*summed)
-        g_attn, g_ff = lax.optimization_barrier((g_attn, g_ff))
+        g_attn, g_ff = plan.scatter_rest(summed, g_ff)
         g_attn = g_attn.astype(F32)
         g_qkv, g_out = g_attn[:ppr], g_attn[ppr : ppr + per]
         g_vec = g_attn[ppr + per, : 4 * per].reshape(4, per)

time: 320 us -> 296 us (0.925)
  Pallas kernels: 177 us -> 154 us
  starting transfers between devices: 35.2 us -> 21 us
  waiting for transfers between devices: 66.3 us -> 78.5 us
    pallas_call x2, Pallas kernels: 53.6 us -> 30.1 us  [attend_backward(): pl.pallas_call(functools.partial(attend_back_kernel, maxlen), grid=(seqs,...]
    ppermute x25 -> x19, starting transfers between devices: 35.2 us -> 20.9 us  [swap(): return lax.ppermute(value, AXES, [(i, i ^ mask) for i in range(self.n)])]
    ppermute x25 -> x19, waiting for transfers between devices: 63.7 us -> 76.6 us  [swap(): return lax.ppermute(value, AXES, [(i, i ^ mask) for i in range(self.n)])]
    convert_element_type x11 -> x6, other arithmetic: 13.2 us -> 11.3 us  [add_low(): return total.astype(first.dtype)]
  transfers between devices with their start and end apart: 27 -> 21, of which waited for: 14 -> 16; matrix products, arithmetic and copies ran while one was open for 4% -> 3% of each run, Pallas kernels for 36% -> 36%
where the time goes in v3:
time: 296 us; the launch traced here: 293 us
  Pallas kernels  154 us (52%)
  waiting for transfers between devices  78.5 us (27%)
  starting transfers between devices  21 us (7%)
  other arithmetic  18.8 us (6%)
  between operations  15.4 us (5%)
  local copies, waits for them, and re-layouts  4.59 us (2%)
    ppermute x19, waiting for transfers between devices, swap(): return lax.ppermute(value, AXES, [(i, i ^ mask) for i in range(self.n)])  76.6 us
    pallas_call x1, Pallas kernels, feed_forward(): pl.pallas_call(functools.partial(mlp_kernel, rows // lengths.shape[0], un...  43.1 us
    pallas_call x1, Pallas kernels, attend_forward(): pl.pallas_call(functools.partial(attend_kernel, maxlen), grid_spec=pltpu....  31.7 us
    pallas_call x2, Pallas kernels, attend_backward(): pl.pallas_call(functools.partial(attend_back_kernel, maxlen), grid=(seqs,...  30.1 us
    ppermute x19, starting transfers between devices, swap(): return lax.ppermute(value, AXES, [(i, i ^ mask) for i in range(self.n)])  20.9 us
    convert_element_type x6, other arithmetic, add_low(): return total.astype(first.dtype)  11.3 us
    pallas_call x1, Pallas kernels, middle_back(): pl.pallas_call(functools.partial(middle_kernel, rows // lengths.shape[0])...  11.2 us
    pallas_call x1, Pallas kernels, qkv_grad(): pl.pallas_call(functools.partial(qkv_grad_kernel, masks, ppr, opr), grid_...  11.1 us
  transfers between devices with their start and end apart: 21, of which 16 were waited for; matrix products, arithmetic and copies ran while one was open for 3% of the time, Pallas kernels for 36%

profile of v3, /device:TPU:0, one launch (start us, length us, event | category | flops | bytes accessed | tf_op | source)
XLA Modules:
  0.0 292.8 jit_solution(4851994980643562215)
XLA Ops:
  10.8 5.1 %collective-permute-start.2 = (bf16[1,80,768]{2,1,0:T(8,128)(2,1)S(1)}, bf16[1,80,768]{2,1,0:T(8,128)(2,1)S(1)}, u32[]{:S(2)}, u32[]{:S(2)}) collective-permute-start(bf16[1,80,768]{2,1,0:T(8,128)(2,1)S(1)} %fusion.14), channel_id=1, source_target_pairs={{0,24},{1,25},{2,26},{3,27},{4,28},{5,29},{6,30},{7,31},{8,16},{9,... | collective-permute-start | bytes 368648 | tf_op jit(solution)/shard_map/ppermute | solution.py:72
  16.5 3.6 %collective-permute-done.2 = bf16[1,80,768]{2,1,0:T(8,128)(2,1)S(1)} collective-permute-done((bf16[1,80,768]{2,1,0:T(8,128)(2,1)S(1)}, bf16[1,80,768]{2,1,0:T(8,128)(2,1)S(1)}, u32[]{:S(2)}, u32[]{:S(2)}) %collective-permute-start.2) | collective-permute-done | bytes 122912 | tf_op jit(solution)/shard_map/ppermute | solution.py:72
  20.1 6.2 %collective-permute-done.1 = bf16[1,80,768]{2,1,0:T(8,128)(2,1)S(1)} collective-permute-done((bf16[1,80,768]{2,1,0:T(8,128)(2,1)S(1)}, bf16[1,80,768]{2,1,0:T(8,128)(2,1)S(1)}, u32[]{:S(2)}, u32[]{:S(2)}) %collective-permute-start.1) | collective-permute-done | bytes 122912 | tf_op jit(solution)/shard_map/ppermute | solution.py:72
  30.1 9.6 %collective-permute-done.3 = bf16[4,80,768]{2,1,0:T(8,128)(2,1)S(1)} collective-permute-done((bf16[4,80,768]{2,1,0:T(8,128)(2,1)S(1)}, bf16[4,80,768]{2,1,0:T(8,128)(2,1)S(1)}, u32[]{:S(2)}, u32[]{:S(2)}) %collective-permute-start.3) | collective-permute-done | bytes 491552 | tf_op jit(solution)/shard_map/ppermute | solution.py:72
  39.7 2.4 collective-permute-done.4
  42.2 16.8 %collective-permute-done.5 = bf16[4,80,768]{2,1,0:T(8,128)(2,1)S(1)} collective-permute-done((bf16[4,80,768]{2,1,0:T(8,128)(2,1)S(1)}, bf16[4,80,768]{2,1,0:T(8,128)(2,1)S(1)}, u32[]{:S(2)}, u32[]{:S(2)}) %collective-permute-start.5) | collective-permute-done | bytes 491552 | tf_op jit(solution)/shard_map/ppermute | solution.py:72
  63.2 10.7 %qkv_project.1 = (bf16[1024,2304]{1,0:T(8,128)(2,1)}, bf16[1024,768]{1,0:T(8,128)(2,1)}, bf16[2304,768]{1,0:T(8,128)(2,1)}, f32[8,768]{1,0:T(8,128)}) custom-call(s32[1]{0:T(128)} %bitcast.me_ref, bf16[1024,768]{1,0:T(8,128)(2,1)} %x_ref.5, bf16[16,80,768]{2,1,0:T(8,128)(2,1)} %copy-done.3, bf16[16,80,768]{2,1,0:T(8,128)(2,1)} %collective-permute-done.6.sib_ref, ...), custom_call_target="tpu_custom_call" | custom-call | flops 3623878656 | bytes 20000000 | tf_op jit(solution)/shard_map/qkv_project/pallas_call | solution.py:167
  73.8 31.7 %attend_forward.1 = (bf16[1024,768]{1,0:T(8,128)(2,1)}, bf16[768,1024]{1,0:T(8,128)(2,1)}, f32[6,8,1024]{2,1,0:T(8,128)}, bf16[6,2,3,10,256,256]{5,4,3,2,1,0:T(8,128)(2,1)}) custom-call(s32[1]{0:T(128)S(6)} %copy.52.len_ref, bf16[1024,2304]{1,0:T(8,128)(2,1)} %get-tuple-element.59.q_ref.k_ref.v_ref, bf16[1024,2304]{1,0:T(8,128)(2,1)} %get-tuple-element.59.q_ref.k_ref.v_ref, ...), custom_call_target="tpu_custom_call" | custom-call | flops 20000000000 | bytes 60000000 | tf_op jit(solution)/shard_map/attend_forward/pallas_call | solution.py:299
  107.4 5.9 %project_out.1 = (f32[1024,768]{1,0:T(8,128)}, bf16[1024,768]{1,0:T(8,128)(2,1)}, bf16[768,768]{1,0:T(8,128)(2,1)}) custom-call(bf16[1024,768]{1,0:T(8,128)(2,1)} %get-tuple-element.60.att_ref, bf16[1024,768]{1,0:T(8,128)(2,1)} %x_ref.5, bf16[32,216,768]{2,1,0:T(8,128)(2,1)} %bitcast.84, f32[8,768]{1,0:T(8,128)} %get-tuple-element.61.vec_ref.refs_7_), custom_call_target="tpu_custom_call" | custom-call | flops 1207959552 | bytes 10000000 | tf_op jit(solution)/shard_map/project_out/pallas_call | solution.py:424
  113.3 43.1 %feed_forward.1 = (bf16[1024,768]{1,0:T(8,128)(2,1)}, f32[1024,768]{1,0:T(8,128)}, bf16[16,192,768]{2,1,0:T(8,128)(2,1)}, bf16[16,192,768]{2,1,0:T(8,128)(2,1)}) custom-call(s32[1]{0:T(128)S(6)} %copy.52.len_ref, s32[1]{0:T(128)} %bitcast.me_ref, bf16[1024,768]{1,0:T(8,128)(2,1)} %get-tuple-element.62.n2_ref, f32[1024,768]{1,0:T(8,128)} %get-tuple-element.63.res_ref, ...), custom_call_target="tpu_custom_call" | custom-call | flops 28991029248 | bytes 40000000 | tf_op jit(solution)/shard_map/feed_forward/pallas_call | solution.py:513
  156.6 11.2 %middle_back.1 = (f32[1024,768]{1,0:T(8,128)}, bf16[1024,768]{1,0:T(8,128)(2,1)}, bf16[768,768]{1,0:T(8,128)(2,1)}, f32[8,768]{1,0:T(8,128)}) custom-call(s32[1]{0:T(128)S(6)} %copy.52.len_ref, f32[1024,768]{1,0:T(8,128)} %get-tuple-element.65.gn_ref, f32[1024,768]{1,0:T(8,128)} %get-tuple-element.63.res_ref, f32[1024,768]{1,0:T(8,128)} %cot_ref.3, ...), custom_call_target="tpu_custom_call" | custom-call | flops 2415919104 | bytes 30000000 | tf_op jit(solution)/shard_map/middle_back/pallas_call | solution.py:564
  169.4 2.6 fusion
  174.0 22.4 %attend_backward.2 = (bf16[3,1024,640]{2,1,0:T(8,128)(2,1)}, f32[1,8,640]{2,1,0:T(8,128)}) custom-call(bf16[1024,2304]{1,0:T(8,128)(2,1)} %get-tuple-element.59.q_ref.k_ref.v_ref, bf16[1024,2304]{1,0:T(8,128)(2,1)} %get-tuple-element.59.q_ref.k_ref.v_ref, bf16[1024,2304]{1,0:T(8,128)(2,1)} %get-tuple-element.59.q_ref.k_ref.v_ref, ...), custom_call_target="tpu_custom_call" | custom-call | flops 24999999488 | bytes 50000000 | tf_op jit(solution)/shard_map/attend_backward/pallas_call | solution.py:381
  196.4 3.9 %collective-permute-done.8 = bf16[4,2,96,768]{3,2,0,1:T(8,128)(2,1)S(1)} collective-permute-done((bf16[4,2,96,768]{3,2,0,1:T(8,128)(2,1)}, bf16[4,2,96,768]{3,2,0,1:T(8,128)(2,1)S(1)}, u32[]{:S(2)}, u32[]{:S(2)}) %collective-permute-start.8) | collective-permute-done | bytes 1179680 | tf_op jit(solution)/shard_map/ppermute | solution.py:72
  201.3 2.7 fusion.6
  206.0 7.8 %attend_backward.3 = (bf16[3,1024,128]{2,1,0:T(8,128)(2,1)}, f32[1,8,128]{2,1,0:T(8,128)}) custom-call(bf16[1024,2304]{1,0:T(8,128)(2,1)} %get-tuple-element.59.q_ref.k_ref.v_ref, bf16[1024,2304]{1,0:T(8,128)(2,1)} %get-tuple-element.59.q_ref.k_ref.v_ref, bf16[1024,2304]{1,0:T(8,128)(2,1)} %get-tuple-element.59.q_ref.k_ref.v_ref, ...), custom_call_target="tpu_custom_call" | custom-call | flops 5000000000 | bytes 10000000 | tf_op jit(solution)/shard_map/attend_backward/pallas_call | solution.py:381
  213.8 11.1 %qkv_grad.1 = (bf16[16,104,768]{2,1,0:T(8,128)(2,1)}, bf16[16,104,768]{2,1,0:T(8,128)(2,1)}) custom-call(s32[1]{0:T(128)} %bitcast.me_ref, bf16[3,1024,640]{2,1,0:T(8,128)(2,1)} %get-tuple-element.79.refs_0_.d1_ref, bf16[3,1024,128]{2,1,0:T(8,128)(2,1)} %get-tuple-element.84.refs_1_.d2_ref, f32[1,8,640]{2,1,0:T(8,128)} %get-tuple-element.87.refs_2_, ...), custom_call_target="tpu_custom_call" | custom-call | flops 3623878656 | bytes 25000000 | tf_op jit(solution)/shard_map/qkv_grad/pallas_call | solution.py:649
  230.2 2.3 add_convert_fusion.4
  236.0 10.6 %first_back.1 = (f32[1024,768]{1,0:T(8,128)}, f32[8,768]{1,0:T(8,128)}) custom-call(bf16[3,1024,640]{2,1,0:T(8,128)(2,1)} %get-tuple-element.79.refs_0_.d1_ref, bf16[3,1024,128]{2,1,0:T(8,128)(2,1)} %get-tuple-element.84.refs_1_.d2_ref, bf16[2304,768]{1,0:T(8,128)(2,1)} %get-tuple-element.85.refs_5_.w_ref, bf16[1024,768]{1,0:T(8,128)(2,1)} %x_ref.5, ...), custom_call_target="tpu_custom_call" | custom-call | flops 3623878656 | bytes 25000000 | tf_op jit(solution)/shard_map/first_back/pallas_call | solution.py:713
  246.6 2.4 collective-permute-done.13
  250.4 13.4 %collective-permute-done.15 = bf16[4,104,768]{2,1,0:T(8,128)(2,1)S(1)} collective-permute-done((bf16[4,104,768]{2,1,0:T(8,128)(2,1)S(1)}, bf16[4,104,768]{2,1,0:T(8,128)(2,1)S(1)}, u32[]{:S(2)}, u32[]{:S(2)}) %collective-permute-start.15) | collective-permute-done | bytes 639008 | tf_op jit(solution)/shard_map/ppermute | solution.py:72
  271.1 3.3 %collective-permute-done.16 = bf16[104,768]{1,0:T(8,128)(2,1)S(1)} collective-permute-done((bf16[104,768]{1,0:T(8,128)(2,1)S(1)}, bf16[104,768]{1,0:T(8,128)(2,1)S(1)}, u32[]{:S(2)}, u32[]{:S(2)}) %collective-permute-start.16) | collective-permute-done | bytes 159776 | tf_op jit(solution)/shard_map/ppermute | solution.py:72
  274.4 3.9 %collective-permute-done.18 = bf16[104,768]{1,0:T(8,128)(2,1)S(1)} collective-permute-done((bf16[104,768]{1,0:T(8,128)(2,1)S(1)}, bf16[104,768]{1,0:T(8,128)(2,1)S(1)}, u32[]{:S(2)}, u32[]{:S(2)}) %collective-permute-start.18) | collective-permute-done | bytes 159776 | tf_op jit(solution)/shard_map/ppermute | solution.py:72
  278.4 5.1 %collective-permute-done.17 = bf16[104,768]{1,0:T(8,128)(2,1)S(1)} collective-permute-done((bf16[104,768]{1,0:T(8,128)(2,1)S(1)}, bf16[104,768]{1,0:T(8,128)(2,1)S(1)}, u32[]{:S(2)}, u32[]{:S(2)}) %collective-permute-start.17) | collective-permute-done | bytes 159776 | tf_op jit(solution)/shard_map/ppermute | solution.py:72
  (76 shorter events, 39.7 us)
Async XLA Ops:
  7.2 22.3 %copy-start.2 = (bf16[768,72]{0,1:T(8,128)(2,1)S(1)}, bf16[768,72]{0,1:T(8,128)(2,1)}, u32[]{:S(2)}) copy-start(bf16[768,72]{0,1:T(8,128)(2,1)} %param.16) | copy-start | bytes 331780
  7.2 100.2 %all-gather.2.cloned.1.call-start = ((), (), s32[]{:S(2)}) async-start(), calls=%async_computation.1 | async-start | bytes 10948608 | tf_op jit(solution)/shard_map/all_gather | solution.py:739
  9.0 255.1 %reduce-scatter.2.cloned.1.call-start = ((), (), s32[]{:S(2)}) async-start(), calls=%async_computation.2 | async-start | bytes 1474560 | tf_op jit(solution)/shard_map/reduce_scatter | solution.py:118
  10.8 9.4 %collective-permute-start.2 = (bf16[1,80,768]{2,1,0:T(8,128)(2,1)S(1)}, bf16[1,80,768]{2,1,0:T(8,128)(2,1)S(1)}, u32[]{:S(2)}, u32[]{:S(2)}) collective-permute-start(bf16[1,80,768]{2,1,0:T(8,128)(2,1)S(1)} %fusion.14), channel_id=1, source_target_pairs={{0,24},{1,25},{2,26},{3,27},{4,28},{5,29},{6,30},{7,31},{8,16},{9,... | collective-permute-start | bytes 368648 | tf_op jit(solution)/shard_map/ppermute | solution.py:72
  15.9 10.4 %collective-permute-start.1 = (bf16[1,80,768]{2,1,0:T(8,128)(2,1)S(1)}, bf16[1,80,768]{2,1,0:T(8,128)(2,1)S(1)}, u32[]{:S(2)}, u32[]{:S(2)}) collective-permute-start(bf16[1,80,768]{2,1,0:T(8,128)(2,1)S(1)} %fusion.14), channel_id=1, source_target_pairs={{0,16},{1,17},{2,18},{3,19},{4,20},{5,21},{6,22},{7,23},{8,24},{9,... | collective-permute-start | bytes 368648 | tf_op jit(solution)/shard_map/ppermute | solution.py:72
  15.9 10.4 %collective-permute-start = (bf16[1,80,768]{2,1,0:T(8,128)(2,1)S(1)}, bf16[1,80,768]{2,1,0:T(8,128)(2,1)S(1)}, u32[]{:S(2)}, u32[]{:S(2)}) collective-permute-start(bf16[1,80,768]{2,1,0:T(8,128)(2,1)S(1)} %fusion.14), channel_id=1, source_target_pairs={{0,8},{1,9},{2,10},{3,11},{4,12},{5,13},{6,14},{7,15},{8,0},{9,1},... | collective-permute-start | bytes 368648 | tf_op jit(solution)/shard_map/ppermute | solution.py:72
  26.4 13.3 %collective-permute-start.3 = (bf16[4,80,768]{2,1,0:T(8,128)(2,1)S(1)}, bf16[4,80,768]{2,1,0:T(8,128)(2,1)S(1)}, u32[]{:S(2)}, u32[]{:S(2)}) collective-permute-start(bf16[4,80,768]{2,1,0:T(8,128)(2,1)S(1)} %pad_maximum_fusion.1), channel_id=1, source_target_pairs={{0,2},{1,3},{2,0},{3,1},{4,6},{5,7},{6,4},{7,5},{8,10},{9,11},{10,... | collective-permute-start | bytes 1474568 | tf_op jit(solution)/shard_map/ppermute | solution.py:72
  28.0 14.2 %collective-permute-start.4 = (bf16[4,80,768]{2,1,0:T(8,128)(2,1)S(1)}, bf16[4,80,768]{2,1,0:T(8,128)(2,1)S(1)}, u32[]{:S(2)}, u32[]{:S(2)}) collective-permute-start(bf16[4,80,768]{2,1,0:T(8,128)(2,1)S(1)} %pad_maximum_fusion.1), channel_id=1, source_target_pairs={{0,4},{1,5},{2,6},{3,7},{4,0},{5,1},{6,2},{7,3},{8,12},{9,13},{10,... | collective-permute-start | bytes 1474568 | tf_op jit(solution)/shard_map/ppermute | solution.py:72
  29.5 29.4 %collective-permute-start.5 = (bf16[4,80,768]{2,1,0:T(8,128)(2,1)S(1)}, bf16[4,80,768]{2,1,0:T(8,128)(2,1)S(1)}, u32[]{:S(2)}, u32[]{:S(2)}) collective-permute-start(bf16[4,80,768]{2,1,0:T(8,128)(2,1)S(1)} %pad_maximum_fusion.1), channel_id=1, source_target_pairs={{0,6},{1,7},{2,4},{3,5},{4,2},{5,3},{6,0},{7,1},{8,14},{9,15},{10,... | collective-permute-start | bytes 1474568 | tf_op jit(solution)/shard_map/ppermute | solution.py:72
  42.2 18.9 %copy-start.4 = (s32[32]{0:T(128)S(1)}, s32[32]{0:T(128)}, u32[]{:S(2)}) copy-start(s32[32]{0:T(128)} %constant.50.clone) | copy-start | bytes 388
  59.0 4.2 %collective-permute-start.6 = (bf16[16,80,768]{2,1,0:T(8,128)(2,1)S(1)}, bf16[16,80,768]{2,1,0:T(8,128)(2,1)}, u32[]{:S(2)}, u32[]{:S(2)}) collective-permute-start(bf16[16,80,768]{2,1,0:T(8,128)(2,1)S(1)} %constant_dynamic-update-slice_fusion.own_ref), channel_id=1, source_target_pairs={{0,1},{1,0},{2,3},{3,2},{4,5},{5,4},{6,7},{7,6},{8,9},{9,8},{10,11... | collective-permute-start | bytes 5898248 | tf_op jit(solution)/shard_map/ppermute | solution.py:72
  156.4 11.5 %collective-permute-start.7 = (bf16[16,192,768]{2,1,0:T(8,128)(2,1)}, bf16[16,192,768]{2,1,0:T(8,128)(2,1)}, u32[]{:S(2)}, u32[]{:S(2)}) collective-permute-start(bf16[16,192,768]{2,1,0:T(8,128)(2,1)} %get-tuple-element.68), channel_id=1, source_target_pairs={{0,1},{1,0},{2,3},{3,2},{4,5},{5,4},{6,7},{7,6},{8,9},{9,8},{10,11... | collective-permute-start | bytes 14155784 | tf_op jit(solution)/shard_map/ppermute | solution.py:72
  156.6 11.2 %copy-start = (bf16[16,192,768]{2,1,0:T(8,128)(2,1)S(1)}, bf16[16,192,768]{2,1,0:T(8,128)(2,1)}, u32[]{:S(2)}) copy-start(bf16[16,192,768]{2,1,0:T(8,128)(2,1)} %get-tuple-element.70) | copy-start | bytes 14155780
  172.0 28.3 %collective-permute-start.8 = (bf16[4,2,96,768]{3,2,0,1:T(8,128)(2,1)}, bf16[4,2,96,768]{3,2,0,1:T(8,128)(2,1)S(1)}, u32[]{:S(2)}, u32[]{:S(2)}) collective-permute-start(bf16[4,2,96,768]{3,2,0,1:T(8,128)(2,1)} %fusion), channel_id=1, source_target_pairs={{0,2},{1,3},{2,0},{3,1},{4,6},{5,7},{6,4},{7,5},{8,10},{9,11},{10,... | collective-permute-start | bytes 3538952 | tf_op jit(solution)/shard_map/ppermute | solution.py:72
  173.5 27.9 %collective-permute-start.9 = (bf16[4,2,96,768]{3,2,0,1:T(8,128)(2,1)S(1)}, bf16[4,2,96,768]{3,2,0,1:T(8,128)(2,1)S(1)}, u32[]{:S(2)}, u32[]{:S(2)}) collective-permute-start(bf16[4,2,96,768]{3,2,0,1:T(8,128)(2,1)S(1)} %fusion.1), channel_id=1, source_target_pairs={{0,4},{1,5},{2,6},{3,7},{4,0},{5,1},{6,2},{7,3},{8,12},{9,13},{10,... | collective-permute-start | bytes 3538952 | tf_op jit(solution)/shard_map/ppermute | solution.py:72
  204.0 20.9 %collective-permute-start.11 = (bf16[4,96,768]{2,1,0:T(8,128)(2,1)}, bf16[4,96,768]{2,1,0:T(8,128)(2,1)S(1)}, u32[]{:S(2)}, u32[]{:S(2)}) collective-permute-start(bf16[4,96,768]{2,1,0:T(8,128)(2,1)} %get-tuple-element.110), channel_id=1, source_target_pairs={{0,2},{1,3},{2,0},{3,1},{4,6},{5,7},{6,4},{7,5},{8,10},{9,11},{10,... | collective-permute-start | bytes 1769480 | tf_op jit(solution)/shard_map/ppermute | solution.py:72
  204.6 20.4 %collective-permute-start.10 = (bf16[4,96,768]{2,1,0:T(8,128)(2,1)}, bf16[4,96,768]{2,1,0:T(8,128)(2,1)S(1)}, u32[]{:S(2)}, u32[]{:S(2)}) collective-permute-start(bf16[4,96,768]{2,1,0:T(8,128)(2,1)} %get-tuple-element.111), channel_id=1, source_target_pairs={{0,4},{1,5},{2,6},{3,7},{4,0},{5,1},{6,2},{7,3},{8,12},{9,13},{10,... | collective-permute-start | bytes 1769480 | tf_op jit(solution)/shard_map/ppermute | solution.py:72
  224.9 5.2 %collective-permute-start.12 = (bf16[16,104,768]{2,1,0:T(8,128)(2,1)}, bf16[16,104,768]{2,1,0:T(8,128)(2,1)}, u32[]{:S(2)}, u32[]{:S(2)}) collective-permute-start(bf16[16,104,768]{2,1,0:T(8,128)(2,1)} %get-tuple-element.98), channel_id=1, source_target_pairs={{0,1},{1,0},{2,3},{3,2},{4,5},{5,4},{6,7},{7,6},{8,9},{9,8},{10,11... | collective-permute-start | bytes 7667720 | tf_op jit(solution)/shard_map/ppermute | solution.py:72
  232.4 16.5 %collective-permute-start.13 = (bf16[4,104,768]{2,1,0:T(8,128)(2,1)S(1)}, bf16[4,104,768]{2,1,0:T(8,128)(2,1)S(1)}, u32[]{:S(2)}, u32[]{:S(2)}) collective-permute-start(bf16[4,104,768]{2,1,0:T(8,128)(2,1)S(1)} %get-tuple-element.102), channel_id=1, source_target_pairs={{0,2},{1,3},{2,0},{3,1},{4,6},{5,7},{6,4},{7,5},{8,10},{9,11},{10,... | collective-permute-start | bytes 1916936 | tf_op jit(solution)/shard_map/ppermute | solution.py:72
  233.1 17.3 %collective-permute-start.14 = (bf16[4,104,768]{2,1,0:T(8,128)(2,1)S(1)}, bf16[4,104,768]{2,1,0:T(8,128)(2,1)S(1)}, u32[]{:S(2)}, u32[]{:S(2)}) collective-permute-start(bf16[4,104,768]{2,1,0:T(8,128)(2,1)S(1)} %get-tuple-element.103), channel_id=1, source_target_pairs={{0,4},{1,5},{2,6},{3,7},{4,0},{5,1},{6,2},{7,3},{8,12},{9,13},{10,... | collective-permute-start | bytes 1916936 | tf_op jit(solution)/shard_map/ppermute | solution.py:72
  234.6 29.2 %collective-permute-start.15 = (bf16[4,104,768]{2,1,0:T(8,128)(2,1)S(1)}, bf16[4,104,768]{2,1,0:T(8,128)(2,1)S(1)}, u32[]{:S(2)}, u32[]{:S(2)}) collective-permute-start(bf16[4,104,768]{2,1,0:T(8,128)(2,1)S(1)} %get-tuple-element.104), channel_id=1, source_target_pairs={{0,6},{1,7},{2,4},{3,5},{4,2},{5,3},{6,0},{7,1},{8,14},{9,15},{10,... | collective-permute-start | bytes 1916936 | tf_op jit(solution)/shard_map/ppermute | solution.py:72
  266.8 7.6 %collective-permute-start.16 = (bf16[104,768]{1,0:T(8,128)(2,1)S(1)}, bf16[104,768]{1,0:T(8,128)(2,1)S(1)}, u32[]{:S(2)}, u32[]{:S(2)}) collective-permute-start(bf16[104,768]{1,0:T(8,128)(2,1)S(1)} %get-tuple-element.116), channel_id=1, source_target_pairs={{0,8},{1,9},{2,10},{3,11},{4,12},{5,13},{6,14},{7,15},{8,0},{9,1},... | collective-permute-start | bytes 479240 | tf_op jit(solution)/shard_map/ppermute | solution.py:72
  268.2 10.2 %collective-permute-start.18 = (bf16[104,768]{1,0:T(8,128)(2,1)S(1)}, bf16[104,768]{1,0:T(8,128)(2,1)S(1)}, u32[]{:S(2)}, u32[]{:S(2)}) collective-permute-start(bf16[104,768]{1,0:T(8,128)(2,1)S(1)} %get-tuple-element.117), channel_id=1, source_target_pairs={{0,24},{1,25},{2,26},{3,27},{4,28},{5,29},{6,30},{7,31},{8,16},{9,... | collective-permute-start | bytes 479240 | tf_op jit(solution)/shard_map/ppermute | solution.py:72
  270.1 13.3 %collective-permute-start.17 = (bf16[104,768]{1,0:T(8,128)(2,1)S(1)}, bf16[104,768]{1,0:T(8,128)(2,1)S(1)}, u32[]{:S(2)}, u32[]{:S(2)}) collective-permute-start(bf16[104,768]{1,0:T(8,128)(2,1)S(1)} %get-tuple-element.118), channel_id=1, source_target_pairs={{0,16},{1,17},{2,18},{3,19},{4,20},{5,21},{6,22},{7,23},{8,24},{9,... | collective-permute-start | bytes 479240 | tf_op jit(solution)/shard_map/ppermute | solution.py:72
  (2 other events, 7.5 us)
Sparse Core Ops, SparseCore 0:
  11.5 95.8 all-gather.1
  228.1 27.7 reduce-scatter.1

commit v4 on v3

--- a/solution.py
+++ b/solution.py
@@ -78,17 +78,26 @@
         held = self.spread_stage(self.spread_stage(piece[None], self.along), self.across)
         return held, self.swap(held, 1)
 
-    def scatter_first(self, keep, send):
+    def scatter_first(self, keep, send, cut):
         got = self.swap(send, 1)
-        grid = (len(self.masks_of(self.across)), -1) + keep.shape[1:]
+        grid = (2, 2, -1) + keep.shape[1:]
         keep, got = keep.reshape(grid), got.reshape(grid)
-        return [add_low(keep[x], [got[x]]) for x in range(grid[0])]
-
-    def scatter_rest(self, held, beside):
-        outer, inner = self.masks_of(self.across), self.masks_of(self.along)
-        held = add_low(held[0], [self.swap(v, m) for v, m in zip(held[1:], outer[1:])])
-        held, beside = lax.optimization_barrier((held, beside))
-        return add_low(held[0], [self.swap(held[z], m) for z, m in list(enumerate(inner))[1:]]), beside
+        pair = lambda at: add_low(keep[at], [got[at]])
+        every, head, tail = slice(None), slice(None, cut), slice(cut, None)
+        one = [pair((every, y, every, head)) for y in range(2)]
+        two = [pair((x, every, every, tail)) for x in range(2)]
+        return one, two
+
+    def scatter_rest(self, one, two, beside):
+        inner = self.masks_of(self.along)
+        arriving = self.swap(one[1], 2), self.swap(two[1], 4)
+        stay = [add_low(own[0][0], [got[0]]) for own, got in ((one, arriving[0]), (two, arriving[1]))]
+        goes = [add_low(own[0][1], [got[1]]) for own, got in ((one, arriving[0]), (two, arriving[1]))]
+        got = self.swap(goes[0], 4), self.swap(goes[1], 2)
+        held = jnp.concatenate([add_low(stay[0], [got[0]]), add_low(stay[1], [got[1]])], axis=1)
+        arriving = [self.swap(held[z], m) for z, m in list(enumerate(inner))[1:]]
+        arriving[0], beside = lax.optimization_barrier((arriving[0], beside))
+        return add_low(held[0], arriving), beside
 
     def view(self, held):
         pieces, rows, width = held.shape
@@ -416,7 +425,7 @@
     n2_ref[...] = (xhat * vec_ref[2:3, :] + vec_ref[3:4, :]).astype(BF16)
 
 
-def project_out(att, tokens, wo_pieces, at, vecs, rows_block=256):
+def project_out(att, tokens, wo_pieces, at, vecs, rows_block=512):
     rows, width = tokens.shape
     pieces = wo_pieces.shape[0]
     block = pl.BlockSpec((rows_block, width), lambda r: (r, 0))
@@ -446,21 +455,19 @@
     return jnp.where(at - seq * maxlen < lengths_ref[seq], cot, 0.0)
 
 
-def mlp_kernel(maxlen, units, len_ref, me_ref, n2_ref, res_ref, cot_ref, w_ref, out_ref, gn_ref, *rest):
-    *gw_refs, gl_s, acc_s = rest
+def mlp_kernel(units, me_ref, n2_ref, gl_ref, w_ref, res_ref, out_ref, gn_ref, *rest):
+    *gw_refs, acc_s, res_s, sem = rest
     step = pl.program_id(0)
     rows, width = n2_ref.shape
 
     @pl.when(step == 0)
     def _():
-        for first in range(0, rows, maxlen):
-            at = slice(first, first + maxlen)
-            gl_s[at, :] = live_grad(cot_ref[at, :], len_ref, maxlen, first).astype(BF16)
+        pltpu.make_async_copy(res_ref, res_s, sem).start()
 
     pieces = w_ref.shape[0]
     wu = w_ref[:, :units, :].reshape(pieces * units, width)
     wd = w_ref[:, units : 2 * units, :].reshape(pieces * units, width)
-    n2, gl = n2_ref[...], gl_s[...]
+    n2, gl = n2_ref[...], gl_ref[...]
     u = mm_nt(n2, wu)
     uu = u * u
     th = jnp.tanh(u * (GELU_A + GELU_B * uu))
@@ -473,7 +480,7 @@
 
     @pl.when(step == 0)
     def _():
-        acc_s[...] = out + res_ref[...]
+        acc_s[...] = out
         gn_ref[...] = gn
 
     @pl.when(step > 0)
@@ -500,10 +507,11 @@
 
     @pl.when(step == pl.num_programs(0) - 1)
     def _():
-        out_ref[...] = acc_s[...].astype(BF16)
-
-
-def feed_forward(lengths, me, n2, residual, cot, w, units, split):
+        pltpu.make_async_copy(res_ref, res_s, sem).wait()
+        out_ref[...] = (acc_s[...] + res_s[...]).astype(BF16)
+
+
+def feed_forward(me, n2, residual, gl, w, units, split):
     rows, width = n2.shape
     pieces, held, _ = w.shape
     take = max(1, 768 // units)
@@ -511,20 +519,23 @@
     outs = 2 if split else 1
     grads = [pl.BlockSpec((take // outs, 2 * units, width), lambda f, *_: (f, 0, 0))] * outs
     return pl.pallas_call(
-        functools.partial(mlp_kernel, rows // lengths.shape[0], units),
+        functools.partial(mlp_kernel, units),
         grid_spec=pltpu.PrefetchScalarGridSpec(
-            num_scalar_prefetch=2,
+            num_scalar_prefetch=1,
             grid=(pieces // take,),
-            in_specs=[full(), full(), full(), pl.BlockSpec((take, held, width), lambda f, *_: (f, 0, 0))],
+            in_specs=[
+                full(), full(), pl.BlockSpec((take, held, width), lambda f, *_: (f, 0, 0)),
+                pl.BlockSpec(memory_space=pl.ANY),
+            ],
             out_specs=[full(), full()] + grads,
-            scratch_shapes=[pltpu.VMEM((rows, width), BF16), pltpu.VMEM((rows, width), F32)],
+            scratch_shapes=[pltpu.VMEM((rows, width), F32)] * 2 + [pltpu.SemaphoreType.DMA],
         ),
         out_shape=[jax.ShapeDtypeStruct((rows, width), BF16), jax.ShapeDtypeStruct((rows, width), F32)]
         + [jax.ShapeDtypeStruct((pieces // outs, 2 * units, width), BF16)] * outs,
         compiler_params=params(),
         cost_estimate=cost(12 * rows * width * pieces * units, 40e6),
         name="feed_forward",
-    )(lengths, me, n2, residual, cot, w)
+    )(me, n2, gl, w, residual)
 
 
 def norm_back(grad, xhat, rinv, gain):
@@ -557,8 +568,9 @@
         gwo_ref[...] = mm_tn(att_ref[...], low_s[...]).astype(BF16)
 
 
-def middle_back(lengths, gn, residual, cot, att, wo, vecs, rows_block=256):
+def middle_back(lengths, gn, residual, cot, att, wo, vecs):
     rows, width = gn.shape
+    rows_block = rows // lengths.shape[0]
     block = pl.BlockSpec((rows_block, width), lambda r, *_: (r, 0))
     full = lambda shape: pl.BlockSpec(shape, lambda r, *_: (0,) * len(shape))
     return pl.pallas_call(
@@ -745,9 +757,13 @@
         w_ff = mlp_all[:, : 2 * units].reshape(n, 2, units, width).transpose(1, 0, 2, 3)
         w_ff = w_ff.reshape(2, ff // 768, 768, width).transpose(1, 0, 2, 3).reshape(ff // 768, 2 * 768, width)
 
+    maxlen = rows // seqs
+    live = (lax.iota(jnp.int32, maxlen)[None, :] < lengths[:, None]).reshape(rows, 1)
+    grad_low = jnp.where(live, cot, 0.0).astype(BF16)
     if plan.direct:
         flat = jnp.pad(vec_piece.reshape(1, -1), ((0, 7), (0, width - 4 * per)))
         gathered = plan.gather(jnp.concatenate([qkv_piece, flat], axis=0))
+        gathered, grad_low = lax.optimization_barrier((gathered, grad_low))
         slots = jnp.array(plan.slot_masks() + [m ^ 1 for m in plan.slot_masks()], jnp.int32)
         column = jnp.arange(width, dtype=jnp.int32)
         place = ((slots ^ me)[:, None] == (column // per)[None]).astype(F32)
@@ -762,7 +778,7 @@
 
     att, attT, inv, kept = attend_forward(mixed, lengths)
     residual, n2, wo = project_out(att, tokens, wo_pieces, wo_at, vecs)
-    output, gn2, *gw_ff = feed_forward(lengths, me_arr, n2, residual, cot, w_ff, ff_units, plan.direct)
+    output, gn2, *gw_ff = feed_forward(me_arr, n2, residual, grad_low, w_ff, ff_units, plan.direct)
     if plan.direct:
         got = plan.swap(gw_ff[1], 1)
     else:
@@ -790,9 +806,9 @@
         again, q_keep, q_send = lax.optimization_barrier((again, q_keep, q_send))
         whole, q_keep = lax.optimization_barrier((plan.last_sum(keep, got, back, again), q_keep))
         g_ff = plan.along_sum(whole)
-        summed = plan.scatter_first(q_keep, q_send)
+        summed = plan.scatter_first(q_keep, q_send, 48)
         gres, summed = lax.optimization_barrier((gres, summed))
-        g_attn, g_ff = plan.scatter_rest(summed, g_ff)
+        g_attn, g_ff = plan.scatter_rest(*summed, g_ff)
         g_attn = g_attn.astype(F32)
         g_qkv, g_out = g_attn[:ppr], g_attn[ppr : ppr + per]
         g_vec = g_attn[ppr + per, : 4 * per].reshape(4, per)

time: 296 us -> 289 us (0.976)
  waiting for transfers between devices: 78.5 us -> 67.4 us
  local copies, waits for them, and re-layouts: 4.59 us -> 7.91 us
  other arithmetic: 18.8 us -> 21.9 us
  Pallas kernels: 154 us -> 151 us
    ppermute x19 -> x20, waiting for transfers between devices: 76.6 us -> 66 us  [swap(): return lax.ppermute(value, AXES, [(i, i ^ mask) for i in range(self.n)])]
    unnamed x15 -> x17, local copies, waits for them, and re-layouts: 0.12 us -> 3.62 us
    convert_element_type x6 -> x11, other arithmetic: 11.3 us -> 13.2 us  [add_low(): return total.astype(first.dtype)]
    ppermute x19 -> x20, starting transfers between devices: 20.9 us -> 21.5 us  [swap(): return lax.ppermute(value, AXES, [(i, i ^ mask) for i in range(self.n)])]
  transfers between devices with their start and end apart: 21 -> 22, of which waited for: 16 -> 15; matrix products, arithmetic and copies ran while one was open for 3% -> 6% of each run, Pallas kernels for 36% -> 36%
where the time goes in v4:
time: 289 us; the launch traced here: 285 us
  Pallas kernels  151 us (52%)
  waiting for transfers between devices  67.4 us (23%)
  other arithmetic  21.9 us (8%)
  starting transfers between devices  21.5 us (7%)
  between operations  15.2 us (5%)
  local copies, waits for them, and re-layouts  7.91 us (3%)
    ppermute x20, waiting for transfers between devices, swap(): return lax.ppermute(value, AXES, [(i, i ^ mask) for i in range(self.n)])  66 us
    pallas_call x1, Pallas kernels, feed_forward(): pl.pallas_call(functools.partial(mlp_kernel, units), grid_spec=pltpu.Pref...  41.7 us
    pallas_call x1, Pallas kernels, attend_forward(): pl.pallas_call(functools.partial(attend_kernel, maxlen), grid_spec=pltpu....  32 us
    pallas_call x2, Pallas kernels, attend_backward(): pl.pallas_call(functools.partial(attend_back_kernel, maxlen), grid=(seqs,...  29.9 us
    ppermute x20, starting transfers between devices, swap(): return lax.ppermute(value, AXES, [(i, i ^ mask) for i in range(self.n)])  21.5 us
    convert_element_type x11, other arithmetic, add_low(): return total.astype(first.dtype)  13.2 us
    pallas_call x1, Pallas kernels, qkv_grad(): pl.pallas_call(functools.partial(qkv_grad_kernel, masks, ppr, opr), grid_...  11.4 us
    pallas_call x1, Pallas kernels, first_back(): pl.pallas_call(first_kernel, grid=(rows // rows_block,), in_specs=[pl.Blo...  10.6 us
  transfers between devices with their start and end apart: 22, of which 15 were waited for; matrix products, arithmetic and copies ran while one was open for 6% of the time, Pallas kernels for 36%

profile of v4, /device:TPU:0, one launch (start us, length us, event | category | flops | bytes accessed | tf_op | source)
XLA Modules:
  0.0 284.8 jit_solution(15225778525922019456)
XLA Ops:
  10.8 5.1 %collective-permute-start.2 = (bf16[1,80,768]{2,1,0:T(8,128)(2,1)S(1)}, bf16[1,80,768]{2,1,0:T(8,128)(2,1)S(1)}, u32[]{:S(2)}, u32[]{:S(2)}) collective-permute-start(bf16[1,80,768]{2,1,0:T(8,128)(2,1)S(1)} %fusion.31), channel_id=1, source_target_pairs={{0,24},{1,25},{2,26},{3,27},{4,28},{5,29},{6,30},{7,31},{8,16},{9,... | collective-permute-start | bytes 368648 | tf_op jit(solution)/shard_map/ppermute | solution.py:72
  16.5 3.6 %collective-permute-done.2 = bf16[1,80,768]{2,1,0:T(8,128)(2,1)S(1)} collective-permute-done((bf16[1,80,768]{2,1,0:T(8,128)(2,1)S(1)}, bf16[1,80,768]{2,1,0:T(8,128)(2,1)S(1)}, u32[]{:S(2)}, u32[]{:S(2)}) %collective-permute-start.2) | collective-permute-done | bytes 122912 | tf_op jit(solution)/shard_map/ppermute | solution.py:72
  20.1 6.2 %collective-permute-done.1 = bf16[1,80,768]{2,1,0:T(8,128)(2,1)S(1)} collective-permute-done((bf16[1,80,768]{2,1,0:T(8,128)(2,1)S(1)}, bf16[1,80,768]{2,1,0:T(8,128)(2,1)S(1)}, u32[]{:S(2)}, u32[]{:S(2)}) %collective-permute-start.1) | collective-permute-done | bytes 122912 | tf_op jit(solution)/shard_map/ppermute | solution.py:72
  33.3 6.4 %collective-permute-done.3 = bf16[4,80,768]{2,1,0:T(8,128)(2,1)S(1)} collective-permute-done((bf16[4,80,768]{2,1,0:T(8,128)(2,1)S(1)}, bf16[4,80,768]{2,1,0:T(8,128)(2,1)S(1)}, u32[]{:S(2)}, u32[]{:S(2)}) %collective-permute-start.3) | collective-permute-done | bytes 491552 | tf_op jit(solution)/shard_map/ppermute | solution.py:72
  42.9 16.0 %collective-permute-done.5 = bf16[4,80,768]{2,1,0:T(8,128)(2,1)S(1)} collective-permute-done((bf16[4,80,768]{2,1,0:T(8,128)(2,1)S(1)}, bf16[4,80,768]{2,1,0:T(8,128)(2,1)S(1)}, u32[]{:S(2)}, u32[]{:S(2)}) %collective-permute-start.5) | collective-permute-done | bytes 491552 | tf_op jit(solution)/shard_map/ppermute | solution.py:72
  64.1 10.0 %qkv_project.1 = (bf16[1024,2304]{1,0:T(8,128)(2,1)}, bf16[1024,768]{1,0:T(8,128)(2,1)}, bf16[2304,768]{1,0:T(8,128)(2,1)}, f32[8,768]{1,0:T(8,128)}) custom-call(s32[1]{0:T(128)} %bitcast.me_ref, bf16[1024,768]{1,0:T(8,128)(2,1)} %x_ref.5, bf16[16,80,768]{2,1,0:T(8,128)(2,1)} %constant_dynamic-update-slice_fusion.own_ref, ...), custom_call_target="tpu_custom_call" | custom-call | flops 3623878656 | bytes 20000000 | tf_op jit(solution)/shard_map/qkv_project/pallas_call | solution.py:176
  74.0 32.0 %attend_forward.1 = (bf16[1024,768]{1,0:T(8,128)(2,1)}, bf16[768,1024]{1,0:T(8,128)(2,1)}, f32[6,8,1024]{2,1,0:T(8,128)}, bf16[6,2,3,10,256,256]{5,4,3,2,1,0:T(8,128)(2,1)}) custom-call(s32[1]{0:T(128)} %copy.56.len_ref, bf16[1024,2304]{1,0:T(8,128)(2,1)} %get-tuple-element.64.q_ref.k_ref.v_ref, bf16[1024,2304]{1,0:T(8,128)(2,1)} %get-tuple-element.64.q_ref.k_ref.v_ref, ...), custom_call_target="tpu_custom_call" | custom-call | flops 20000000000 | bytes 60000000 | tf_op jit(solution)/shard_map/attend_forward/pallas_call | solution.py:308
  107.4 5.3 %project_out.1 = (f32[1024,768]{1,0:T(8,128)}, bf16[1024,768]{1,0:T(8,128)(2,1)}, bf16[768,768]{1,0:T(8,128)(2,1)}) custom-call(bf16[1024,768]{1,0:T(8,128)(2,1)} %get-tuple-element.65.att_ref, bf16[1024,768]{1,0:T(8,128)(2,1)} %x_ref.5, bf16[32,216,768]{2,1,0:T(8,128)(2,1)} %bitcast.120, f32[8,768]{1,0:T(8,128)} %get-tuple-element.66.vec_ref.refs_7_), custom_call_target="tpu_custom_call" | custom-call | flops 1207959552 | bytes 10000000 | tf_op jit(solution)/shard_map/project_out/pallas_call | solution.py:433
  112.7 41.7 %feed_forward.1 = (bf16[1024,768]{1,0:T(8,128)(2,1)}, f32[1024,768]{1,0:T(8,128)}, bf16[16,192,768]{2,1,0:T(8,128)(2,1)}, bf16[16,192,768]{2,1,0:T(8,128)(2,1)}) custom-call(s32[1]{0:T(128)} %bitcast.me_ref, bf16[1024,768]{1,0:T(8,128)(2,1)} %get-tuple-element.67.n2_ref, bf16[1024,768]{1,0:T(8,128)(2,1)} %select_convert_fusion.gl_ref, ...), custom_call_target="tpu_custom_call" | custom-call | flops 28991029248 | bytes 40000000 | tf_op jit(solution)/shard_map/feed_forward/pallas_call | solution.py:521
  154.7 10.0 %middle_back.1 = (f32[1024,768]{1,0:T(8,128)}, bf16[1024,768]{1,0:T(8,128)(2,1)}, bf16[768,768]{1,0:T(8,128)(2,1)}, f32[8,768]{1,0:T(8,128)}) custom-call(s32[1]{0:T(128)} %copy.56.len_ref, f32[1024,768]{1,0:T(8,128)} %get-tuple-element.71.gn_ref, f32[1024,768]{1,0:T(8,128)} %get-tuple-element.69.res_ref, f32[1024,768]{1,0:T(8,128)} %cot_ref.1, ...), custom_call_target="tpu_custom_call" | custom-call | flops 2415919104 | bytes 30000000 | tf_op jit(solution)/shard_map/middle_back/pallas_call | solution.py:576
  166.3 2.6 fusion
  171.4 22.1 %attend_backward.2 = (bf16[3,1024,640]{2,1,0:T(8,128)(2,1)}, f32[1,8,640]{2,1,0:T(8,128)}) custom-call(bf16[1024,2304]{1,0:T(8,128)(2,1)} %get-tuple-element.64.q_ref.k_ref.v_ref, bf16[1024,2304]{1,0:T(8,128)(2,1)} %get-tuple-element.64.q_ref.k_ref.v_ref, bf16[1024,2304]{1,0:T(8,128)(2,1)} %get-tuple-element.64.q_ref.k_ref.v_ref, ...), custom_call_target="tpu_custom_call" | custom-call | flops 24999999488 | bytes 50000000 | tf_op jit(solution)/shard_map/attend_backward/pallas_call | solution.py:390
  193.5 3.8 %collective-permute-done.8 = bf16[4,2,96,768]{3,2,0,1:T(8,128)(2,1)S(1)} collective-permute-done((bf16[4,2,96,768]{3,2,0,1:T(8,128)(2,1)}, bf16[4,2,96,768]{3,2,0,1:T(8,128)(2,1)S(1)}, u32[]{:S(2)}, u32[]{:S(2)}) %collective-permute-start.8) | collective-permute-done | bytes 1179680 | tf_op jit(solution)/shard_map/ppermute | solution.py:72
  198.2 2.7 fusion.6
  202.9 7.8 %attend_backward.3 = (bf16[3,1024,128]{2,1,0:T(8,128)(2,1)}, f32[1,8,128]{2,1,0:T(8,128)}) custom-call(bf16[1024,2304]{1,0:T(8,128)(2,1)} %get-tuple-element.64.q_ref.k_ref.v_ref, bf16[1024,2304]{1,0:T(8,128)(2,1)} %get-tuple-element.64.q_ref.k_ref.v_ref, bf16[1024,2304]{1,0:T(8,128)(2,1)} %get-tuple-element.64.q_ref.k_ref.v_ref, ...), custom_call_target="tpu_custom_call" | custom-call | flops 5000000000 | bytes 10000000 | tf_op jit(solution)/shard_map/attend_backward/pallas_call | solution.py:390
  210.7 11.4 %qkv_grad.1 = (bf16[16,104,768]{2,1,0:T(8,128)(2,1)}, bf16[16,104,768]{2,1,0:T(8,128)(2,1)}) custom-call(s32[1]{0:T(128)} %bitcast.me_ref, bf16[3,1024,640]{2,1,0:T(8,128)(2,1)} %get-tuple-element.85.refs_0_.d1_ref, bf16[3,1024,128]{2,1,0:T(8,128)(2,1)} %get-tuple-element.90.refs_1_.d2_ref, f32[1,8,640]{2,1,0:T(8,128)} %get-tuple-element.93.refs_2_, ...), custom_call_target="tpu_custom_call" | custom-call | flops 3623878656 | bytes 25000000 | tf_op jit(solution)/shard_map/qkv_grad/pallas_call | solution.py:661
  222.2 1.8 fusion.5
  225.2 2.2 collective-permute-done.12
  233.5 13.3 %collective-permute-done.13 = bf16[2,4,48,768]{3,2,1,0:T(8,128)(2,1)S(1)} collective-permute-done((bf16[2,4,48,768]{3,2,1,0:T(8,128)(2,1)S(1)}, bf16[2,4,48,768]{3,2,1,0:T(8,128)(2,1)S(1)}, u32[]{:S(2)}, u32[]{:S(2)}) %collective-permute-start.13) | collective-permute-done | bytes 589856 | tf_op jit(solution)/shard_map/ppermute | solution.py:72
  247.5 2.8 collective-permute-done.15
  251.4 4.6 %collective-permute-done.14 = bf16[4,48,768]{2,1,0:T(8,128)(2,1)S(1)} collective-permute-done((bf16[4,48,768]{2,1,0:T(8,128)(2,1)S(1)}, bf16[4,48,768]{2,1,0:T(8,128)(2,1)S(1)}, u32[]{:S(2)}, u32[]{:S(2)}) %collective-permute-start.14) | collective-permute-done | bytes 294944 | tf_op jit(solution)/shard_map/ppermute | solution.py:72
  256.2 2.8 collective-permute-done.16
  260.0 2.0 collective-permute-start.19
  262.7 10.6 %first_back.1 = (f32[1024,768]{1,0:T(8,128)}, f32[8,768]{1,0:T(8,128)}) custom-call(bf16[3,1024,640]{2,1,0:T(8,128)(2,1)} %get-tuple-element.85.refs_0_.d1_ref, bf16[3,1024,128]{2,1,0:T(8,128)(2,1)} %get-tuple-element.90.refs_1_.d2_ref, bf16[2304,768]{1,0:T(8,128)(2,1)} %get-tuple-element.91.refs_5_.w_ref, bf16[1024,768]{1,0:T(8,128)(2,1)} %x_ref.5, ...), custom_call_target="tpu_custom_call" | custom-call | flops 3623878656 | bytes 25000000 | tf_op jit(solution)/shard_map/first_back/pallas_call | solution.py:725
  (87 shorter events, 42.8 us)
Async XLA Ops:
  7.2 22.3 %copy-start.4 = (bf16[768,72]{0,1:T(8,128)(2,1)S(1)}, bf16[768,72]{0,1:T(8,128)(2,1)}, u32[]{:S(2)}) copy-start(bf16[768,72]{0,1:T(8,128)(2,1)} %param.16) | copy-start | bytes 331780
  7.2 100.2 %all-gather.2.cloned.1.call-start = ((), (), s32[]{:S(2)}) async-start(), calls=%async_computation.1 | async-start | bytes 10948608 | tf_op jit(solution)/shard_map/all_gather | solution.py:751
  9.0 264.2 %reduce-scatter.2.cloned.1.call-start = ((), (), s32[]{:S(2)}) async-start(), calls=%async_computation.2 | async-start | bytes 1474560 | tf_op jit(solution)/shard_map/reduce_scatter | solution.py:127
  10.8 9.4 %collective-permute-start.2 = (bf16[1,80,768]{2,1,0:T(8,128)(2,1)S(1)}, bf16[1,80,768]{2,1,0:T(8,128)(2,1)S(1)}, u32[]{:S(2)}, u32[]{:S(2)}) collective-permute-start(bf16[1,80,768]{2,1,0:T(8,128)(2,1)S(1)} %fusion.31), channel_id=1, source_target_pairs={{0,24},{1,25},{2,26},{3,27},{4,28},{5,29},{6,30},{7,31},{8,16},{9,... | collective-permute-start | bytes 368648 | tf_op jit(solution)/shard_map/ppermute | solution.py:72
  15.9 10.4 %collective-permute-start.1 = (bf16[1,80,768]{2,1,0:T(8,128)(2,1)S(1)}, bf16[1,80,768]{2,1,0:T(8,128)(2,1)S(1)}, u32[]{:S(2)}, u32[]{:S(2)}) collective-permute-start(bf16[1,80,768]{2,1,0:T(8,128)(2,1)S(1)} %fusion.31), channel_id=1, source_target_pairs={{0,16},{1,17},{2,18},{3,19},{4,20},{5,21},{6,22},{7,23},{8,24},{9,... | collective-permute-start | bytes 368648 | tf_op jit(solution)/shard_map/ppermute | solution.py:72
  15.9 10.4 %collective-permute-start = (bf16[1,80,768]{2,1,0:T(8,128)(2,1)S(1)}, bf16[1,80,768]{2,1,0:T(8,128)(2,1)S(1)}, u32[]{:S(2)}, u32[]{:S(2)}) collective-permute-start(bf16[1,80,768]{2,1,0:T(8,128)(2,1)S(1)} %fusion.31), channel_id=1, source_target_pairs={{0,8},{1,9},{2,10},{3,11},{4,12},{5,13},{6,14},{7,15},{8,0},{9,1},... | collective-permute-start | bytes 368648 | tf_op jit(solution)/shard_map/ppermute | solution.py:72
  26.4 13.3 %collective-permute-start.3 = (bf16[4,80,768]{2,1,0:T(8,128)(2,1)S(1)}, bf16[4,80,768]{2,1,0:T(8,128)(2,1)S(1)}, u32[]{:S(2)}, u32[]{:S(2)}) collective-permute-start(bf16[4,80,768]{2,1,0:T(8,128)(2,1)S(1)} %pad_maximum_fusion.1), channel_id=1, source_target_pairs={{0,2},{1,3},{2,0},{3,1},{4,6},{5,7},{6,4},{7,5},{8,10},{9,11},{10,... | collective-permute-start | bytes 1474568 | tf_op jit(solution)/shard_map/ppermute | solution.py:72
  28.0 14.2 %collective-permute-start.4 = (bf16[4,80,768]{2,1,0:T(8,128)(2,1)S(1)}, bf16[4,80,768]{2,1,0:T(8,128)(2,1)S(1)}, u32[]{:S(2)}, u32[]{:S(2)}) collective-permute-start(bf16[4,80,768]{2,1,0:T(8,128)(2,1)S(1)} %pad_maximum_fusion.1), channel_id=1, source_target_pairs={{0,4},{1,5},{2,6},{3,7},{4,0},{5,1},{6,2},{7,3},{8,12},{9,13},{10,... | collective-permute-start | bytes 1474568 | tf_op jit(solution)/shard_map/ppermute | solution.py:72
  30.8 28.1 %collective-permute-start.5 = (bf16[4,80,768]{2,1,0:T(8,128)(2,1)S(1)}, bf16[4,80,768]{2,1,0:T(8,128)(2,1)S(1)}, u32[]{:S(2)}, u32[]{:S(2)}) collective-permute-start(bf16[4,80,768]{2,1,0:T(8,128)(2,1)S(1)} %pad_maximum_fusion.1), channel_id=1, source_target_pairs={{0,6},{1,7},{2,4},{3,5},{4,2},{5,3},{6,0},{7,1},{8,14},{9,15},{10,... | collective-permute-start | bytes 1474568 | tf_op jit(solution)/shard_map/ppermute | solution.py:72
  40.5 20.5 %copy-start.5 = (s32[32]{0:T(128)S(1)}, s32[32]{0:T(128)}, u32[]{:S(2)}) copy-start(s32[32]{0:T(128)} %constant.52.clone) | copy-start | bytes 388
  59.7 4.3 %collective-permute-start.6 = (bf16[16,80,768]{2,1,0:T(8,128)(2,1)}, bf16[16,80,768]{2,1,0:T(8,128)(2,1)}, u32[]{:S(2)}, u32[]{:S(2)}) collective-permute-start(bf16[16,80,768]{2,1,0:T(8,128)(2,1)} %constant_dynamic-update-slice_fusion.own_ref), channel_id=1, source_target_pairs={{0,1},{1,0},{2,3},{3,2},{4,5},{5,4},{6,7},{7,6},{8,9},{9,8},{10,11... | collective-permute-start | bytes 5898248 | tf_op jit(solution)/shard_map/ppermute | solution.py:72
  154.4 10.3 %collective-permute-start.7 = (bf16[16,192,768]{2,1,0:T(8,128)(2,1)}, bf16[16,192,768]{2,1,0:T(8,128)(2,1)}, u32[]{:S(2)}, u32[]{:S(2)}) collective-permute-start(bf16[16,192,768]{2,1,0:T(8,128)(2,1)} %get-tuple-element.74), channel_id=1, source_target_pairs={{0,1},{1,0},{2,3},{3,2},{4,5},{5,4},{6,7},{7,6},{8,9},{9,8},{10,11... | collective-permute-start | bytes 14155784 | tf_op jit(solution)/shard_map/ppermute | solution.py:72
  168.9 28.4 %collective-permute-start.8 = (bf16[4,2,96,768]{3,2,0,1:T(8,128)(2,1)}, bf16[4,2,96,768]{3,2,0,1:T(8,128)(2,1)S(1)}, u32[]{:S(2)}, u32[]{:S(2)}) collective-permute-start(bf16[4,2,96,768]{3,2,0,1:T(8,128)(2,1)} %fusion), channel_id=1, source_target_pairs={{0,2},{1,3},{2,0},{3,1},{4,6},{5,7},{6,4},{7,5},{8,10},{9,11},{10,... | collective-permute-start | bytes 3538952 | tf_op jit(solution)/shard_map/ppermute | solution.py:72
  170.4 27.9 %collective-permute-start.9 = (bf16[4,2,96,768]{3,2,0,1:T(8,128)(2,1)S(1)}, bf16[4,2,96,768]{3,2,0,1:T(8,128)(2,1)S(1)}, u32[]{:S(2)}, u32[]{:S(2)}) collective-permute-start(bf16[4,2,96,768]{3,2,0,1:T(8,128)(2,1)S(1)} %fusion.1), channel_id=1, source_target_pairs={{0,4},{1,5},{2,6},{3,7},{4,0},{5,1},{6,2},{7,3},{8,12},{9,13},{10,... | collective-permute-start | bytes 3538952 | tf_op jit(solution)/shard_map/ppermute | solution.py:72
  201.0 21.1 %collective-permute-start.11 = (bf16[4,96,768]{2,1,0:T(8,128)(2,1)}, bf16[4,96,768]{2,1,0:T(8,128)(2,1)S(1)}, u32[]{:S(2)}, u32[]{:S(2)}) collective-permute-start(bf16[4,96,768]{2,1,0:T(8,128)(2,1)} %get-tuple-element.116), channel_id=1, source_target_pairs={{0,2},{1,3},{2,0},{3,1},{4,6},{5,7},{6,4},{7,5},{8,10},{9,11},{10,... | collective-permute-start | bytes 1769480 | tf_op jit(solution)/shard_map/ppermute | solution.py:72
  201.5 20.6 %collective-permute-start.10 = (bf16[4,96,768]{2,1,0:T(8,128)(2,1)}, bf16[4,96,768]{2,1,0:T(8,128)(2,1)S(1)}, u32[]{:S(2)}, u32[]{:S(2)}) collective-permute-start(bf16[4,96,768]{2,1,0:T(8,128)(2,1)} %get-tuple-element.117), channel_id=1, source_target_pairs={{0,4},{1,5},{2,6},{3,7},{4,0},{5,1},{6,2},{7,3},{8,12},{9,13},{10,... | collective-permute-start | bytes 1769480 | tf_op jit(solution)/shard_map/ppermute | solution.py:72
  222.1 5.2 %collective-permute-start.12 = (bf16[16,104,768]{2,1,0:T(8,128)(2,1)}, bf16[16,104,768]{2,1,0:T(8,128)(2,1)}, u32[]{:S(2)}, u32[]{:S(2)}) collective-permute-start(bf16[16,104,768]{2,1,0:T(8,128)(2,1)} %get-tuple-element.104), channel_id=1, source_target_pairs={{0,1},{1,0},{2,3},{3,2},{4,5},{5,4},{6,7},{7,6},{8,9},{9,8},{10,11... | collective-permute-start | bytes 7667720 | tf_op jit(solution)/shard_map/ppermute | solution.py:72
  231.4 15.4 %collective-permute-start.13 = (bf16[2,4,48,768]{3,2,1,0:T(8,128)(2,1)S(1)}, bf16[2,4,48,768]{3,2,1,0:T(8,128)(2,1)S(1)}, u32[]{:S(2)}, u32[]{:S(2)}) collective-permute-start(bf16[2,4,48,768]{3,2,1,0:T(8,128)(2,1)S(1)} %fusion.12), channel_id=1, source_target_pairs={{0,2},{1,3},{2,0},{3,1},{4,6},{5,7},{6,4},{7,5},{8,10},{9,11},{10,... | collective-permute-start | bytes 1769480 | tf_op jit(solution)/shard_map/ppermute | solution.py:72
  232.5 17.8 %collective-permute-start.15 = (bf16[2,4,56,768]{3,2,1,0:T(8,128)(2,1)S(1)}, bf16[2,4,56,768]{3,2,1,0:T(8,128)(2,1)S(1)}, u32[]{:S(2)}, u32[]{:S(2)}) collective-permute-start(bf16[2,4,56,768]{3,2,1,0:T(8,128)(2,1)S(1)} %get-tuple-element.110), channel_id=1, source_target_pairs={{0,4},{1,5},{2,6},{3,7},{4,0},{5,1},{6,2},{7,3},{8,12},{9,13},{10,... | collective-permute-start | bytes 2064392 | tf_op jit(solution)/shard_map/ppermute | solution.py:72
  246.9 9.1 %collective-permute-start.14 = (bf16[4,48,768]{2,1,0:T(8,128)(2,1)S(1)}, bf16[4,48,768]{2,1,0:T(8,128)(2,1)S(1)}, u32[]{:S(2)}, u32[]{:S(2)}) collective-permute-start(bf16[4,48,768]{2,1,0:T(8,128)(2,1)S(1)} %fusion.20), channel_id=1, source_target_pairs={{0,4},{1,5},{2,6},{3,7},{4,0},{5,1},{6,2},{7,3},{8,12},{9,13},{10,... | collective-permute-start | bytes 884744 | tf_op jit(solution)/shard_map/ppermute | solution.py:72
  250.5 8.5 %collective-permute-start.16 = (bf16[4,56,768]{2,1,0:T(8,128)(2,1)S(1)}, bf16[4,56,768]{2,1,0:T(8,128)(2,1)S(1)}, u32[]{:S(2)}, u32[]{:S(2)}) collective-permute-start(bf16[4,56,768]{2,1,0:T(8,128)(2,1)S(1)} %fusion.15), channel_id=1, source_target_pairs={{0,2},{1,3},{2,0},{3,1},{4,6},{5,7},{6,4},{7,5},{8,10},{9,11},{10,... | collective-permute-start | bytes 1032200 | tf_op jit(solution)/shard_map/ppermute | solution.py:72
  259.1 14.2 %collective-permute-start.17 = (bf16[104,768]{1,0:T(8,128)(2,1)S(1)}, bf16[104,768]{1,0:T(8,128)(2,1)S(1)}, u32[]{:S(2)}, u32[]{:S(2)}) collective-permute-start(bf16[104,768]{1,0:T(8,128)(2,1)S(1)} %get-tuple-element.120), channel_id=1, source_target_pairs={{0,8},{1,9},{2,10},{3,11},{4,12},{5,13},{6,14},{7,15},{8,0},{9,1},... | collective-permute-start | bytes 479240 | tf_op jit(solution)/shard_map/ppermute | solution.py:72
  260.0 13.3 %collective-permute-start.19 = (bf16[104,768]{1,0:T(8,128)(2,1)S(1)}, bf16[104,768]{1,0:T(8,128)(2,1)S(1)}, u32[]{:S(2)}, u32[]{:S(2)}) collective-permute-start(bf16[104,768]{1,0:T(8,128)(2,1)S(1)} %get-tuple-element.121), channel_id=1, source_target_pairs={{0,24},{1,25},{2,26},{3,27},{4,28},{5,29},{6,30},{7,31},{8,16},{9,... | collective-permute-start | bytes 479240 | tf_op jit(solution)/shard_map/ppermute | solution.py:72
  262.0 12.2 %collective-permute-start.18 = (bf16[104,768]{1,0:T(8,128)(2,1)S(1)}, bf16[104,768]{1,0:T(8,128)(2,1)S(1)}, u32[]{:S(2)}, u32[]{:S(2)}) collective-permute-start(bf16[104,768]{1,0:T(8,128)(2,1)S(1)} %get-tuple-element.122), channel_id=1, source_target_pairs={{0,16},{1,17},{2,18},{3,19},{4,20},{5,21},{6,22},{7,23},{8,24},{9,... | collective-permute-start | bytes 479240 | tf_op jit(solution)/shard_map/ppermute | solution.py:72
  (4 other events, 35.9 us)
Sparse Core Ops, SparseCore 0:
  11.5 95.7 all-gather.1
  225.3 28.3 reduce-scatter.1

commit v5 on v4

--- a/solution.py
+++ b/solution.py
@@ -88,16 +88,18 @@
         two = [pair((x, every, every, tail)) for x in range(2)]
         return one, two
 
-    def scatter_rest(self, one, two, beside):
+    def scatter_rest(self, one, two, done, beside, late):
         inner = self.masks_of(self.along)
         arriving = self.swap(one[1], 2), self.swap(two[1], 4)
         stay = [add_low(own[0][0], [got[0]]) for own, got in ((one, arriving[0]), (two, arriving[1]))]
         goes = [add_low(own[0][1], [got[1]]) for own, got in ((one, arriving[0]), (two, arriving[1]))]
+        goes, done = lax.optimization_barrier((goes, done))
         got = self.swap(goes[0], 4), self.swap(goes[1], 2)
         held = jnp.concatenate([add_low(stay[0], [got[0]]), add_low(stay[1], [got[1]])], axis=1)
+        held, late = lax.optimization_barrier((held, late))
         arriving = [self.swap(held[z], m) for z, m in list(enumerate(inner))[1:]]
         arriving[0], beside = lax.optimization_barrier((arriving[0], beside))
-        return add_low(held[0], arriving), beside
+        return add_low(held[0], arriving), done, beside, late
 
     def view(self, held):
         pieces, rows, width = held.shape
@@ -455,14 +457,9 @@
     return jnp.where(at - seq * maxlen < lengths_ref[seq], cot, 0.0)
 
 
-def mlp_kernel(units, me_ref, n2_ref, gl_ref, w_ref, res_ref, out_ref, gn_ref, *rest):
-    *gw_refs, acc_s, res_s, sem = rest
+def mlp_kernel(units, me_ref, n2_ref, gl_ref, w_ref, act_ref, gn_ref, *gw_refs):
     step = pl.program_id(0)
     rows, width = n2_ref.shape
-
-    @pl.when(step == 0)
-    def _():
-        pltpu.make_async_copy(res_ref, res_s, sem).start()
 
     pieces = w_ref.shape[0]
     wu = w_ref[:, :units, :].reshape(pieces * units, width)
@@ -474,18 +471,16 @@
     half = 0.5 * u
     act = (half + half * th).astype(BF16)
     slope = 0.5 + 0.5 * th + (half - half * (th * th)) * (GELU_A + (3.0 * GELU_B) * uu)
+    act_ref[...] = act
     gp = (mm_nt(gl, wd) * slope).astype(BF16)
-    out = mm_nn(act, wd)
     gn = mm_nn(gp, wu)
 
     @pl.when(step == 0)
     def _():
-        acc_s[...] = out
         gn_ref[...] = gn
 
     @pl.when(step > 0)
     def _():
-        acc_s[...] += out
         gn_ref[...] += gn
 
     for at, grad in ((0, mm_tn(gp, n2)), (units, mm_tn(act, gl))):
@@ -505,13 +500,8 @@
                     gw_refs[0][slot, at : at + units, :] = grad[place, side]
                     gw_refs[1][slot, at : at + units, :] = grad[place, 1 - side]
 
-    @pl.when(step == pl.num_programs(0) - 1)
-    def _():
-        pltpu.make_async_copy(res_ref, res_s, sem).wait()
-        out_ref[...] = (acc_s[...] + res_s[...]).astype(BF16)
-
-
-def feed_forward(me, n2, residual, gl, w, units, split):
+
+def feed_forward(me, n2, gl, w, units, split):
     rows, width = n2.shape
     pieces, held, _ = w.shape
     take = max(1, 768 // units)
@@ -525,17 +515,54 @@
             grid=(pieces // take,),
             in_specs=[
                 full(), full(), pl.BlockSpec((take, held, width), lambda f, *_: (f, 0, 0)),
-                pl.BlockSpec(memory_space=pl.ANY),
             ],
-            out_specs=[full(), full()] + grads,
-            scratch_shapes=[pltpu.VMEM((rows, width), F32)] * 2 + [pltpu.SemaphoreType.DMA],
+            out_specs=[pl.BlockSpec((rows, take * units), lambda f, *_: (0, f)), full()] + grads,
         ),
-        out_shape=[jax.ShapeDtypeStruct((rows, width), BF16), jax.ShapeDtypeStruct((rows, width), F32)]
+        out_shape=[jax.ShapeDtypeStruct((rows, pieces * units), BF16), jax.ShapeDtypeStruct((rows, width), F32)]
         + [jax.ShapeDtypeStruct((pieces // outs, 2 * units, width), BF16)] * outs,
         compiler_params=params(),
-        cost_estimate=cost(12 * rows * width * pieces * units, 40e6),
+        cost_estimate=cost(10 * rows * width * pieces * units, 40e6),
         name="feed_forward",
-    )(me, n2, gl, w, residual)
+    )(me, n2, gl, w)
+
+
+def finish_kernel(units, act_ref, w_ref, res_ref, out_ref, acc_s):
+    step = pl.program_id(0)
+    pieces, _, width = w_ref.shape
+    part = mm_nn(act_ref[...], w_ref[:, units : 2 * units, :].reshape(pieces * units, width))
+
+    @pl.when(step == 0)
+    def _():
+        acc_s[...] = part + res_ref[...]
+
+    @pl.when(step > 0)
+    def _():
+        acc_s[...] += part
+
+    @pl.when(step == pl.num_programs(0) - 1)
+    def _():
+        out_ref[...] = acc_s[...].astype(BF16)
+
+
+def finish_output(act, w, residual, units):
+    rows, width = residual.shape
+    pieces, held, _ = w.shape
+    take = max(1, 768 // units)
+    full = lambda: pl.BlockSpec((rows, width), lambda f: (0, 0))
+    return pl.pallas_call(
+        functools.partial(finish_kernel, units),
+        grid=(pieces // take,),
+        in_specs=[
+            pl.BlockSpec((rows, take * units), lambda f: (0, f)),
+            pl.BlockSpec((take, held, width), lambda f: (f, 0, 0)), full(),
+        ],
+        out_specs=full(),
+        out_shape=jax.ShapeDtypeStruct((rows, width), BF16),
+        scratch_shapes=[pltpu.VMEM((rows, width), F32)],
+        compiler_params=params(),
+        cost_estimate=cost(2 * rows * width * pieces * units, 20e6),
+        name="finish_output",
+    )(act, w, residual)
 
 
 def norm_back(grad, xhat, rinv, gain):
@@ -778,7 +805,7 @@
 
     att, attT, inv, kept = attend_forward(mixed, lengths)
     residual, n2, wo = project_out(att, tokens, wo_pieces, wo_at, vecs)
-    output, gn2, *gw_ff = feed_forward(me_arr, n2, residual, grad_low, w_ff, ff_units, plan.direct)
+    act, gn2, *gw_ff = feed_forward(me_arr, n2, grad_low, w_ff, ff_units, plan.direct)
     if plan.direct:
         got = plan.swap(gw_ff[1], 1)
     else:
@@ -807,8 +834,9 @@
         whole, q_keep = lax.optimization_barrier((plan.last_sum(keep, got, back, again), q_keep))
         g_ff = plan.along_sum(whole)
         summed = plan.scatter_first(q_keep, q_send, 48)
-        gres, summed = lax.optimization_barrier((gres, summed))
-        g_attn, g_ff = plan.scatter_rest(*summed, g_ff)
+        act, summed = lax.optimization_barrier((act, summed))
+        output = finish_output(act, w_ff, residual, ff_units)
+        g_attn, output, g_ff, gres = plan.scatter_rest(*summed, output, g_ff, gres)
         g_attn = g_attn.astype(F32)
         g_qkv, g_out = g_attn[:ppr], g_attn[ppr : ppr + per]
         g_vec = g_attn[ppr + per, : 4 * per].reshape(4, per)
@@ -817,6 +845,7 @@
         g_out = lax.psum_scatter(gwo, AXES, scatter_dimension=0, tiled=True)
     gtok, gvec1 = first_back(grads, w_abs, tokens, gres, vecs)
     if not plan.direct:
+        output = finish_output(act, w_ff, residual, ff_units)
         gvec = jnp.concatenate([gvec1[:2], gvec2[:2]], axis=0)
         g_vec = lax.psum_scatter(gvec, AXES, scatter_dimension=1, tiled=True)
     g_ff = g_ff.astype(F32)

time: 289 us -> 287 us (level)
  waiting for transfers between devices: 67.4 us -> 55.5 us
  Pallas kernels: 151 us -> 157 us
  other arithmetic: 21.9 us -> 24.8 us
    ppermute x20, waiting for transfers between devices: 66 us -> 53.9 us  [swap(): return lax.ppermute(value, AXES, [(i, i ^ mask) for i in range(self.n)])]
    pallas_call x0 -> x1, Pallas kernels: none -> 12.1 us  [finish_output(): pl.pallas_call(functools.partial(finish_kernel, units), grid=(pieces // t...]
    pallas_call x1, Pallas kernels: 41.7 us -> 35.9 us  [feed_forward(): pl.pallas_call(functools.partial(mlp_kernel, units), grid_spec=pltpu.Pref...]
  transfers between devices with their start and end apart: 22 -> 22, of which waited for: 15 -> 15; matrix products, arithmetic and copies ran while one was open for 6% -> 5% of each run, Pallas kernels for 36% -> 41%
where the time goes in v5:
time: 287 us; the launch traced here: 283 us
  Pallas kernels  157 us (55%)
  waiting for transfers between devices  55.5 us (19%)
  other arithmetic  24.8 us (9%)
  starting transfers between devices  21.6 us (8%)
  between operations  15.1 us (5%)
  local copies, waits for them, and re-layouts  8.94 us (3%)
    ppermute x20, waiting for transfers between devices, swap(): return lax.ppermute(value, AXES, [(i, i ^ mask) for i in range(self.n)])  53.9 us
    pallas_call x1, Pallas kernels, feed_forward(): pl.pallas_call(functools.partial(mlp_kernel, units), grid_spec=pltpu.Pref...  35.9 us
    pallas_call x1, Pallas kernels, attend_forward(): pl.pallas_call(functools.partial(attend_kernel, maxlen), grid_spec=pltpu....  31.7 us
    pallas_call x2, Pallas kernels, attend_backward(): pl.pallas_call(functools.partial(attend_back_kernel, maxlen), grid=(seqs,...  30.3 us
    ppermute x20, starting transfers between devices, swap(): return lax.ppermute(value, AXES, [(i, i ^ mask) for i in range(self.n)])  21.6 us
    convert_element_type x11, other arithmetic, add_low(): return total.astype(first.dtype)  16 us
    pallas_call x1, Pallas kernels, finish_output(): pl.pallas_call(functools.partial(finish_kernel, units), grid=(pieces // t...  12.1 us
    pallas_call x1, Pallas kernels, qkv_grad(): pl.pallas_call(functools.partial(qkv_grad_kernel, masks, ppr, opr), grid_...  11.2 us
  transfers between devices with their start and end apart: 22, of which 15 were waited for; matrix products, arithmetic and copies ran while one was open for 5% of the time, Pallas kernels for 41%

profile of v5, /device:TPU:0, one launch (start us, length us, event | category | flops | bytes accessed | tf_op | source)
XLA Modules:
  0.0 283.2 jit_solution(11414481377514952732)
XLA Ops:
  10.8 5.1 %collective-permute-start.2 = (bf16[1,80,768]{2,1,0:T(8,128)(2,1)S(1)}, bf16[1,80,768]{2,1,0:T(8,128)(2,1)S(1)}, u32[]{:S(2)}, u32[]{:S(2)}) collective-permute-start(bf16[1,80,768]{2,1,0:T(8,128)(2,1)S(1)} %fusion.24), channel_id=1, source_target_pairs={{0,24},{1,25},{2,26},{3,27},{4,28},{5,29},{6,30},{7,31},{8,16},{9,... | collective-permute-start | bytes 368648 | tf_op jit(solution)/shard_map/ppermute | solution.py:72
  16.5 3.6 %collective-permute-done.2 = bf16[1,80,768]{2,1,0:T(8,128)(2,1)S(1)} collective-permute-done((bf16[1,80,768]{2,1,0:T(8,128)(2,1)S(1)}, bf16[1,80,768]{2,1,0:T(8,128)(2,1)S(1)}, u32[]{:S(2)}, u32[]{:S(2)}) %collective-permute-start.2) | collective-permute-done | bytes 122912 | tf_op jit(solution)/shard_map/ppermute | solution.py:72
  20.1 6.3 %collective-permute-done.1 = bf16[1,80,768]{2,1,0:T(8,128)(2,1)S(1)} collective-permute-done((bf16[1,80,768]{2,1,0:T(8,128)(2,1)S(1)}, bf16[1,80,768]{2,1,0:T(8,128)(2,1)S(1)}, u32[]{:S(2)}, u32[]{:S(2)}) %collective-permute-start.1) | collective-permute-done | bytes 122912 | tf_op jit(solution)/shard_map/ppermute | solution.py:72
  33.4 6.4 %collective-permute-done.3 = bf16[4,80,768]{2,1,0:T(8,128)(2,1)S(1)} collective-permute-done((bf16[4,80,768]{2,1,0:T(8,128)(2,1)S(1)}, bf16[4,80,768]{2,1,0:T(8,128)(2,1)S(1)}, u32[]{:S(2)}, u32[]{:S(2)}) %collective-permute-start.3) | collective-permute-done | bytes 491552 | tf_op jit(solution)/shard_map/ppermute | solution.py:72
  43.1 15.8 %collective-permute-done.5 = bf16[4,80,768]{2,1,0:T(8,128)(2,1)S(1)} collective-permute-done((bf16[4,80,768]{2,1,0:T(8,128)(2,1)S(1)}, bf16[4,80,768]{2,1,0:T(8,128)(2,1)S(1)}, u32[]{:S(2)}, u32[]{:S(2)}) %collective-permute-start.5) | collective-permute-done | bytes 491552 | tf_op jit(solution)/shard_map/ppermute | solution.py:72
  64.1 10.0 %qkv_project.1 = (bf16[1024,2304]{1,0:T(8,128)(2,1)}, bf16[1024,768]{1,0:T(8,128)(2,1)}, bf16[2304,768]{1,0:T(8,128)(2,1)}, f32[8,768]{1,0:T(8,128)}) custom-call(s32[1]{0:T(128)} %bitcast.me_ref, bf16[1024,768]{1,0:T(8,128)(2,1)} %x_ref.5, bf16[16,80,768]{2,1,0:T(8,128)(2,1)} %constant_dynamic-update-slice_fusion.own_ref, ...), custom_call_target="tpu_custom_call" | custom-call | flops 3623878656 | bytes 20000000 | tf_op jit(solution)/shard_map/qkv_project/pallas_call | solution.py:178
  74.0 31.7 %attend_forward.1 = (bf16[1024,768]{1,0:T(8,128)(2,1)}, bf16[768,1024]{1,0:T(8,128)(2,1)}, f32[6,8,1024]{2,1,0:T(8,128)}, bf16[6,2,3,10,256,256]{5,4,3,2,1,0:T(8,128)(2,1)}) custom-call(s32[1]{0:T(128)} %copy.56.len_ref, bf16[1024,2304]{1,0:T(8,128)(2,1)} %get-tuple-element.69.q_ref.k_ref.v_ref, bf16[1024,2304]{1,0:T(8,128)(2,1)} %get-tuple-element.69.q_ref.k_ref.v_ref, ...), custom_call_target="tpu_custom_call" | custom-call | flops 20000000000 | bytes 60000000 | tf_op jit(solution)/shard_map/attend_forward/pallas_call | solution.py:310
  107.4 5.3 %project_out.1 = (f32[1024,768]{1,0:T(8,128)}, bf16[1024,768]{1,0:T(8,128)(2,1)}, bf16[768,768]{1,0:T(8,128)(2,1)}) custom-call(bf16[1024,768]{1,0:T(8,128)(2,1)} %get-tuple-element.70.att_ref, bf16[1024,768]{1,0:T(8,128)(2,1)} %x_ref.5, bf16[32,216,768]{2,1,0:T(8,128)(2,1)} %bitcast.118, f32[8,768]{1,0:T(8,128)} %get-tuple-element.71.vec_ref.refs_7_), custom_call_target="tpu_custom_call" | custom-call | flops 1207959552 | bytes 10000000 | tf_op jit(solution)/shard_map/project_out/pallas_call | solution.py:435
  112.7 35.9 %feed_forward.1 = (bf16[1024,3072]{1,0:T(8,128)(2,1)}, f32[1024,768]{1,0:T(8,128)}, bf16[16,192,768]{2,1,0:T(8,128)(2,1)}, bf16[16,192,768]{2,1,0:T(8,128)(2,1)}) custom-call(s32[1]{0:T(128)} %bitcast.me_ref, bf16[1024,768]{1,0:T(8,128)(2,1)} %get-tuple-element.72.n2_ref, bf16[1024,768]{1,0:T(8,128)(2,1)} %select_convert_fusion.gl_ref, ...), custom_call_target="tpu_custom_call" | custom-call | flops 24159191040 | bytes 40000000 | tf_op jit(solution)/shard_map/feed_forward/pallas_call | solution.py:511
  148.9 10.0 %middle_back.1 = (f32[1024,768]{1,0:T(8,128)}, bf16[1024,768]{1,0:T(8,128)(2,1)}, bf16[768,768]{1,0:T(8,128)(2,1)}, f32[8,768]{1,0:T(8,128)}) custom-call(s32[1]{0:T(128)} %copy.56.len_ref, f32[1024,768]{1,0:T(8,128)} %get-tuple-element.75.gn_ref, f32[1024,768]{1,0:T(8,128)} %get-tuple-element.76.res_ref, f32[1024,768]{1,0:T(8,128)} %cot_ref.1, ...), custom_call_target="tpu_custom_call" | custom-call | flops 2415919104 | bytes 30000000 | tf_op jit(solution)/shard_map/middle_back/pallas_call | solution.py:603
  160.5 2.7 fusion.1
  165.2 22.6 %attend_backward.2 = (bf16[3,1024,640]{2,1,0:T(8,128)(2,1)}, f32[1,8,640]{2,1,0:T(8,128)}) custom-call(bf16[1024,2304]{1,0:T(8,128)(2,1)} %get-tuple-element.69.q_ref.k_ref.v_ref, bf16[1024,2304]{1,0:T(8,128)(2,1)} %get-tuple-element.69.q_ref.k_ref.v_ref, bf16[1024,2304]{1,0:T(8,128)(2,1)} %get-tuple-element.69.q_ref.k_ref.v_ref, ...), custom_call_target="tpu_custom_call" | custom-call | flops 24999999488 | bytes 50000000 | tf_op jit(solution)/shard_map/attend_backward/pallas_call | solution.py:392
  187.8 3.6 %collective-permute-done.9 = bf16[4,2,96,768]{3,2,0,1:T(8,128)(2,1)S(1)} collective-permute-done((bf16[4,2,96,768]{3,2,0,1:T(8,128)(2,1)}, bf16[4,2,96,768]{3,2,0,1:T(8,128)(2,1)S(1)}, u32[]{:S(2)}, u32[]{:S(2)}) %collective-permute-start.9) | collective-permute-done | bytes 1179680 | tf_op jit(solution)/shard_map/ppermute | solution.py:72
  192.4 2.1 fusion.4
  196.7 7.8 %attend_backward.3 = (bf16[3,1024,128]{2,1,0:T(8,128)(2,1)}, f32[1,8,128]{2,1,0:T(8,128)}) custom-call(bf16[1024,2304]{1,0:T(8,128)(2,1)} %get-tuple-element.69.q_ref.k_ref.v_ref, bf16[1024,2304]{1,0:T(8,128)(2,1)} %get-tuple-element.69.q_ref.k_ref.v_ref, bf16[1024,2304]{1,0:T(8,128)(2,1)} %get-tuple-element.69.q_ref.k_ref.v_ref, ...), custom_call_target="tpu_custom_call" | custom-call | flops 5000000000 | bytes 10000000 | tf_op jit(solution)/shard_map/attend_backward/pallas_call | solution.py:392
  204.4 11.2 %qkv_grad.1 = (bf16[16,104,768]{2,1,0:T(8,128)(2,1)}, bf16[16,104,768]{2,1,0:T(8,128)(2,1)}) custom-call(s32[1]{0:T(128)} %bitcast.me_ref, bf16[3,1024,640]{2,1,0:T(8,128)(2,1)} %get-tuple-element.92.refs_0_.d1_ref, bf16[3,1024,128]{2,1,0:T(8,128)(2,1)} %get-tuple-element.95.refs_1_.d2_ref, f32[1,8,640]{2,1,0:T(8,128)} %get-tuple-element.96.refs_2_, ...), custom_call_target="tpu_custom_call" | custom-call | flops 3623878656 | bytes 25000000 | tf_op jit(solution)/shard_map/qkv_grad/pallas_call | solution.py:688
  216.6 2.7 fusion.7
  221.8 2.0 fusion.12
  223.8 2.1 fusion.11
  225.9 2.5 fusion.9
  230.5 12.1 %finish_output.1 = bf16[1024,768]{1,0:T(8,128)(2,1)} custom-call(bf16[1024,3072]{1,0:T(8,128)(2,1)} %get-tuple-element.113.act_ref, bf16[32,216,768]{2,1,0:T(8,128)(2,1)} %bitcast.120, f32[1024,768]{1,0:T(8,128)} %get-tuple-element.76.res_ref), custom_call_target="tpu_custom_call" | custom-call | flops 4831838208 | bytes 20000000 | tf_op jit(solution)/shard_map/finish_output/pallas_call | solution.py:552
  244.0 2.8 collective-permute-done.14
  249.0 6.0 %collective-permute-done.15 = bf16[4,48,768]{2,1,0:T(8,128)(2,1)S(1)} collective-permute-done((bf16[4,48,768]{2,1,0:T(8,128)(2,1)S(1)}, bf16[4,48,768]{2,1,0:T(8,128)(2,1)S(1)}, u32[]{:S(2)}, u32[]{:S(2)}) %collective-permute-start.15) | collective-permute-done | bytes 294944 | tf_op jit(solution)/shard_map/ppermute | solution.py:72
  260.6 10.6 %first_back.1 = (f32[1024,768]{1,0:T(8,128)}, f32[8,768]{1,0:T(8,128)}) custom-call(bf16[3,1024,640]{2,1,0:T(8,128)(2,1)} %get-tuple-element.92.refs_0_.d1_ref, bf16[3,1024,128]{2,1,0:T(8,128)(2,1)} %get-tuple-element.95.refs_1_.d2_ref, bf16[2304,768]{1,0:T(8,128)(2,1)} %get-tuple-element.99.refs_5_.w_ref, bf16[1024,768]{1,0:T(8,128)(2,1)} %x_ref.5, ...), custom_call_target="tpu_custom_call" | custom-call | flops 3623878656 | bytes 25000000 | tf_op jit(solution)/shard_map/first_back/pallas_call | solution.py:752
  (99 shorter events, 47.2 us)
Async XLA Ops:
  7.2 22.5 %copy-start.9 = (bf16[768,72]{0,1:T(8,128)(2,1)S(1)}, bf16[768,72]{0,1:T(8,128)(2,1)}, u32[]{:S(2)}) copy-start(bf16[768,72]{0,1:T(8,128)(2,1)} %param.16) | copy-start | bytes 331780
  7.2 100.2 %all-gather.2.cloned.1.call-start = ((), (), s32[]{:S(2)}) async-start(), calls=%async_computation.1 | async-start | bytes 10948608 | tf_op jit(solution)/shard_map/all_gather | solution.py:778
  9.0 262.2 %reduce-scatter.2.cloned.1.call-start = ((), (), s32[]{:S(2)}) async-start(), calls=%async_computation.2 | async-start | bytes 1474560 | tf_op jit(solution)/shard_map/reduce_scatter | solution.py:129
  10.8 9.4 %collective-permute-start.2 = (bf16[1,80,768]{2,1,0:T(8,128)(2,1)S(1)}, bf16[1,80,768]{2,1,0:T(8,128)(2,1)S(1)}, u32[]{:S(2)}, u32[]{:S(2)}) collective-permute-start(bf16[1,80,768]{2,1,0:T(8,128)(2,1)S(1)} %fusion.24), channel_id=1, source_target_pairs={{0,24},{1,25},{2,26},{3,27},{4,28},{5,29},{6,30},{7,31},{8,16},{9,... | collective-permute-start | bytes 368648 | tf_op jit(solution)/shard_map/ppermute | solution.py:72
  15.9 10.5 %collective-permute-start.1 = (bf16[1,80,768]{2,1,0:T(8,128)(2,1)S(1)}, bf16[1,80,768]{2,1,0:T(8,128)(2,1)S(1)}, u32[]{:S(2)}, u32[]{:S(2)}) collective-permute-start(bf16[1,80,768]{2,1,0:T(8,128)(2,1)S(1)} %fusion.24), channel_id=1, source_target_pairs={{0,16},{1,17},{2,18},{3,19},{4,20},{5,21},{6,22},{7,23},{8,24},{9,... | collective-permute-start | bytes 368648 | tf_op jit(solution)/shard_map/ppermute | solution.py:72
  15.9 10.5 %collective-permute-start = (bf16[1,80,768]{2,1,0:T(8,128)(2,1)S(1)}, bf16[1,80,768]{2,1,0:T(8,128)(2,1)S(1)}, u32[]{:S(2)}, u32[]{:S(2)}) collective-permute-start(bf16[1,80,768]{2,1,0:T(8,128)(2,1)S(1)} %fusion.24), channel_id=1, source_target_pairs={{0,8},{1,9},{2,10},{3,11},{4,12},{5,13},{6,14},{7,15},{8,0},{9,1},... | collective-permute-start | bytes 368648 | tf_op jit(solution)/shard_map/ppermute | solution.py:72
  26.5 13.3 %collective-permute-start.3 = (bf16[4,80,768]{2,1,0:T(8,128)(2,1)S(1)}, bf16[4,80,768]{2,1,0:T(8,128)(2,1)S(1)}, u32[]{:S(2)}, u32[]{:S(2)}) collective-permute-start(bf16[4,80,768]{2,1,0:T(8,128)(2,1)S(1)} %pad_maximum_fusion.2), channel_id=1, source_target_pairs={{0,2},{1,3},{2,0},{3,1},{4,6},{5,7},{6,4},{7,5},{8,10},{9,11},{10,... | collective-permute-start | bytes 1474568 | tf_op jit(solution)/shard_map/ppermute | solution.py:72
  28.1 14.2 %collective-permute-start.4 = (bf16[4,80,768]{2,1,0:T(8,128)(2,1)S(1)}, bf16[4,80,768]{2,1,0:T(8,128)(2,1)S(1)}, u32[]{:S(2)}, u32[]{:S(2)}) collective-permute-start(bf16[4,80,768]{2,1,0:T(8,128)(2,1)S(1)} %pad_maximum_fusion.2), channel_id=1, source_target_pairs={{0,4},{1,5},{2,6},{3,7},{4,0},{5,1},{6,2},{7,3},{8,12},{9,13},{10,... | collective-permute-start | bytes 1474568 | tf_op jit(solution)/shard_map/ppermute | solution.py:72
  30.9 28.0 %collective-permute-start.5 = (bf16[4,80,768]{2,1,0:T(8,128)(2,1)S(1)}, bf16[4,80,768]{2,1,0:T(8,128)(2,1)S(1)}, u32[]{:S(2)}, u32[]{:S(2)}) collective-permute-start(bf16[4,80,768]{2,1,0:T(8,128)(2,1)S(1)} %pad_maximum_fusion.2), channel_id=1, source_target_pairs={{0,6},{1,7},{2,4},{3,5},{4,2},{5,3},{6,0},{7,1},{8,14},{9,15},{10,... | collective-permute-start | bytes 1474568 | tf_op jit(solution)/shard_map/ppermute | solution.py:72
  40.6 20.4 %copy-start.10 = (s32[32]{0:T(128)S(1)}, s32[32]{0:T(128)}, u32[]{:S(2)}) copy-start(s32[32]{0:T(128)} %constant.52.clone) | copy-start | bytes 388
  59.7 4.3 %collective-permute-start.6 = (bf16[16,80,768]{2,1,0:T(8,128)(2,1)}, bf16[16,80,768]{2,1,0:T(8,128)(2,1)}, u32[]{:S(2)}, u32[]{:S(2)}) collective-permute-start(bf16[16,80,768]{2,1,0:T(8,128)(2,1)} %constant_dynamic-update-slice_fusion.own_ref), channel_id=1, source_target_pairs={{0,1},{1,0},{2,3},{3,2},{4,5},{5,4},{6,7},{7,6},{8,9},{9,8},{10,11... | collective-permute-start | bytes 5898248 | tf_op jit(solution)/shard_map/ppermute | solution.py:72
  148.6 10.3 %collective-permute-start.7 = (bf16[16,192,768]{2,1,0:T(8,128)(2,1)}, bf16[16,192,768]{2,1,0:T(8,128)(2,1)}, u32[]{:S(2)}, u32[]{:S(2)}) collective-permute-start(bf16[16,192,768]{2,1,0:T(8,128)(2,1)} %get-tuple-element.79), channel_id=1, source_target_pairs={{0,1},{1,0},{2,3},{3,2},{4,5},{5,4},{6,7},{7,6},{8,9},{9,8},{10,11... | collective-permute-start | bytes 14155784 | tf_op jit(solution)/shard_map/ppermute | solution.py:72
  163.1 28.3 %collective-permute-start.9 = (bf16[4,2,96,768]{3,2,0,1:T(8,128)(2,1)}, bf16[4,2,96,768]{3,2,0,1:T(8,128)(2,1)S(1)}, u32[]{:S(2)}, u32[]{:S(2)}) collective-permute-start(bf16[4,2,96,768]{3,2,0,1:T(8,128)(2,1)} %fusion.1), channel_id=1, source_target_pairs={{0,4},{1,5},{2,6},{3,7},{4,0},{5,1},{6,2},{7,3},{8,12},{9,13},{10,... | collective-permute-start | bytes 3538952 | tf_op jit(solution)/shard_map/ppermute | solution.py:72
  164.5 27.9 %collective-permute-start.8 = (bf16[4,2,96,768]{3,2,0,1:T(8,128)(2,1)S(1)}, bf16[4,2,96,768]{3,2,0,1:T(8,128)(2,1)S(1)}, u32[]{:S(2)}, u32[]{:S(2)}) collective-permute-start(bf16[4,2,96,768]{3,2,0,1:T(8,128)(2,1)S(1)} %fusion), channel_id=1, source_target_pairs={{0,2},{1,3},{2,0},{3,1},{4,6},{5,7},{6,4},{7,5},{8,10},{9,11},{10,... | collective-permute-start | bytes 3538952 | tf_op jit(solution)/shard_map/ppermute | solution.py:72
  194.6 21.1 %collective-permute-start.11 = (bf16[4,96,768]{2,1,0:T(8,128)(2,1)S(1)}, bf16[4,96,768]{2,1,0:T(8,128)(2,1)S(1)}, u32[]{:S(2)}, u32[]{:S(2)}) collective-permute-start(bf16[4,96,768]{2,1,0:T(8,128)(2,1)S(1)} %get-tuple-element.126), channel_id=1, source_target_pairs={{0,2},{1,3},{2,0},{3,1},{4,6},{5,7},{6,4},{7,5},{8,10},{9,11},{10,... | collective-permute-start | bytes 1769480 | tf_op jit(solution)/shard_map/ppermute | solution.py:72
  195.5 20.1 %collective-permute-start.10 = (bf16[4,96,768]{2,1,0:T(8,128)(2,1)S(1)}, bf16[4,96,768]{2,1,0:T(8,128)(2,1)S(1)}, u32[]{:S(2)}, u32[]{:S(2)}) collective-permute-start(bf16[4,96,768]{2,1,0:T(8,128)(2,1)S(1)} %get-tuple-element.127), channel_id=1, source_target_pairs={{0,4},{1,5},{2,6},{3,7},{4,0},{5,1},{6,2},{7,3},{8,12},{9,13},{10,... | collective-permute-start | bytes 1769480 | tf_op jit(solution)/shard_map/ppermute | solution.py:72
  216.6 5.2 %collective-permute-start.12 = (bf16[16,104,768]{2,1,0:T(8,128)(2,1)}, bf16[16,104,768]{2,1,0:T(8,128)(2,1)}, u32[]{:S(2)}, u32[]{:S(2)}) collective-permute-start(bf16[16,104,768]{2,1,0:T(8,128)(2,1)} %get-tuple-element.108), channel_id=1, source_target_pairs={{0,1},{1,0},{2,3},{3,2},{4,5},{5,4},{6,7},{7,6},{8,9},{9,8},{10,11... | collective-permute-start | bytes 7667720 | tf_op jit(solution)/shard_map/ppermute | solution.py:72
  228.4 15.6 %collective-permute-start.13 = (bf16[2,4,48,768]{3,2,1,0:T(8,128)(2,1)}, bf16[2,4,48,768]{3,2,1,0:T(8,128)(2,1)S(1)}, u32[]{:S(2)}, u32[]{:S(2)}) collective-permute-start(bf16[2,4,48,768]{3,2,1,0:T(8,128)(2,1)} %fusion.12), channel_id=1, source_target_pairs={{0,2},{1,3},{2,0},{3,1},{4,6},{5,7},{6,4},{7,5},{8,10},{9,11},{10,... | collective-permute-start | bytes 1769480 | tf_op jit(solution)/shard_map/ppermute | solution.py:72
  229.3 17.5 %collective-permute-start.14 = (bf16[2,4,56,768]{3,2,1,0:T(8,128)(2,1)}, bf16[2,4,56,768]{3,2,1,0:T(8,128)(2,1)S(1)}, u32[]{:S(2)}, u32[]{:S(2)}) collective-permute-start(bf16[2,4,56,768]{3,2,1,0:T(8,128)(2,1)} %get-tuple-element.112), channel_id=1, source_target_pairs={{0,4},{1,5},{2,6},{3,7},{4,0},{5,1},{6,2},{7,3},{8,12},{9,13},{10,... | collective-permute-start | bytes 2064392 | tf_op jit(solution)/shard_map/ppermute | solution.py:72
  246.9 8.1 %collective-permute-start.15 = (bf16[4,48,768]{2,1,0:T(8,128)(2,1)S(1)}, bf16[4,48,768]{2,1,0:T(8,128)(2,1)S(1)}, u32[]{:S(2)}, u32[]{:S(2)}) collective-permute-start(bf16[4,48,768]{2,1,0:T(8,128)(2,1)S(1)} %fusion.19), channel_id=1, source_target_pairs={{0,4},{1,5},{2,6},{3,7},{4,0},{5,1},{6,2},{7,3},{8,12},{9,13},{10,... | collective-permute-start | bytes 884744 | tf_op jit(solution)/shard_map/ppermute | solution.py:72
  248.1 8.8 %collective-permute-start.16 = (bf16[4,56,768]{2,1,0:T(8,128)(2,1)S(1)}, bf16[4,56,768]{2,1,0:T(8,128)(2,1)S(1)}, u32[]{:S(2)}, u32[]{:S(2)}) collective-permute-start(bf16[4,56,768]{2,1,0:T(8,128)(2,1)S(1)} %fusion.14), channel_id=1, source_target_pairs={{0,2},{1,3},{2,0},{3,1},{4,6},{5,7},{6,4},{7,5},{8,10},{9,11},{10,... | collective-permute-start | bytes 1032200 | tf_op jit(solution)/shard_map/ppermute | solution.py:72
  257.1 14.2 %collective-permute-start.17 = (bf16[104,768]{1,0:T(8,128)(2,1)S(1)}, bf16[104,768]{1,0:T(8,128)(2,1)S(1)}, u32[]{:S(2)}, u32[]{:S(2)}) collective-permute-start(bf16[104,768]{1,0:T(8,128)(2,1)S(1)} %get-tuple-element.130), channel_id=1, source_target_pairs={{0,8},{1,9},{2,10},{3,11},{4,12},{5,13},{6,14},{7,15},{8,0},{9,1},... | collective-permute-start | bytes 479240 | tf_op jit(solution)/shard_map/ppermute | solution.py:72
  258.4 12.9 %collective-permute-start.19 = (bf16[104,768]{1,0:T(8,128)(2,1)S(1)}, bf16[104,768]{1,0:T(8,128)(2,1)S(1)}, u32[]{:S(2)}, u32[]{:S(2)}) collective-permute-start(bf16[104,768]{1,0:T(8,128)(2,1)S(1)} %get-tuple-element.131), channel_id=1, source_target_pairs={{0,24},{1,25},{2,26},{3,27},{4,28},{5,29},{6,30},{7,31},{8,16},{9,... | collective-permute-start | bytes 479240 | tf_op jit(solution)/shard_map/ppermute | solution.py:72
  260.4 12.3 %collective-permute-start.18 = (bf16[104,768]{1,0:T(8,128)(2,1)S(1)}, bf16[104,768]{1,0:T(8,128)(2,1)S(1)}, u32[]{:S(2)}, u32[]{:S(2)}) collective-permute-start(bf16[104,768]{1,0:T(8,128)(2,1)S(1)} %get-tuple-element.132), channel_id=1, source_target_pairs={{0,16},{1,17},{2,18},{3,19},{4,20},{5,21},{6,22},{7,23},{8,24},{9,... | collective-permute-start | bytes 479240 | tf_op jit(solution)/shard_map/ppermute | solution.py:72
  (9 other events, 59.8 us)
Sparse Core Ops, SparseCore 0:
  10.9 96.3 all-gather.1
  229.4 28.4 reduce-scatter.1

commit v6 on v5

--- a/solution.py
+++ b/solution.py
@@ -17,7 +17,6 @@
 TILE = 256
 CHUNK = 32
 AXES = ("dp", "fsdp")
-VMEM_LIMIT = 56 << 20
 GELU_A = math.sqrt(2.0 / math.pi)
 GELU_B = GELU_A * 0.044715
 
@@ -42,8 +41,8 @@
     return centred * rinv, rinv
 
 
-def params(**kw):
-    return pltpu.CompilerParams(vmem_limit_bytes=VMEM_LIMIT, **kw)
+def params(mib=56):
+    return pltpu.CompilerParams(vmem_limit_bytes=mib << 20)
 
 
 def cost(flops, moved):
@@ -407,7 +406,7 @@
             jax.ShapeDtypeStruct((seqs, 8, count * PAIR), F32),
         ],
         scratch_shapes=[pltpu.VMEM((PAIR, maxlen), F32)],
-        compiler_params=params(),
+        compiler_params=params(40),
         cost_estimate=cost(5e9 * count, 10e6 * count),
         name="attend_backward",
     )(mixed, mixed, mixed, ga, attT, inv, keep)
@@ -615,7 +614,7 @@
             jax.ShapeDtypeStruct(wo.shape, BF16),
             jax.ShapeDtypeStruct((8, width), F32),
         ],
-        compiler_params=params(),
+        compiler_params=params(48),
         cost_estimate=cost(4 * rows * width * width, 30e6),
         name="middle_back",
     )(lengths, gn, residual, cot, att, wo, vecs)
@@ -698,7 +697,7 @@
             scratch_shapes=[pltpu.VMEM((3 * width, width), BF16), pltpu.VMEM((8, width), F32)],
         ),
         out_shape=[shape, shape],
-        compiler_params=params(),
+        compiler_params=params(40),
         cost_estimate=cost(6 * rows * width * width, 25e6),
         name="qkv_grad",
     )(me, *grads, *sums, n1, w_abs, gwo, vecs, gvec2, spread)
@@ -837,9 +836,8 @@
         act, summed = lax.optimization_barrier((act, summed))
         output = finish_output(act, w_ff, residual, ff_units)
         g_attn, output, g_ff, gres = plan.scatter_rest(*summed, output, g_ff, gres)
-        g_attn = g_attn.astype(F32)
         g_qkv, g_out = g_attn[:ppr], g_attn[ppr : ppr + per]
-        g_vec = g_attn[ppr + per, : 4 * per].reshape(4, per)
+        g_vec = g_attn[ppr + per, : 4 * per].astype(F32).reshape(4, per)
     else:
         g_qkv = lax.psum_scatter(qkv_grad_plain(grads, n1), AXES, scatter_dimension=0, tiled=True)
         g_out = lax.psum_scatter(gwo, AXES, scatter_dimension=0, tiled=True)
@@ -848,10 +846,9 @@
         output = finish_output(act, w_ff, residual, ff_units)
         gvec = jnp.concatenate([gvec1[:2], gvec2[:2]], axis=0)
         g_vec = lax.psum_scatter(gvec, AXES, scatter_dimension=1, tiled=True)
-    g_ff = g_ff.astype(F32)
     return (
         output, gtok, g_vec[0], g_vec[1], g_qkv.astype(F32).T, g_out.astype(F32), g_vec[2], g_vec[3],
-        g_ff[:units].T, g_ff[units:],
+        g_ff[:units].astype(F32).T, g_ff[units:].astype(F32),
     )
 
 

time: 287 us -> 283 us (0.986)
  Pallas kernels: 157 us -> 151 us
    convert_element_type x11 -> x12, other arithmetic: 16 us -> 14.8 us  [add_low(): return total.astype(first.dtype)]
    unnamed x27 -> x39, local copies, waits for them, and re-layouts: 4.61 us -> 5.76 us
  transfers between devices with their start and end apart: 22 -> 22, of which waited for: 15 -> 15; matrix products, arithmetic and copies ran while one was open for 5% -> 5% of each run, Pallas kernels for 41% -> 39%
where the time goes in v6:
time: 283 us; the launch traced here: 279 us
  Pallas kernels  151 us (53%)
  waiting for transfers between devices  57.4 us (20%)
  other arithmetic  26.7 us (9%)
  starting transfers between devices  21.9 us (8%)
  between operations  15.2 us (5%)
  local copies, waits for them, and re-layouts  7.28 us (3%)
    ppermute x20, waiting for transfers between devices, swap(): return lax.ppermute(value, AXES, [(i, i ^ mask) for i in range(self.n)])  55.7 us
    pallas_call x1, Pallas kernels, feed_forward(): pl.pallas_call(functools.partial(mlp_kernel, units), grid_spec=pltpu.Pref...  36 us
    pallas_call x1, Pallas kernels, attend_forward(): pl.pallas_call(functools.partial(attend_kernel, maxlen), grid_spec=pltpu....  31.6 us
    pallas_call x2, Pallas kernels, attend_backward(): pl.pallas_call(functools.partial(attend_back_kernel, maxlen), grid=(seqs,...  27.9 us
    ppermute x20, starting transfers between devices, swap(): return lax.ppermute(value, AXES, [(i, i ^ mask) for i in range(self.n)])  21.8 us
    convert_element_type x12, other arithmetic, add_low(): return total.astype(first.dtype)  14.8 us
    pallas_call x1, Pallas kernels, finish_output(): pl.pallas_call(functools.partial(finish_kernel, units), grid=(pieces // t...  12.1 us
    pallas_call x1, Pallas kernels, first_back(): pl.pallas_call(first_kernel, grid=(rows // rows_block,), in_specs=[pl.Blo...  10.6 us
  transfers between devices with their start and end apart: 22, of which 15 were waited for; matrix products, arithmetic and copies ran while one was open for 5% of the time, Pallas kernels for 39%

profile of v6, /device:TPU:0, one launch (start us, length us, event | category | flops | bytes accessed | tf_op | source)
XLA Modules:
  0.0 279.2 jit_solution(3043480442511150376)
XLA Ops:
  10.8 5.1 %collective-permute-start.2 = (bf16[1,80,768]{2,1,0:T(8,128)(2,1)S(1)}, bf16[1,80,768]{2,1,0:T(8,128)(2,1)S(1)}, u32[]{:S(2)}, u32[]{:S(2)}) collective-permute-start(bf16[1,80,768]{2,1,0:T(8,128)(2,1)S(1)} %fusion.23), channel_id=1, source_target_pairs={{0,24},{1,25},{2,26},{3,27},{4,28},{5,29},{6,30},{7,31},{8,16},{9,... | collective-permute-start | bytes 368648 | tf_op jit(solution)/shard_map/ppermute | solution.py:71
  16.5 3.6 %collective-permute-done.2 = bf16[1,80,768]{2,1,0:T(8,128)(2,1)S(1)} collective-permute-done((bf16[1,80,768]{2,1,0:T(8,128)(2,1)S(1)}, bf16[1,80,768]{2,1,0:T(8,128)(2,1)S(1)}, u32[]{:S(2)}, u32[]{:S(2)}) %collective-permute-start.2) | collective-permute-done | bytes 122912 | tf_op jit(solution)/shard_map/ppermute | solution.py:71
  20.1 6.3 %collective-permute-done.1 = bf16[1,80,768]{2,1,0:T(8,128)(2,1)S(1)} collective-permute-done((bf16[1,80,768]{2,1,0:T(8,128)(2,1)S(1)}, bf16[1,80,768]{2,1,0:T(8,128)(2,1)S(1)}, u32[]{:S(2)}, u32[]{:S(2)}) %collective-permute-start.1) | collective-permute-done | bytes 122912 | tf_op jit(solution)/shard_map/ppermute | solution.py:71
  33.4 6.4 %collective-permute-done.3 = bf16[4,80,768]{2,1,0:T(8,128)(2,1)S(1)} collective-permute-done((bf16[4,80,768]{2,1,0:T(8,128)(2,1)S(1)}, bf16[4,80,768]{2,1,0:T(8,128)(2,1)S(1)}, u32[]{:S(2)}, u32[]{:S(2)}) %collective-permute-start.3) | collective-permute-done | bytes 491552 | tf_op jit(solution)/shard_map/ppermute | solution.py:71
  43.1 15.8 %collective-permute-done.5 = bf16[4,80,768]{2,1,0:T(8,128)(2,1)S(1)} collective-permute-done((bf16[4,80,768]{2,1,0:T(8,128)(2,1)S(1)}, bf16[4,80,768]{2,1,0:T(8,128)(2,1)S(1)}, u32[]{:S(2)}, u32[]{:S(2)}) %collective-permute-start.5) | collective-permute-done | bytes 491552 | tf_op jit(solution)/shard_map/ppermute | solution.py:71
  64.1 10.0 %qkv_project.1 = (bf16[1024,2304]{1,0:T(8,128)(2,1)}, bf16[1024,768]{1,0:T(8,128)(2,1)}, bf16[2304,768]{1,0:T(8,128)(2,1)}, f32[8,768]{1,0:T(8,128)}) custom-call(s32[1]{0:T(128)} %bitcast.me_ref, bf16[1024,768]{1,0:T(8,128)(2,1)} %x_ref.5, bf16[16,80,768]{2,1,0:T(8,128)(2,1)} %constant_dynamic-update-slice_fusion.own_ref, ...), custom_call_target="tpu_custom_call" | custom-call | flops 3623878656 | bytes 20000000 | tf_op jit(solution)/shard_map/qkv_project/pallas_call | solution.py:177
  74.0 31.6 %attend_forward.1 = (bf16[1024,768]{1,0:T(8,128)(2,1)}, bf16[768,1024]{1,0:T(8,128)(2,1)}, f32[6,8,1024]{2,1,0:T(8,128)}, bf16[6,2,3,10,256,256]{5,4,3,2,1,0:T(8,128)(2,1)}) custom-call(s32[1]{0:T(128)} %copy.56.len_ref, bf16[1024,2304]{1,0:T(8,128)(2,1)} %get-tuple-element.69.q_ref.k_ref.v_ref, bf16[1024,2304]{1,0:T(8,128)(2,1)} %get-tuple-element.69.q_ref.k_ref.v_ref, ...), custom_call_target="tpu_custom_call" | custom-call | flops 20000000000 | bytes 60000000 | tf_op jit(solution)/shard_map/attend_forward/pallas_call | solution.py:309
  107.4 5.5 %project_out.1 = (f32[1024,768]{1,0:T(8,128)}, bf16[1024,768]{1,0:T(8,128)(2,1)}, bf16[768,768]{1,0:T(8,128)(2,1)}) custom-call(bf16[1024,768]{1,0:T(8,128)(2,1)} %get-tuple-element.70.att_ref, bf16[1024,768]{1,0:T(8,128)(2,1)} %x_ref.5, bf16[32,216,768]{2,1,0:T(8,128)(2,1)} %bitcast.123, f32[8,768]{1,0:T(8,128)} %get-tuple-element.71.vec_ref.refs_7_), custom_call_target="tpu_custom_call" | custom-call | flops 1207959552 | bytes 10000000 | tf_op jit(solution)/shard_map/project_out/pallas_call | solution.py:434
  112.9 36.0 %feed_forward.1 = (bf16[1024,3072]{1,0:T(8,128)(2,1)}, f32[1024,768]{1,0:T(8,128)}, bf16[16,192,768]{2,1,0:T(8,128)(2,1)}, bf16[16,192,768]{2,1,0:T(8,128)(2,1)}) custom-call(s32[1]{0:T(128)} %bitcast.me_ref, bf16[1024,768]{1,0:T(8,128)(2,1)} %get-tuple-element.72.n2_ref, bf16[1024,768]{1,0:T(8,128)(2,1)} %select_convert_fusion.gl_ref, ...), custom_call_target="tpu_custom_call" | custom-call | flops 24159191040 | bytes 40000000 | tf_op jit(solution)/shard_map/feed_forward/pallas_call | solution.py:510
  149.1 8.2 %middle_back.1 = (f32[1024,768]{1,0:T(8,128)}, bf16[1024,768]{1,0:T(8,128)(2,1)S(1)}, bf16[768,768]{1,0:T(8,128)(2,1)S(1)}, f32[8,768]{1,0:T(8,128)S(1)}) custom-call(s32[1]{0:T(128)} %copy.56.len_ref, f32[1024,768]{1,0:T(8,128)} %get-tuple-element.75.gn_ref, f32[1024,768]{1,0:T(8,128)} %get-tuple-element.76.res_ref, f32[1024,768]{1,0:T(8,128)} %cot_ref.1, ...), custom_call_target="tpu_custom_call" | custom-call | flops 2415919104 | bytes 30000000 | tf_op jit(solution)/shard_map/middle_back/pallas_call | solution.py:602
  157.3 2.1 copy-done.11
  161.0 2.0 fusion.1
  165.3 21.0 %attend_backward.2 = (bf16[3,1024,640]{2,1,0:T(8,128)(2,1)S(1)}, f32[1,8,640]{2,1,0:T(8,128)S(1)}) custom-call(bf16[1024,2304]{1,0:T(8,128)(2,1)S(1)} %bitcast.119, bf16[1024,2304]{1,0:T(8,128)(2,1)S(1)} %bitcast.119, bf16[1024,2304]{1,0:T(8,128)(2,1)S(1)} %bitcast.119, bf16[1024,768]{1,0:T(8,128)(2,1)S(1)} %get-tuple-element.94.ga_ref, ...), custom_call_target="tpu_custom_call" | custom-call | flops 24999999488 | bytes 50000000 | tf_op jit(solution)/shard_map/attend_backward/pallas_call | solution.py:391
  186.3 5.0 %collective-permute-done.9 = bf16[4,2,96,768]{3,2,0,1:T(8,128)(2,1)S(1)} collective-permute-done((bf16[4,2,96,768]{3,2,0,1:T(8,128)(2,1)S(1)}, bf16[4,2,96,768]{3,2,0,1:T(8,128)(2,1)S(1)}, u32[]{:S(2)}, u32[]{:S(2)}) %collective-permute-start.9) | collective-permute-done | bytes 1179680 | tf_op jit(solution)/shard_map/ppermute | solution.py:71
  192.4 2.0 fusion.4
  196.6 6.9 %attend_backward.3 = (bf16[3,1024,128]{2,1,0:T(8,128)(2,1)S(1)}, f32[1,8,128]{2,1,0:T(8,128)S(1)}) custom-call(bf16[1024,2304]{1,0:T(8,128)(2,1)S(1)} %bitcast.119, bf16[1024,2304]{1,0:T(8,128)(2,1)S(1)} %bitcast.119, bf16[1024,2304]{1,0:T(8,128)(2,1)S(1)} %bitcast.119, bf16[1024,768]{1,0:T(8,128)(2,1)S(1)} %get-tuple-element.94.ga_ref, ...), custom_call_target="tpu_custom_call" | custom-call | flops 5000000000 | bytes 10000000 | tf_op jit(solution)/shard_map/attend_backward/pallas_call | solution.py:391
  203.5 9.0 %qkv_grad.1 = (bf16[16,104,768]{2,1,0:T(8,128)(2,1)S(1)}, bf16[16,104,768]{2,1,0:T(8,128)(2,1)}) custom-call(s32[1]{0:T(128)} %bitcast.me_ref, bf16[3,1024,640]{2,1,0:T(8,128)(2,1)} %copy-done.7, bf16[3,1024,128]{2,1,0:T(8,128)(2,1)S(1)} %get-tuple-element.95.refs_1_.d2_ref, f32[1,8,640]{2,1,0:T(8,128)S(1)} %get-tuple-element.96.refs_2_, ...), custom_call_target="tpu_custom_call" | custom-call | flops 3623878656 | bytes 25000000 | tf_op jit(solution)/shard_map/qkv_grad/pallas_call | solution.py:687
  212.6 2.2 fusion.7
  219.7 2.0 fusion.11
  221.8 2.5 fusion.9
  226.2 12.1 %finish_output.1 = bf16[1024,768]{1,0:T(8,128)(2,1)} custom-call(bf16[1024,3072]{1,0:T(8,128)(2,1)} %get-tuple-element.113.act_ref, bf16[32,216,768]{2,1,0:T(8,128)(2,1)} %bitcast.125, f32[1024,768]{1,0:T(8,128)} %get-tuple-element.76.res_ref), custom_call_target="tpu_custom_call" | custom-call | flops 4831838208 | bytes 20000000 | tf_op jit(solution)/shard_map/finish_output/pallas_call | solution.py:551
  239.9 2.5 collective-permute-done.14
  244.8 5.8 %collective-permute-done.15 = bf16[4,48,768]{2,1,0:T(8,128)(2,1)S(1)} collective-permute-done((bf16[4,48,768]{2,1,0:T(8,128)(2,1)S(1)}, bf16[4,48,768]{2,1,0:T(8,128)(2,1)S(1)}, u32[]{:S(2)}, u32[]{:S(2)}) %collective-permute-start.15) | collective-permute-done | bytes 294944 | tf_op jit(solution)/shard_map/ppermute | solution.py:71
  256.3 10.6 %first_back.1 = (f32[1024,768]{1,0:T(8,128)}, f32[8,768]{1,0:T(8,128)}) custom-call(bf16[3,1024,640]{2,1,0:T(8,128)(2,1)} %copy-done.7, bf16[3,1024,128]{2,1,0:T(8,128)(2,1)} %copy-done.6, bf16[2304,768]{1,0:T(8,128)(2,1)} %get-tuple-element.99.refs_5_.w_ref, bf16[1024,768]{1,0:T(8,128)(2,1)} %x_ref.5, f32[1024,768]{1,0:T(8,128)} %get-tuple-element.118.gres_ref, ...), custom_call_target="tpu_custom_call" | custom-call | flops 3623878656 | bytes 25000000 | tf_op jit(solution)/shard_map/first_back/pallas_call | solution.py:751
  (111 shorter events, 49.8 us)
Async XLA Ops:
  7.2 100.2 %all-gather.2.cloned.1.call-start = ((), (), s32[]{:S(2)}) async-start(), calls=%async_computation.1 | async-start | bytes 10948608 | tf_op jit(solution)/shard_map/all_gather | solution.py:777
  9.0 257.9 %reduce-scatter.2.cloned.1.call-start = ((), (), s32[]{:S(2)}) async-start(), calls=%async_computation.2 | async-start | bytes 1474560 | tf_op jit(solution)/shard_map/reduce_scatter | solution.py:128
  10.8 9.4 %collective-permute-start.2 = (bf16[1,80,768]{2,1,0:T(8,128)(2,1)S(1)}, bf16[1,80,768]{2,1,0:T(8,128)(2,1)S(1)}, u32[]{:S(2)}, u32[]{:S(2)}) collective-permute-start(bf16[1,80,768]{2,1,0:T(8,128)(2,1)S(1)} %fusion.23), channel_id=1, source_target_pairs={{0,24},{1,25},{2,26},{3,27},{4,28},{5,29},{6,30},{7,31},{8,16},{9,... | collective-permute-start | bytes 368648 | tf_op jit(solution)/shard_map/ppermute | solution.py:71
  15.9 10.5 %collective-permute-start.1 = (bf16[1,80,768]{2,1,0:T(8,128)(2,1)S(1)}, bf16[1,80,768]{2,1,0:T(8,128)(2,1)S(1)}, u32[]{:S(2)}, u32[]{:S(2)}) collective-permute-start(bf16[1,80,768]{2,1,0:T(8,128)(2,1)S(1)} %fusion.23), channel_id=1, source_target_pairs={{0,16},{1,17},{2,18},{3,19},{4,20},{5,21},{6,22},{7,23},{8,24},{9,... | collective-permute-start | bytes 368648 | tf_op jit(solution)/shard_map/ppermute | solution.py:71
  15.9 10.5 %collective-permute-start = (bf16[1,80,768]{2,1,0:T(8,128)(2,1)S(1)}, bf16[1,80,768]{2,1,0:T(8,128)(2,1)S(1)}, u32[]{:S(2)}, u32[]{:S(2)}) collective-permute-start(bf16[1,80,768]{2,1,0:T(8,128)(2,1)S(1)} %fusion.23), channel_id=1, source_target_pairs={{0,8},{1,9},{2,10},{3,11},{4,12},{5,13},{6,14},{7,15},{8,0},{9,1},... | collective-permute-start | bytes 368648 | tf_op jit(solution)/shard_map/ppermute | solution.py:71
  26.5 13.3 %collective-permute-start.3 = (bf16[4,80,768]{2,1,0:T(8,128)(2,1)S(1)}, bf16[4,80,768]{2,1,0:T(8,128)(2,1)S(1)}, u32[]{:S(2)}, u32[]{:S(2)}) collective-permute-start(bf16[4,80,768]{2,1,0:T(8,128)(2,1)S(1)} %pad_maximum_fusion.2), channel_id=1, source_target_pairs={{0,2},{1,3},{2,0},{3,1},{4,6},{5,7},{6,4},{7,5},{8,10},{9,11},{10,... | collective-permute-start | bytes 1474568 | tf_op jit(solution)/shard_map/ppermute | solution.py:71
  28.1 14.2 %collective-permute-start.4 = (bf16[4,80,768]{2,1,0:T(8,128)(2,1)S(1)}, bf16[4,80,768]{2,1,0:T(8,128)(2,1)S(1)}, u32[]{:S(2)}, u32[]{:S(2)}) collective-permute-start(bf16[4,80,768]{2,1,0:T(8,128)(2,1)S(1)} %pad_maximum_fusion.2), channel_id=1, source_target_pairs={{0,4},{1,5},{2,6},{3,7},{4,0},{5,1},{6,2},{7,3},{8,12},{9,13},{10,... | collective-permute-start | bytes 1474568 | tf_op jit(solution)/shard_map/ppermute | solution.py:71
  31.0 28.0 %collective-permute-start.5 = (bf16[4,80,768]{2,1,0:T(8,128)(2,1)S(1)}, bf16[4,80,768]{2,1,0:T(8,128)(2,1)S(1)}, u32[]{:S(2)}, u32[]{:S(2)}) collective-permute-start(bf16[4,80,768]{2,1,0:T(8,128)(2,1)S(1)} %pad_maximum_fusion.2), channel_id=1, source_target_pairs={{0,6},{1,7},{2,4},{3,5},{4,2},{5,3},{6,0},{7,1},{8,14},{9,15},{10,... | collective-permute-start | bytes 1474568 | tf_op jit(solution)/shard_map/ppermute | solution.py:71
  59.7 4.3 %collective-permute-start.6 = (bf16[16,80,768]{2,1,0:T(8,128)(2,1)}, bf16[16,80,768]{2,1,0:T(8,128)(2,1)}, u32[]{:S(2)}, u32[]{:S(2)}) collective-permute-start(bf16[16,80,768]{2,1,0:T(8,128)(2,1)} %constant_dynamic-update-slice_fusion.own_ref), channel_id=1, source_target_pairs={{0,1},{1,0},{2,3},{3,2},{4,5},{5,4},{6,7},{7,6},{8,9},{9,8},{10,11... | collective-permute-start | bytes 5898248 | tf_op jit(solution)/shard_map/ppermute | solution.py:71
  107.4 57.9 %slice-start = ((s8[4718592]{0:T(1024)(128)(4,1)}), s8[4194304]{0:T(1024)(128)(4,1)S(1)}, s32[]{:S(2)}) async-start(s8[4718592]{0:T(1024)(128)(4,1)} %bitcast.118), calls=%async_computation.3 | async-start | bytes 8388608
  112.8 52.4 %slice-start.1 = ((s8[4718592]{0:T(1024)(128)(4,1)}), s8[524288]{0:T(1024)(128)(4,1)S(1)}, s32[]{:S(2)}) async-start(s8[4718592]{0:T(1024)(128)(4,1)} %bitcast.118), calls=%async_computation.4 | async-start | bytes 1048576
  148.8 8.5 %collective-permute-start.7 = (bf16[16,192,768]{2,1,0:T(8,128)(2,1)}, bf16[16,192,768]{2,1,0:T(8,128)(2,1)S(1)}, u32[]{:S(2)}, u32[]{:S(2)}) collective-permute-start(bf16[16,192,768]{2,1,0:T(8,128)(2,1)} %get-tuple-element.79), channel_id=1, source_target_pairs={{0,1},{1,0},{2,3},{3,2},{4,5},{5,4},{6,7},{7,6},{8,9},{9,8},{10,11... | collective-permute-start | bytes 14155784 | tf_op jit(solution)/shard_map/ppermute | solution.py:71
  163.1 28.2 %collective-permute-start.9 = (bf16[4,2,96,768]{3,2,0,1:T(8,128)(2,1)S(1)}, bf16[4,2,96,768]{3,2,0,1:T(8,128)(2,1)S(1)}, u32[]{:S(2)}, u32[]{:S(2)}) collective-permute-start(bf16[4,2,96,768]{3,2,0,1:T(8,128)(2,1)S(1)} %fusion.1), channel_id=1, source_target_pairs={{0,4},{1,5},{2,6},{3,7},{4,0},{5,1},{6,2},{7,3},{8,12},{9,13},{10,... | collective-permute-start | bytes 3538952 | tf_op jit(solution)/shard_map/ppermute | solution.py:71
  164.6 27.8 %collective-permute-start.8 = (bf16[4,2,96,768]{3,2,0,1:T(8,128)(2,1)S(1)}, bf16[4,2,96,768]{3,2,0,1:T(8,128)(2,1)S(1)}, u32[]{:S(2)}, u32[]{:S(2)}) collective-permute-start(bf16[4,2,96,768]{3,2,0,1:T(8,128)(2,1)S(1)} %fusion), channel_id=1, source_target_pairs={{0,2},{1,3},{2,0},{3,1},{4,6},{5,7},{6,4},{7,5},{8,10},{9,11},{10,... | collective-permute-start | bytes 3538952 | tf_op jit(solution)/shard_map/ppermute | solution.py:71
  194.5 18.0 %collective-permute-start.11 = (bf16[4,96,768]{2,1,0:T(8,128)(2,1)S(1)}, bf16[4,96,768]{2,1,0:T(8,128)(2,1)S(1)}, u32[]{:S(2)}, u32[]{:S(2)}) collective-permute-start(bf16[4,96,768]{2,1,0:T(8,128)(2,1)S(1)} %get-tuple-element.126), channel_id=1, source_target_pairs={{0,2},{1,3},{2,0},{3,1},{4,6},{5,7},{6,4},{7,5},{8,10},{9,11},{10,... | collective-permute-start | bytes 1769480 | tf_op jit(solution)/shard_map/ppermute | solution.py:71
  195.3 17.2 %collective-permute-start.10 = (bf16[4,96,768]{2,1,0:T(8,128)(2,1)S(1)}, bf16[4,96,768]{2,1,0:T(8,128)(2,1)S(1)}, u32[]{:S(2)}, u32[]{:S(2)}) collective-permute-start(bf16[4,96,768]{2,1,0:T(8,128)(2,1)S(1)} %get-tuple-element.127), channel_id=1, source_target_pairs={{0,4},{1,5},{2,6},{3,7},{4,0},{5,1},{6,2},{7,3},{8,12},{9,13},{10,... | collective-permute-start | bytes 1769480 | tf_op jit(solution)/shard_map/ppermute | solution.py:71
  212.5 5.2 %collective-permute-start.12 = (bf16[16,104,768]{2,1,0:T(8,128)(2,1)}, bf16[16,104,768]{2,1,0:T(8,128)(2,1)}, u32[]{:S(2)}, u32[]{:S(2)}) collective-permute-start(bf16[16,104,768]{2,1,0:T(8,128)(2,1)} %get-tuple-element.108), channel_id=1, source_target_pairs={{0,1},{1,0},{2,3},{3,2},{4,5},{5,4},{6,7},{7,6},{8,9},{9,8},{10,11... | collective-permute-start | bytes 7667720 | tf_op jit(solution)/shard_map/ppermute | solution.py:71
  224.2 15.6 %collective-permute-start.13 = (bf16[2,4,48,768]{3,2,1,0:T(8,128)(2,1)}, bf16[2,4,48,768]{3,2,1,0:T(8,128)(2,1)S(1)}, u32[]{:S(2)}, u32[]{:S(2)}) collective-permute-start(bf16[2,4,48,768]{3,2,1,0:T(8,128)(2,1)} %fusion.12), channel_id=1, source_target_pairs={{0,2},{1,3},{2,0},{3,1},{4,6},{5,7},{6,4},{7,5},{8,10},{9,11},{10,... | collective-permute-start | bytes 1769480 | tf_op jit(solution)/shard_map/ppermute | solution.py:71
  224.9 17.5 %collective-permute-start.14 = (bf16[2,4,56,768]{3,2,1,0:T(8,128)(2,1)}, bf16[2,4,56,768]{3,2,1,0:T(8,128)(2,1)S(1)}, u32[]{:S(2)}, u32[]{:S(2)}) collective-permute-start(bf16[2,4,56,768]{3,2,1,0:T(8,128)(2,1)} %get-tuple-element.112), channel_id=1, source_target_pairs={{0,4},{1,5},{2,6},{3,7},{4,0},{5,1},{6,2},{7,3},{8,12},{9,13},{10,... | collective-permute-start | bytes 2064392 | tf_op jit(solution)/shard_map/ppermute | solution.py:71
  242.5 8.1 %collective-permute-start.15 = (bf16[4,48,768]{2,1,0:T(8,128)(2,1)S(1)}, bf16[4,48,768]{2,1,0:T(8,128)(2,1)S(1)}, u32[]{:S(2)}, u32[]{:S(2)}) collective-permute-start(bf16[4,48,768]{2,1,0:T(8,128)(2,1)S(1)} %fusion.19), channel_id=1, source_target_pairs={{0,4},{1,5},{2,6},{3,7},{4,0},{5,1},{6,2},{7,3},{8,12},{9,13},{10,... | collective-permute-start | bytes 884744 | tf_op jit(solution)/shard_map/ppermute | solution.py:71
  243.8 8.8 %collective-permute-start.16 = (bf16[4,56,768]{2,1,0:T(8,128)(2,1)S(1)}, bf16[4,56,768]{2,1,0:T(8,128)(2,1)S(1)}, u32[]{:S(2)}, u32[]{:S(2)}) collective-permute-start(bf16[4,56,768]{2,1,0:T(8,128)(2,1)S(1)} %fusion.14), channel_id=1, source_target_pairs={{0,2},{1,3},{2,0},{3,1},{4,6},{5,7},{6,4},{7,5},{8,10},{9,11},{10,... | collective-permute-start | bytes 1032200 | tf_op jit(solution)/shard_map/ppermute | solution.py:71
  252.8 14.1 %collective-permute-start.17 = (bf16[104,768]{1,0:T(8,128)(2,1)S(1)}, bf16[104,768]{1,0:T(8,128)(2,1)S(1)}, u32[]{:S(2)}, u32[]{:S(2)}) collective-permute-start(bf16[104,768]{1,0:T(8,128)(2,1)S(1)} %get-tuple-element.130), channel_id=1, source_target_pairs={{0,8},{1,9},{2,10},{3,11},{4,12},{5,13},{6,14},{7,15},{8,0},{9,1},... | collective-permute-start | bytes 479240 | tf_op jit(solution)/shard_map/ppermute | solution.py:71
  254.1 12.8 %collective-permute-start.19 = (bf16[104,768]{1,0:T(8,128)(2,1)S(1)}, bf16[104,768]{1,0:T(8,128)(2,1)S(1)}, u32[]{:S(2)}, u32[]{:S(2)}) collective-permute-start(bf16[104,768]{1,0:T(8,128)(2,1)S(1)} %get-tuple-element.131), channel_id=1, source_target_pairs={{0,24},{1,25},{2,26},{3,27},{4,28},{5,29},{6,30},{7,31},{8,16},{9,... | collective-permute-start | bytes 479240 | tf_op jit(solution)/shard_map/ppermute | solution.py:71
  256.1 12.3 %collective-permute-start.18 = (bf16[104,768]{1,0:T(8,128)(2,1)S(1)}, bf16[104,768]{1,0:T(8,128)(2,1)S(1)}, u32[]{:S(2)}, u32[]{:S(2)}) collective-permute-start(bf16[104,768]{1,0:T(8,128)(2,1)S(1)} %get-tuple-element.132), channel_id=1, source_target_pairs={{0,16},{1,17},{2,18},{3,19},{4,20},{5,21},{6,22},{7,23},{8,24},{9,... | collective-permute-start | bytes 479240 | tf_op jit(solution)/shard_map/ppermute | solution.py:71
  (15 other events, 238.3 us)
Sparse Core Ops, SparseCore 0:
  10.9 96.3 all-gather.1
  225.1 28.4 reduce-scatter.1

commit v7 on v6

--- a/solution.py
+++ b/solution.py
@@ -519,7 +519,7 @@
         ),
         out_shape=[jax.ShapeDtypeStruct((rows, pieces * units), BF16), jax.ShapeDtypeStruct((rows, width), F32)]
         + [jax.ShapeDtypeStruct((pieces // outs, 2 * units, width), BF16)] * outs,
-        compiler_params=params(),
+        compiler_params=params(50),
         cost_estimate=cost(10 * rows * width * pieces * units, 40e6),
         name="feed_forward",
     )(me, n2, gl, w)

time: 283 us -> 283 us (level)
  local copies, waits for them, and re-layouts: 7.28 us -> 2.34 us
  waiting for transfers between devices: 57.4 us -> 61 us
    unnamed x39 -> x49, local copies, waits for them, and re-layouts: 5.76 us -> 1.6 us
    ppermute x20, waiting for transfers between devices: 55.7 us -> 59.2 us  [swap(): return lax.ppermute(value, AXES, [(i, i ^ mask) for i in range(self.n)])]
  transfers between devices with their start and end apart: 22 -> 22, of which waited for: 15 -> 14; matrix products, arithmetic and copies ran while one was open for 5% -> 4% of each run, Pallas kernels for 39% -> 39%
where the time goes in v7:
time: 283 us; the launch traced here: 279 us
  Pallas kernels  151 us (53%)
  waiting for transfers between devices  61 us (22%)
  other arithmetic  28.1 us (10%)
  starting transfers between devices  21.8 us (8%)
  between operations  15.3 us (5%)
    ppermute x20, waiting for transfers between devices, swap(): return lax.ppermute(value, AXES, [(i, i ^ mask) for i in range(self.n)])  59.2 us
    pallas_call x1, Pallas kernels, feed_forward(): pl.pallas_call(functools.partial(mlp_kernel, units), grid_spec=pltpu.Pref...  35.2 us
    pallas_call x1, Pallas kernels, attend_forward(): pl.pallas_call(functools.partial(attend_kernel, maxlen), grid_spec=pltpu....  31.7 us
    pallas_call x2, Pallas kernels, attend_backward(): pl.pallas_call(functools.partial(attend_back_kernel, maxlen), grid=(seqs,...  27.9 us
    ppermute x20, starting transfers between devices, swap(): return lax.ppermute(value, AXES, [(i, i ^ mask) for i in range(self.n)])  21.7 us
    convert_element_type x12, other arithmetic, add_low(): return total.astype(first.dtype)  16.1 us
    pallas_call x1, Pallas kernels, finish_output(): pl.pallas_call(functools.partial(finish_kernel, units), grid=(pieces // t...  12.1 us
    pallas_call x1, Pallas kernels, first_back(): pl.pallas_call(first_kernel, grid=(rows // rows_block,), in_specs=[pl.Blo...  10.6 us
  transfers between devices with their start and end apart: 22, of which 14 were waited for; matrix products, arithmetic and copies ran while one was open for 4% of the time, Pallas kernels for 39%

profile of v7, /device:TPU:0, one launch (start us, length us, event | category | flops | bytes accessed | tf_op | source)
XLA Modules:
  0.0 279.2 jit_solution(2593956283369079037)
XLA Ops:
  10.8 5.1 %collective-permute-start.2 = (bf16[1,80,768]{2,1,0:T(8,128)(2,1)S(1)}, bf16[1,80,768]{2,1,0:T(8,128)(2,1)S(1)}, u32[]{:S(2)}, u32[]{:S(2)}) collective-permute-start(bf16[1,80,768]{2,1,0:T(8,128)(2,1)S(1)} %fusion.23), channel_id=1, source_target_pairs={{0,24},{1,25},{2,26},{3,27},{4,28},{5,29},{6,30},{7,31},{8,16},{9,... | collective-permute-start | bytes 368648 | tf_op jit(solution)/shard_map/ppermute | solution.py:71
  16.5 3.6 %collective-permute-done.2 = bf16[1,80,768]{2,1,0:T(8,128)(2,1)S(1)} collective-permute-done((bf16[1,80,768]{2,1,0:T(8,128)(2,1)S(1)}, bf16[1,80,768]{2,1,0:T(8,128)(2,1)S(1)}, u32[]{:S(2)}, u32[]{:S(2)}) %collective-permute-start.2) | collective-permute-done | bytes 122912 | tf_op jit(solution)/shard_map/ppermute | solution.py:71
  20.1 6.3 %collective-permute-done.1 = bf16[1,80,768]{2,1,0:T(8,128)(2,1)S(1)} collective-permute-done((bf16[1,80,768]{2,1,0:T(8,128)(2,1)S(1)}, bf16[1,80,768]{2,1,0:T(8,128)(2,1)S(1)}, u32[]{:S(2)}, u32[]{:S(2)}) %collective-permute-start.1) | collective-permute-done | bytes 122912 | tf_op jit(solution)/shard_map/ppermute | solution.py:71
  30.8 9.0 %collective-permute-done.3 = bf16[4,80,768]{2,1,0:T(8,128)(2,1)S(1)} collective-permute-done((bf16[4,80,768]{2,1,0:T(8,128)(2,1)S(1)}, bf16[4,80,768]{2,1,0:T(8,128)(2,1)S(1)}, u32[]{:S(2)}, u32[]{:S(2)}) %collective-permute-start.3) | collective-permute-done | bytes 491552 | tf_op jit(solution)/shard_map/ppermute | solution.py:71
  39.9 2.4 collective-permute-done.4
  42.3 16.6 %collective-permute-done.5 = bf16[4,80,768]{2,1,0:T(8,128)(2,1)S(1)} collective-permute-done((bf16[4,80,768]{2,1,0:T(8,128)(2,1)S(1)}, bf16[4,80,768]{2,1,0:T(8,128)(2,1)S(1)}, u32[]{:S(2)}, u32[]{:S(2)}) %collective-permute-start.5) | collective-permute-done | bytes 491552 | tf_op jit(solution)/shard_map/ppermute | solution.py:71
  61.2 2.1 select_convert_fusion.gl_ref
  63.4 10.5 %qkv_project.1 = (bf16[1024,2304]{1,0:T(8,128)(2,1)}, bf16[1024,768]{1,0:T(8,128)(2,1)}, bf16[2304,768]{1,0:T(8,128)(2,1)}, f32[8,768]{1,0:T(8,128)}) custom-call(s32[1]{0:T(128)} %bitcast.me_ref, bf16[1024,768]{1,0:T(8,128)(2,1)} %x_ref.5, bf16[16,80,768]{2,1,0:T(8,128)(2,1)} %copy-done.18, bf16[16,80,768]{2,1,0:T(8,128)(2,1)} %collective-permute-done.6.sib_ref, ...), custom_call_target="tpu_custom_call" | custom-call | flops 3623878656 | bytes 20000000 | tf_op jit(solution)/shard_map/qkv_project/pallas_call | solution.py:177
  74.0 31.7 %attend_forward.1 = (bf16[1024,768]{1,0:T(8,128)(2,1)}, bf16[768,1024]{1,0:T(8,128)(2,1)}, f32[6,8,1024]{2,1,0:T(8,128)}, bf16[6,2,3,10,256,256]{5,4,3,2,1,0:T(8,128)(2,1)}) custom-call(s32[1]{0:T(128)} %copy.56.len_ref, bf16[1024,2304]{1,0:T(8,128)(2,1)} %get-tuple-element.69.q_ref.k_ref.v_ref, bf16[1024,2304]{1,0:T(8,128)(2,1)} %get-tuple-element.69.q_ref.k_ref.v_ref, ...), custom_call_target="tpu_custom_call" | custom-call | flops 20000000000 | bytes 60000000 | tf_op jit(solution)/shard_map/attend_forward/pallas_call | solution.py:309
  107.4 5.5 %project_out.1 = (f32[1024,768]{1,0:T(8,128)}, bf16[1024,768]{1,0:T(8,128)(2,1)}, bf16[768,768]{1,0:T(8,128)(2,1)}) custom-call(bf16[1024,768]{1,0:T(8,128)(2,1)} %get-tuple-element.70.att_ref, bf16[1024,768]{1,0:T(8,128)(2,1)} %x_ref.5, bf16[32,216,768]{2,1,0:T(8,128)(2,1)} %bitcast.123, f32[8,768]{1,0:T(8,128)} %get-tuple-element.71.vec_ref.refs_7_), custom_call_target="tpu_custom_call" | custom-call | flops 1207959552 | bytes 10000000 | tf_op jit(solution)/shard_map/project_out/pallas_call | solution.py:434
  114.2 35.2 %feed_forward.1 = (bf16[1024,3072]{1,0:T(8,128)(2,1)}, f32[1024,768]{1,0:T(8,128)}, bf16[16,192,768]{2,1,0:T(8,128)(2,1)}, bf16[16,192,768]{2,1,0:T(8,128)(2,1)}) custom-call(s32[1]{0:T(128)} %bitcast.me_ref, bf16[1024,768]{1,0:T(8,128)(2,1)S(1)} %copy-done.6, bf16[1024,768]{1,0:T(8,128)(2,1)S(1)} %select_convert_fusion.gl_ref, bf16[32,216,768]{2,1,0:T(8,128)(2,1)} %bitcast.124), custom_call_target="tpu_custom_call" | custom-call | flops 24159191040 | bytes 40000000 | tf_op jit(solution)/shard_map/feed_forward/pallas_call | solution.py:510
  149.7 8.3 %middle_back.1 = (f32[1024,768]{1,0:T(8,128)}, bf16[1024,768]{1,0:T(8,128)(2,1)S(1)}, bf16[768,768]{1,0:T(8,128)(2,1)S(1)}, f32[8,768]{1,0:T(8,128)S(1)}) custom-call(s32[1]{0:T(128)} %copy.56.len_ref, f32[1024,768]{1,0:T(8,128)} %get-tuple-element.75.gn_ref, f32[1024,768]{1,0:T(8,128)} %get-tuple-element.76.res_ref, f32[1024,768]{1,0:T(8,128)} %cot_ref.1, ...), custom_call_target="tpu_custom_call" | custom-call | flops 2415919104 | bytes 30000000 | tf_op jit(solution)/shard_map/middle_back/pallas_call | solution.py:602
  163.9 21.0 %attend_backward.2 = (bf16[3,1024,640]{2,1,0:T(8,128)(2,1)S(1)}, f32[1,8,640]{2,1,0:T(8,128)S(1)}) custom-call(bf16[1024,2304]{1,0:T(8,128)(2,1)S(1)} %bitcast.119, bf16[1024,2304]{1,0:T(8,128)(2,1)S(1)} %bitcast.119, bf16[1024,2304]{1,0:T(8,128)(2,1)S(1)} %bitcast.119, bf16[1024,768]{1,0:T(8,128)(2,1)S(1)} %get-tuple-element.94.ga_ref, ...), custom_call_target="tpu_custom_call" | custom-call | flops 24999999488 | bytes 50000000 | tf_op jit(solution)/shard_map/attend_backward/pallas_call | solution.py:391
  184.9 5.1 %collective-permute-done.9 = bf16[4,2,96,768]{3,2,0,1:T(8,128)(2,1)S(1)} collective-permute-done((bf16[4,2,96,768]{3,2,0,1:T(8,128)(2,1)S(1)}, bf16[4,2,96,768]{3,2,0,1:T(8,128)(2,1)S(1)}, u32[]{:S(2)}, u32[]{:S(2)}) %collective-permute-start.9) | collective-permute-done | bytes 1179680 | tf_op jit(solution)/shard_map/ppermute | solution.py:71
  191.1 3.1 %fusion.4 = (bf16[4,96,768]{2,1,0:T(8,128)(2,1)}, bf16[4,96,768]{2,1,0:T(8,128)(2,1)}) fusion(bf16[4,2,2,2,96,768]{5,4,3,2,1,0:T(8,128)(2,1)} %bitcast.11, bf16[4,2,2,2,96,768]{5,4,3,2,1,0:T(8,128)(2,1)S(1)} %bitcast.129, bf16[4,2,96,768]{3,2,0,1:T(8,128)(2,1)S(1)} %collective-permute-done.9, bf16[4,2,96,768]{3,2,0,1:T(8,128)(2,1)S(1)} %collective-permute-done.8), kind=kLoop, calls=%fused_computation.13 | loop fusion | flops 3538944 | bytes 4718592 | tf_op jit(solution)/shard_map/convert_element_type | solution.py:135
  196.4 7.0 %attend_backward.3 = (bf16[3,1024,128]{2,1,0:T(8,128)(2,1)S(1)}, f32[1,8,128]{2,1,0:T(8,128)S(1)}) custom-call(bf16[1024,2304]{1,0:T(8,128)(2,1)S(1)} %bitcast.119, bf16[1024,2304]{1,0:T(8,128)(2,1)S(1)} %bitcast.119, bf16[1024,2304]{1,0:T(8,128)(2,1)S(1)} %bitcast.119, bf16[1024,768]{1,0:T(8,128)(2,1)S(1)} %get-tuple-element.94.ga_ref, ...), custom_call_target="tpu_custom_call" | custom-call | flops 5000000000 | bytes 10000000 | tf_op jit(solution)/shard_map/attend_backward/pallas_call | solution.py:391
  203.4 8.8 %qkv_grad.1 = (bf16[16,104,768]{2,1,0:T(8,128)(2,1)S(1)}, bf16[16,104,768]{2,1,0:T(8,128)(2,1)}) custom-call(s32[1]{0:T(128)} %bitcast.me_ref, bf16[3,1024,640]{2,1,0:T(8,128)(2,1)} %copy-done.10, bf16[3,1024,128]{2,1,0:T(8,128)(2,1)S(1)} %get-tuple-element.95.refs_1_.d2_ref, f32[1,8,640]{2,1,0:T(8,128)S(1)} %get-tuple-element.96.refs_2_, ...), custom_call_target="tpu_custom_call" | custom-call | flops 3623878656 | bytes 25000000 | tf_op jit(solution)/shard_map/qkv_grad/pallas_call | solution.py:687
  212.3 2.2 fusion.7
  221.6 2.5 fusion.9
  226.2 12.1 %finish_output.1 = bf16[1024,768]{1,0:T(8,128)(2,1)} custom-call(bf16[1024,3072]{1,0:T(8,128)(2,1)} %get-tuple-element.113.act_ref, bf16[32,216,768]{2,1,0:T(8,128)(2,1)} %bitcast.125, f32[1024,768]{1,0:T(8,128)} %get-tuple-element.76.res_ref), custom_call_target="tpu_custom_call" | custom-call | flops 4831838208 | bytes 20000000 | tf_op jit(solution)/shard_map/finish_output/pallas_call | solution.py:551
  239.7 2.5 collective-permute-done.14
  244.4 6.0 %collective-permute-done.15 = bf16[4,48,768]{2,1,0:T(8,128)(2,1)S(1)} collective-permute-done((bf16[4,48,768]{2,1,0:T(8,128)(2,1)S(1)}, bf16[4,48,768]{2,1,0:T(8,128)(2,1)S(1)}, u32[]{:S(2)}, u32[]{:S(2)}) %collective-permute-start.15) | collective-permute-done | bytes 294944 | tf_op jit(solution)/shard_map/ppermute | solution.py:71
  250.4 2.1 collective-permute-done.16
  256.3 10.6 %first_back.1 = (f32[1024,768]{1,0:T(8,128)}, f32[8,768]{1,0:T(8,128)}) custom-call(bf16[3,1024,640]{2,1,0:T(8,128)(2,1)} %copy-done.10, bf16[3,1024,128]{2,1,0:T(8,128)(2,1)} %copy-done.9, bf16[2304,768]{1,0:T(8,128)(2,1)} %get-tuple-element.99.refs_5_.w_ref, bf16[1024,768]{1,0:T(8,128)(2,1)} %x_ref.5, f32[1024,768]{1,0:T(8,128)} %get-tuple-element.118.gres_ref, ...), custom_call_target="tpu_custom_call" | custom-call | flops 3623878656 | bytes 25000000 | tf_op jit(solution)/shard_map/first_back/pallas_call | solution.py:751
  (121 shorter events, 44.7 us)
Async XLA Ops:
  7.2 100.2 %all-gather.2.cloned.1.call-start = ((), (), s32[]{:S(2)}) async-start(), calls=%async_computation.1 | async-start | bytes 10948608 | tf_op jit(solution)/shard_map/all_gather | solution.py:777
  9.0 257.9 %reduce-scatter.2.cloned.1.call-start = ((), (), s32[]{:S(2)}) async-start(), calls=%async_computation.2 | async-start | bytes 1474560 | tf_op jit(solution)/shard_map/reduce_scatter | solution.py:128
  10.8 9.4 %collective-permute-start.2 = (bf16[1,80,768]{2,1,0:T(8,128)(2,1)S(1)}, bf16[1,80,768]{2,1,0:T(8,128)(2,1)S(1)}, u32[]{:S(2)}, u32[]{:S(2)}) collective-permute-start(bf16[1,80,768]{2,1,0:T(8,128)(2,1)S(1)} %fusion.23), channel_id=1, source_target_pairs={{0,24},{1,25},{2,26},{3,27},{4,28},{5,29},{6,30},{7,31},{8,16},{9,... | collective-permute-start | bytes 368648 | tf_op jit(solution)/shard_map/ppermute | solution.py:71
  15.9 10.5 %collective-permute-start.1 = (bf16[1,80,768]{2,1,0:T(8,128)(2,1)S(1)}, bf16[1,80,768]{2,1,0:T(8,128)(2,1)S(1)}, u32[]{:S(2)}, u32[]{:S(2)}) collective-permute-start(bf16[1,80,768]{2,1,0:T(8,128)(2,1)S(1)} %fusion.23), channel_id=1, source_target_pairs={{0,16},{1,17},{2,18},{3,19},{4,20},{5,21},{6,22},{7,23},{8,24},{9,... | collective-permute-start | bytes 368648 | tf_op jit(solution)/shard_map/ppermute | solution.py:71
  15.9 10.5 %collective-permute-start = (bf16[1,80,768]{2,1,0:T(8,128)(2,1)S(1)}, bf16[1,80,768]{2,1,0:T(8,128)(2,1)S(1)}, u32[]{:S(2)}, u32[]{:S(2)}) collective-permute-start(bf16[1,80,768]{2,1,0:T(8,128)(2,1)S(1)} %fusion.23), channel_id=1, source_target_pairs={{0,8},{1,9},{2,10},{3,11},{4,12},{5,13},{6,14},{7,15},{8,0},{9,1},... | collective-permute-start | bytes 368648 | tf_op jit(solution)/shard_map/ppermute | solution.py:71
  26.5 13.3 %collective-permute-start.3 = (bf16[4,80,768]{2,1,0:T(8,128)(2,1)S(1)}, bf16[4,80,768]{2,1,0:T(8,128)(2,1)S(1)}, u32[]{:S(2)}, u32[]{:S(2)}) collective-permute-start(bf16[4,80,768]{2,1,0:T(8,128)(2,1)S(1)} %pad_maximum_fusion.2), channel_id=1, source_target_pairs={{0,2},{1,3},{2,0},{3,1},{4,6},{5,7},{6,4},{7,5},{8,10},{9,11},{10,... | collective-permute-start | bytes 1474568 | tf_op jit(solution)/shard_map/ppermute | solution.py:71
  28.1 14.2 %collective-permute-start.4 = (bf16[4,80,768]{2,1,0:T(8,128)(2,1)S(1)}, bf16[4,80,768]{2,1,0:T(8,128)(2,1)S(1)}, u32[]{:S(2)}, u32[]{:S(2)}) collective-permute-start(bf16[4,80,768]{2,1,0:T(8,128)(2,1)S(1)} %pad_maximum_fusion.2), channel_id=1, source_target_pairs={{0,4},{1,5},{2,6},{3,7},{4,0},{5,1},{6,2},{7,3},{8,12},{9,13},{10,... | collective-permute-start | bytes 1474568 | tf_op jit(solution)/shard_map/ppermute | solution.py:71
  30.3 28.6 %collective-permute-start.5 = (bf16[4,80,768]{2,1,0:T(8,128)(2,1)S(1)}, bf16[4,80,768]{2,1,0:T(8,128)(2,1)S(1)}, u32[]{:S(2)}, u32[]{:S(2)}) collective-permute-start(bf16[4,80,768]{2,1,0:T(8,128)(2,1)S(1)} %pad_maximum_fusion.2), channel_id=1, source_target_pairs={{0,6},{1,7},{2,4},{3,5},{4,2},{5,3},{6,0},{7,1},{8,14},{9,15},{10,... | collective-permute-start | bytes 1474568 | tf_op jit(solution)/shard_map/ppermute | solution.py:71
  59.0 4.4 %collective-permute-start.6 = (bf16[16,80,768]{2,1,0:T(8,128)(2,1)S(1)}, bf16[16,80,768]{2,1,0:T(8,128)(2,1)}, u32[]{:S(2)}, u32[]{:S(2)}) collective-permute-start(bf16[16,80,768]{2,1,0:T(8,128)(2,1)S(1)} %constant_dynamic-update-slice_fusion.own_ref), channel_id=1, source_target_pairs={{0,1},{1,0},{2,3},{3,2},{4,5},{5,4},{6,7},{7,6},{8,9},{9,8},{10,11... | collective-permute-start | bytes 5898248 | tf_op jit(solution)/shard_map/ppermute | solution.py:71
  107.4 56.5 %slice-start = ((s8[4718592]{0:T(1024)(128)(4,1)}), s8[524288]{0:T(1024)(128)(4,1)S(1)}, s32[]{:S(2)}) async-start(s8[4718592]{0:T(1024)(128)(4,1)} %bitcast.118), calls=%async_computation.3 | async-start | bytes 1048576
  114.2 49.6 %slice-start.1 = ((s8[4718592]{0:T(1024)(128)(4,1)}), s8[4194304]{0:T(1024)(128)(4,1)S(1)}, s32[]{:S(2)}) async-start(s8[4718592]{0:T(1024)(128)(4,1)} %bitcast.118), calls=%async_computation.4 | async-start | bytes 8388608
  149.5 8.6 %collective-permute-start.7 = (bf16[16,192,768]{2,1,0:T(8,128)(2,1)}, bf16[16,192,768]{2,1,0:T(8,128)(2,1)}, u32[]{:S(2)}, u32[]{:S(2)}) collective-permute-start(bf16[16,192,768]{2,1,0:T(8,128)(2,1)} %get-tuple-element.79), channel_id=1, source_target_pairs={{0,1},{1,0},{2,3},{3,2},{4,5},{5,4},{6,7},{7,6},{8,9},{9,8},{10,11... | collective-permute-start | bytes 14155784 | tf_op jit(solution)/shard_map/ppermute | solution.py:71
  161.8 28.2 %collective-permute-start.9 = (bf16[4,2,96,768]{3,2,0,1:T(8,128)(2,1)S(1)}, bf16[4,2,96,768]{3,2,0,1:T(8,128)(2,1)S(1)}, u32[]{:S(2)}, u32[]{:S(2)}) collective-permute-start(bf16[4,2,96,768]{3,2,0,1:T(8,128)(2,1)S(1)} %fusion.1), channel_id=1, source_target_pairs={{0,4},{1,5},{2,6},{3,7},{4,0},{5,1},{6,2},{7,3},{8,12},{9,13},{10,... | collective-permute-start | bytes 3538952 | tf_op jit(solution)/shard_map/ppermute | solution.py:71
  163.2 27.9 %collective-permute-start.8 = (bf16[4,2,96,768]{3,2,0,1:T(8,128)(2,1)S(1)}, bf16[4,2,96,768]{3,2,0,1:T(8,128)(2,1)S(1)}, u32[]{:S(2)}, u32[]{:S(2)}) collective-permute-start(bf16[4,2,96,768]{3,2,0,1:T(8,128)(2,1)S(1)} %fusion), channel_id=1, source_target_pairs={{0,2},{1,3},{2,0},{3,1},{4,6},{5,7},{6,4},{7,5},{8,10},{9,11},{10,... | collective-permute-start | bytes 3538952 | tf_op jit(solution)/shard_map/ppermute | solution.py:71
  194.3 18.0 %collective-permute-start.11 = (bf16[4,96,768]{2,1,0:T(8,128)(2,1)}, bf16[4,96,768]{2,1,0:T(8,128)(2,1)S(1)}, u32[]{:S(2)}, u32[]{:S(2)}) collective-permute-start(bf16[4,96,768]{2,1,0:T(8,128)(2,1)} %get-tuple-element.126), channel_id=1, source_target_pairs={{0,2},{1,3},{2,0},{3,1},{4,6},{5,7},{6,4},{7,5},{8,10},{9,11},{10,... | collective-permute-start | bytes 1769480 | tf_op jit(solution)/shard_map/ppermute | solution.py:71
  194.9 17.4 %collective-permute-start.10 = (bf16[4,96,768]{2,1,0:T(8,128)(2,1)}, bf16[4,96,768]{2,1,0:T(8,128)(2,1)S(1)}, u32[]{:S(2)}, u32[]{:S(2)}) collective-permute-start(bf16[4,96,768]{2,1,0:T(8,128)(2,1)} %get-tuple-element.127), channel_id=1, source_target_pairs={{0,4},{1,5},{2,6},{3,7},{4,0},{5,1},{6,2},{7,3},{8,12},{9,13},{10,... | collective-permute-start | bytes 1769480 | tf_op jit(solution)/shard_map/ppermute | solution.py:71
  212.3 5.2 %collective-permute-start.12 = (bf16[16,104,768]{2,1,0:T(8,128)(2,1)}, bf16[16,104,768]{2,1,0:T(8,128)(2,1)}, u32[]{:S(2)}, u32[]{:S(2)}) collective-permute-start(bf16[16,104,768]{2,1,0:T(8,128)(2,1)} %get-tuple-element.108), channel_id=1, source_target_pairs={{0,1},{1,0},{2,3},{3,2},{4,5},{5,4},{6,7},{7,6},{8,9},{9,8},{10,11... | collective-permute-start | bytes 7667720 | tf_op jit(solution)/shard_map/ppermute | solution.py:71
  224.1 15.6 %collective-permute-start.13 = (bf16[2,4,48,768]{3,2,1,0:T(8,128)(2,1)}, bf16[2,4,48,768]{3,2,1,0:T(8,128)(2,1)S(1)}, u32[]{:S(2)}, u32[]{:S(2)}) collective-permute-start(bf16[2,4,48,768]{3,2,1,0:T(8,128)(2,1)} %fusion.12), channel_id=1, source_target_pairs={{0,2},{1,3},{2,0},{3,1},{4,6},{5,7},{6,4},{7,5},{8,10},{9,11},{10,... | collective-permute-start | bytes 1769480 | tf_op jit(solution)/shard_map/ppermute | solution.py:71
  224.7 17.5 %collective-permute-start.14 = (bf16[2,4,56,768]{3,2,1,0:T(8,128)(2,1)}, bf16[2,4,56,768]{3,2,1,0:T(8,128)(2,1)S(1)}, u32[]{:S(2)}, u32[]{:S(2)}) collective-permute-start(bf16[2,4,56,768]{3,2,1,0:T(8,128)(2,1)} %get-tuple-element.112), channel_id=1, source_target_pairs={{0,4},{1,5},{2,6},{3,7},{4,0},{5,1},{6,2},{7,3},{8,12},{9,13},{10,... | collective-permute-start | bytes 2064392 | tf_op jit(solution)/shard_map/ppermute | solution.py:71
  242.3 8.1 %collective-permute-start.15 = (bf16[4,48,768]{2,1,0:T(8,128)(2,1)S(1)}, bf16[4,48,768]{2,1,0:T(8,128)(2,1)S(1)}, u32[]{:S(2)}, u32[]{:S(2)}) collective-permute-start(bf16[4,48,768]{2,1,0:T(8,128)(2,1)S(1)} %fusion.19), channel_id=1, source_target_pairs={{0,4},{1,5},{2,6},{3,7},{4,0},{5,1},{6,2},{7,3},{8,12},{9,13},{10,... | collective-permute-start | bytes 884744 | tf_op jit(solution)/shard_map/ppermute | solution.py:71
  243.7 8.8 %collective-permute-start.16 = (bf16[4,56,768]{2,1,0:T(8,128)(2,1)S(1)}, bf16[4,56,768]{2,1,0:T(8,128)(2,1)S(1)}, u32[]{:S(2)}, u32[]{:S(2)}) collective-permute-start(bf16[4,56,768]{2,1,0:T(8,128)(2,1)S(1)} %fusion.14), channel_id=1, source_target_pairs={{0,2},{1,3},{2,0},{3,1},{4,6},{5,7},{6,4},{7,5},{8,10},{9,11},{10,... | collective-permute-start | bytes 1032200 | tf_op jit(solution)/shard_map/ppermute | solution.py:71
  252.7 14.1 %collective-permute-start.17 = (bf16[104,768]{1,0:T(8,128)(2,1)S(1)}, bf16[104,768]{1,0:T(8,128)(2,1)S(1)}, u32[]{:S(2)}, u32[]{:S(2)}) collective-permute-start(bf16[104,768]{1,0:T(8,128)(2,1)S(1)} %get-tuple-element.130), channel_id=1, source_target_pairs={{0,8},{1,9},{2,10},{3,11},{4,12},{5,13},{6,14},{7,15},{8,0},{9,1},... | collective-permute-start | bytes 479240 | tf_op jit(solution)/shard_map/ppermute | solution.py:71
  254.1 12.8 %collective-permute-start.19 = (bf16[104,768]{1,0:T(8,128)(2,1)S(1)}, bf16[104,768]{1,0:T(8,128)(2,1)S(1)}, u32[]{:S(2)}, u32[]{:S(2)}) collective-permute-start(bf16[104,768]{1,0:T(8,128)(2,1)S(1)} %get-tuple-element.131), channel_id=1, source_target_pairs={{0,24},{1,25},{2,26},{3,27},{4,28},{5,29},{6,30},{7,31},{8,16},{9,... | collective-permute-start | bytes 479240 | tf_op jit(solution)/shard_map/ppermute | solution.py:71
  256.0 12.3 %collective-permute-start.18 = (bf16[104,768]{1,0:T(8,128)(2,1)S(1)}, bf16[104,768]{1,0:T(8,128)(2,1)S(1)}, u32[]{:S(2)}, u32[]{:S(2)}) collective-permute-start(bf16[104,768]{1,0:T(8,128)(2,1)S(1)} %get-tuple-element.132), channel_id=1, source_target_pairs={{0,16},{1,17},{2,18},{3,19},{4,20},{5,21},{6,22},{7,23},{8,24},{9,... | collective-permute-start | bytes 479240 | tf_op jit(solution)/shard_map/ppermute | solution.py:71
  (20 other events, 253.5 us)
Sparse Core Ops, SparseCore 0:
  10.9 96.3 all-gather.1
  224.8 28.5 reduce-scatter.1
